TPU v7x, 32 devices: a whole 2x2x4 slice. The times are simulated.
32 devices in a mesh: grp: 2 (over x), fiber: 8 (over z, y), tm: 2 (over core).
Axes of the slice: x: 2, y: 2, z: 4, core: 2. Of those that a mesh axis runs over, the one named last changes fastest.
Arguments:
- samples: bfloat16 [64, 5120, 128], P('tm', ('grp', 'fiber')), parts along dimension 1, may hold values from -6 to 6
- counts: int32 [16], P(('grp', 'fiber')), parts along dimension 0, may hold values from 80 to 320
- reach_limit: int32 [5120], P(('grp', 'fiber')), parts along dimension 0, may hold values from 320 to 960
Outputs:
- coherence_real: bfloat16 [32, 5120, 960], P('tm', ('grp', 'fiber')), parts along dimension 1
- coherence_imag: bfloat16 [32, 5120, 960], P('tm', ('grp', 'fiber')), parts along dimension 1
There are 2 independent parts, one for each index of `grp`. A program takes and returns all parts, laid end to end along the dimension named above; each array names one. Nothing has to cross between parts.
All inputs are finite; a program needn't handle non-finite values.
Results may differ from a plain program's by a relative error of at most 0.0069.
Values may be sent and summed in bfloat16 or wider, within the bound.
No kernel may reach another device: no remote copies, remote signals or barrier semaphores. Data moves between devices by JAX's collectives and lax.ppermute only.
A program may use at most 576 MiB of HBM per device.

v0:
```python
import math

import jax
import jax.numpy as jnp
from jax import lax
from jax.sharding import PartitionSpec as P

FREQS = 32
FIRST_BIN = 8


def from_behind(block, axis, distance):
    devices = range(lax.axis_size(axis))
    route = [(i - distance, i) for i in devices if i - distance in devices]
    return lax.ppermute(block, axis, route)


def make_table(length, bins, first_bin):
    steps_index = jnp.arange(length, dtype=jnp.int32)
    bin_index = jnp.arange(bins, dtype=jnp.int32) + first_bin
    products = steps_index[:, None] * bin_index[None, :] % length
    phases = 2.0 * math.pi * products.astype(jnp.float32) / length
    taper = 0.5 - 0.5 * jnp.cos(2.0 * math.pi * steps_index.astype(jnp.float32) / length)
    cosines = taper[:, None] * jnp.cos(phases)
    sines = -taper[:, None] * jnp.sin(phases)
    return jnp.concatenate([cosines, sines], axis=1).astype(jnp.bfloat16)


def diagonal_band(matrix):
    bins_here, rows, columns = matrix.shape
    flattened = matrix.reshape(bins_here, rows * columns)
    flattened = jnp.pad(flattened, ((0, 0), (0, rows)))
    return flattened.reshape(bins_here, rows, columns + 1)[:, :, 1 : columns - rows + 1]


def banded_products(left_real, left_imag, right_real, right_imag):
    bins_here = left_real.shape[0]
    bin_group = 8

    def tile_band(operands):
        lreal, limag, rreal, rimag = operands
        left_both = jnp.concatenate([lreal, limag], axis=1)
        left_turned = jnp.concatenate([limag, -lreal], axis=1)
        right_both = jnp.concatenate([rreal, rimag], axis=1)
        cross_real = jnp.einsum(
            "fwc,fwj->fcj", left_both, right_both, preferred_element_type=jnp.float32
        )
        cross_imag = jnp.einsum(
            "fwc,fwj->fcj", left_turned, right_both, preferred_element_type=jnp.float32
        )
        return (diagonal_band(cross_real), diagonal_band(cross_imag))

    stacked = tuple(
        (
            array.reshape((bins_here // bin_group, bin_group) + array.shape[1:])
            for array in (left_real, left_imag, right_real, right_imag)
        )
    )
    band_real, band_imag = lax.map(tile_band, stacked)
    shape_out = (bins_here,) + band_real.shape[2:]
    return (band_real.reshape(shape_out), band_imag.reshape(shape_out))


def body(samples, counts, reach_limit):
    windows_here = samples.shape[0]
    block_width = samples.shape[1]
    dft_table = make_table(samples.shape[2], FREQS, FIRST_BIN)
    raw_spectra = jnp.einsum("wcl,lg->gwc", samples, dft_table, preferred_element_type=jnp.float32)
    real_raw = raw_spectra[:FREQS]
    imag_raw = raw_spectra[FREQS:]
    level = jnp.mean(real_raw * real_raw + imag_raw * imag_raw, axis=0)
    scale = lax.rsqrt(level + 1e-06)
    active = (lax.iota(jnp.int32, block_width) < counts[0]).astype(jnp.float32)
    real_part = (real_raw * scale * active).astype(jnp.bfloat16)
    imag_part = (imag_raw * scale * active).astype(jnp.bfloat16)
    total_windows = windows_here * lax.axis_size("tm")
    real_part, imag_part = (
        lax.all_to_all(real_part, "tm", split_axis=0, concat_axis=1, tiled=True),
        lax.all_to_all(imag_part, "tm", split_axis=0, concat_axis=1, tiled=True),
    )
    pieces = []
    current = (real_part, imag_part)
    for distance in range(1, 4):
        current = from_behind((current[0], current[1]), "fiber", -1)
        pieces.append(current)
    right_real = jnp.concatenate([real_part] + [piece[0] for piece in pieces], axis=2)
    right_imag = jnp.concatenate([imag_part] + [piece[1] for piece in pieces], axis=2)
    band_real, band_imag = banded_products(real_part, imag_part, right_real, right_imag)
    wide_real = right_real.astype(jnp.float32)
    wide_imag = right_imag.astype(jnp.float32)
    power_sum = jnp.sum(wide_real * wide_real + wide_imag * wide_imag, axis=1)
    inverse_root = lax.rsqrt(power_sum / total_windows + 1e-06)
    bins_here = inverse_root.shape[0]
    own_scale = inverse_root[:, :block_width]
    partner = diagonal_band(
        jnp.broadcast_to(inverse_root[:, None, :], (bins_here, block_width, 4 * block_width))
    )
    offsets = jnp.arange(1, 3 * block_width + 1, dtype=jnp.int32)
    in_reach = (offsets[None, :] <= reach_limit[:, None]).astype(jnp.float32)
    factor = own_scale[:, :, None] * partner * in_reach[None, :, :] / math.sqrt(total_windows)
    return ((band_real * factor).astype(jnp.bfloat16), (band_imag * factor).astype(jnp.bfloat16))


def solution(mesh):
    placed = (P("tm", ("grp", "fiber"), None), P(("grp", "fiber")), P(("grp", "fiber")))
    return jax.shard_map(
        body,
        mesh=mesh,
        in_specs=placed,
        out_specs=(P("tm", ("grp", "fiber"), None), P("tm", ("grp", "fiber"), None)),
        check_vma=False,
    )
```

profile of v0, /device:TPU:0, one launch (start us, length us, event | category | flops | bytes accessed | tf_op | source)
XLA Modules:
  0.0 617.5 jit_solution(14195285776358515443)
XLA Ops:
  18.0 20.2 %collective-permute-done.3 = bf16[16,64,320]{2,1,0:T(8,128)(2,1)} collective-permute-done((bf16[16,64,320]{2,1,0:T(8,128)(2,1)S(1)}, bf16[16,64,320]{2,1,0:T(8,128)(2,1)}, u32[]{:S(2)}, u32[]{:S(2)}) %collective-permute-start.3) | collective-permute-done | bytes 655392 | tf_op jit(solution)/shard_map/ppermute | solution.py:15
  39.5 15.5 %collective-permute-done = bf16[16,64,320]{2,1,0:T(8,128)(2,1)S(1)} collective-permute-done((bf16[16,64,320]{2,1,0:T(8,128)(2,1)S(1)}, bf16[16,64,320]{2,1,0:T(8,128)(2,1)S(1)}, u32[]{:S(2)}, u32[]{:S(2)}) %collective-permute-start) | collective-permute-done | bytes 655392 | tf_op jit(solution)/shard_map/ppermute | solution.py:15
  56.2 15.7 %collective-permute-done.4 = bf16[16,64,320]{2,1,0:T(8,128)(2,1)} collective-permute-done((bf16[16,64,320]{2,1,0:T(8,128)(2,1)}, bf16[16,64,320]{2,1,0:T(8,128)(2,1)}, u32[]{:S(2)}, u32[]{:S(2)}) %collective-permute-start.4) | collective-permute-done | bytes 655392 | tf_op jit(solution)/shard_map/ppermute | solution.py:15
  73.2 15.6 %collective-permute-done.1 = bf16[16,64,320]{2,1,0:T(8,128)(2,1)} collective-permute-done((bf16[16,64,320]{2,1,0:T(8,128)(2,1)S(1)}, bf16[16,64,320]{2,1,0:T(8,128)(2,1)}, u32[]{:S(2)}, u32[]{:S(2)}) %collective-permute-start.1) | collective-permute-done | bytes 655392 | tf_op jit(solution)/shard_map/ppermute | solution.py:15
  91.3 14.3 %collective-permute-done.5 = bf16[16,64,320]{2,1,0:T(8,128)(2,1)} collective-permute-done((bf16[16,64,320]{2,1,0:T(8,128)(2,1)}, bf16[16,64,320]{2,1,0:T(8,128)(2,1)}, u32[]{:S(2)}, u32[]{:S(2)}) %collective-permute-start.5) | collective-permute-done | bytes 655392 | tf_op jit(solution)/shard_map/ppermute | solution.py:15
  111.4 10.9 %collective-permute-done.2 = bf16[16,64,320]{2,1,0:T(8,128)(2,1)} collective-permute-done((bf16[16,64,320]{2,1,0:T(8,128)(2,1)}, bf16[16,64,320]{2,1,0:T(8,128)(2,1)}, u32[]{:S(2)}, u32[]{:S(2)}) %collective-permute-start.2) | collective-permute-done | bytes 655392 | tf_op jit(solution)/shard_map/ppermute | solution.py:15
  143.1 355.5 %while.14 = (s32[]{:T(128)}, f32[2,8,320,960]{3,2,1,0:T(8,128)}, f32[2,8,320,960]{3,2,1,0:T(8,128)}, bf16[2,8,64,320]{3,2,1,0:T(8,128)(2,1)S(1)}, bf16[2,8,64,32...) while((s32[]{:T(128)}, f32[2,8,320,960]{3,2,1,0:T(8,128)}, ...), condition=%wide.region_2.3_spmd, body=%wide.region_1.2_spmd.sunk | while | flops 1690992640 | bytes 306155808 | solution.py:59
  155.7 17.0 %copy.37 = f32[1,8,320,1280]{3,1,2,0:T(8,128)} copy(f32[1,8,320,1280]{3,2,1,0:T(8,128)} %convolution_bitcast_fusion.5) | data formatting | bytes 26214400 | tf_op jit(solution)/shard_map/while
  182.5 15.0 %reshape.140 = f32[3279360]{0:T(1024)} reshape(f32[8,409920]{1,0:T(8,128)} %pad.75) | data formatting | bytes 26234880 | tf_op jit(solution)/shard_map/while
  197.5 26.7 %reshape.141 = f32[8,320,1281]{2,1,0:T(8,128)} reshape(f32[3279360]{0:T(1024)} %reshape.140) | data formatting | bytes 26234880 | tf_op jit(solution)/shard_map/while/body/eval_jaxpr/reshape | solution.py:33
  231.9 17.1 %copy.36 = f32[1,8,320,1280]{3,1,2,0:T(8,128)} copy(f32[1,8,320,1280]{3,2,1,0:T(8,128)} %convolution_bitcast_fusion.4) | data formatting | bytes 26214400 | tf_op jit(solution)/shard_map/while
  258.8 15.0 %reshape.138 = f32[3279360]{0:T(1024)} reshape(f32[8,409920]{1,0:T(8,128)} %pad.74) | data formatting | bytes 26234880 | tf_op jit(solution)/shard_map/while
  273.8 26.6 %reshape.139 = f32[8,320,1281]{2,1,0:T(8,128)} reshape(f32[3279360]{0:T(1024)} %reshape.138) | data formatting | bytes 26234880 | tf_op jit(solution)/shard_map/while/body/eval_jaxpr/reshape | solution.py:33
  300.4 18.2 %fusion.32 = (f32[2,8,320,960]{3,2,1,0:T(8,128)}, f32[2,8,320,960]{3,2,1,0:T(8,128)}) fusion(f32[2,8,320,960]{3,2,1,0:T(8,128)} %get-tuple-element.197, s32[]{:T(128)S(6)} %copy.43, f32[8,320,1281]{2,1,0:T(8,128)} %reshape.139, f32[2,8,320,960]{3,2,1,0:T(8,128)} %get-tuple-element.196, f32[8,320,1281]{2,1,0:T(8,128)} %reshape.141), kind=kLoop, calls=%fused_computation.1.clone.1 | loop fusion | bytes 41943044 | tf_op jit(solution)/shard_map/while/body/jit(dynamic_update_index_in_dim)/dynamic_update_slice | solution.py:59
  331.3 17.0 %copy.37 = f32[1,8,320,1280]{3,1,2,0:T(8,128)} copy(f32[1,8,320,1280]{3,2,1,0:T(8,128)} %convolution_bitcast_fusion.5) | data formatting | bytes 26214400 | tf_op jit(solution)/shard_map/while
  358.0 15.0 %reshape.140 = f32[3279360]{0:T(1024)} reshape(f32[8,409920]{1,0:T(8,128)} %pad.75) | data formatting | bytes 26234880 | tf_op jit(solution)/shard_map/while
  373.0 26.8 %reshape.141 = f32[8,320,1281]{2,1,0:T(8,128)} reshape(f32[3279360]{0:T(1024)} %reshape.140) | data formatting | bytes 26234880 | tf_op jit(solution)/shard_map/while/body/eval_jaxpr/reshape | solution.py:33
  407.5 17.1 %copy.36 = f32[1,8,320,1280]{3,1,2,0:T(8,128)} copy(f32[1,8,320,1280]{3,2,1,0:T(8,128)} %convolution_bitcast_fusion.4) | data formatting | bytes 26214400 | tf_op jit(solution)/shard_map/while
  434.3 15.0 %reshape.138 = f32[3279360]{0:T(1024)} reshape(f32[8,409920]{1,0:T(8,128)} %pad.74) | data formatting | bytes 26234880 | tf_op jit(solution)/shard_map/while
  449.3 26.4 %reshape.139 = f32[8,320,1281]{2,1,0:T(8,128)} reshape(f32[3279360]{0:T(1024)} %reshape.138) | data formatting | bytes 26234880 | tf_op jit(solution)/shard_map/while/body/eval_jaxpr/reshape | solution.py:33
  475.7 18.2 %fusion.32 = (f32[2,8,320,960]{3,2,1,0:T(8,128)}, f32[2,8,320,960]{3,2,1,0:T(8,128)}) fusion(f32[2,8,320,960]{3,2,1,0:T(8,128)} %get-tuple-element.197, s32[]{:T(128)S(6)} %copy.43, f32[8,320,1281]{2,1,0:T(8,128)} %reshape.139, f32[2,8,320,960]{3,2,1,0:T(8,128)} %get-tuple-element.196, f32[8,320,1281]{2,1,0:T(8,128)} %reshape.141), kind=kLoop, calls=%fused_computation.1.clone.1 | loop fusion | bytes 41943044 | tf_op jit(solution)/shard_map/while/body/jit(dynamic_update_index_in_dim)/dynamic_update_slice | solution.py:59
  509.3 21.0 %copy.29 = f32[2,8,320,1280]{3,1,2,0:T(8,128)S(1)} copy(f32[2,8,320,1280]{3,2,1,0:T(8,128)} %bitcast.79) | data formatting | bytes 52428800
  539.3 47.4 %reshape.127 = f32[16,320,1281]{2,1,0:T(8,128)} reshape(f32[16,409920]{1,0:T(8,128)} %pad.17) | data formatting | bytes 52469760 | tf_op jit(solution)/shard_map/reshape | solution.py:33
  586.8 30.5 %fusion.12 = (bf16[16,320,960]{2,1,0:T(8,128)(2,1)}, bf16[16,320,960]{2,1,0:T(8,128)(2,1)}) fusion(f32[2,8,320,960]{3,2,1,0:T(8,128)} %get-tuple-element.93, f32[16,320,1281]{2,1,0:T(8,128)} %reshape.127, f32[320,960]{1,0:T(8,128)} %compare_convert_fusion, f32[16,320]{1,0:T(8,128)S(1)} %slice-done, f32[2,8,320,960]{3,2,1,0:T(8,128)} %get-tuple-element.92), kind=kLoop, calls=%fused_computation.24 | loop fusion | flops 34406400 | bytes 79892480 | tf_op jit(solution)/shard_map/convert_element_type | solution.py:101
  (92 shorter events, 148.2 us)
Async XLA Ops:
  0.6 1.8 copy-start
  4.5 85.5 %copy-start.10 = (s32[320]{0:T(512)S(1)}, s32[320]{0:T(512)}, u32[]{:S(2)}) copy-start(s32[320]{0:T(512)} %param.7) | copy-start | bytes 3844
  5.7 5.5 all-to-all-start.1
  11.1 5.5 all-to-all-start
  14.8 23.4 %collective-permute-start.3 = (bf16[16,64,320]{2,1,0:T(8,128)(2,1)S(1)}, bf16[16,64,320]{2,1,0:T(8,128)(2,1)}, u32[]{:S(2)}, u32[]{:S(2)}) collective-permute-start(bf16[16,64,320]{2,1,0:T(8,128)(2,1)S(1)} %bitcast.80), channel_id=1, source_target_pairs={{2,0},{4,2},{6,4},{8,6},{10,8},{12,10},{14,12},{3,1},{5,3},{7,5},{... | collective-permute-start | bytes 1966088 | tf_op jit(solution)/shard_map/ppermute | solution.py:15
  16.7 38.2 %collective-permute-start = (bf16[16,64,320]{2,1,0:T(8,128)(2,1)S(1)}, bf16[16,64,320]{2,1,0:T(8,128)(2,1)S(1)}, u32[]{:S(2)}, u32[]{:S(2)}) collective-permute-start(bf16[16,64,320]{2,1,0:T(8,128)(2,1)S(1)} %bitcast.84), channel_id=1, source_target_pairs={{2,0},{4,2},{6,4},{8,6},{10,8},{12,10},{14,12},{3,1},{5,3},{7,5},{... | collective-permute-start | bytes 1966088 | tf_op jit(solution)/shard_map/ppermute | solution.py:15
  38.2 33.7 %collective-permute-start.4 = (bf16[16,64,320]{2,1,0:T(8,128)(2,1)}, bf16[16,64,320]{2,1,0:T(8,128)(2,1)}, u32[]{:S(2)}, u32[]{:S(2)}) collective-permute-start(bf16[16,64,320]{2,1,0:T(8,128)(2,1)} %collective-permute-done.3), channel_id=1, source_target_pairs={{2,0},{4,2},{6,4},{8,6},{10,8},{12,10},{14,12},{3,1},{5,3},{7,5},{... | collective-permute-start | bytes 1966088 | tf_op jit(solution)/shard_map/ppermute | solution.py:15
  54.9 33.8 %collective-permute-start.1 = (bf16[16,64,320]{2,1,0:T(8,128)(2,1)S(1)}, bf16[16,64,320]{2,1,0:T(8,128)(2,1)}, u32[]{:S(2)}, u32[]{:S(2)}) collective-permute-start(bf16[16,64,320]{2,1,0:T(8,128)(2,1)S(1)} %collective-permute-done), channel_id=1, source_target_pairs={{2,0},{4,2},{6,4},{8,6},{10,8},{12,10},{14,12},{3,1},{5,3},{7,5},{... | collective-permute-start | bytes 1966088 | tf_op jit(solution)/shard_map/ppermute | solution.py:15
  71.9 33.7 %collective-permute-start.5 = (bf16[16,64,320]{2,1,0:T(8,128)(2,1)}, bf16[16,64,320]{2,1,0:T(8,128)(2,1)}, u32[]{:S(2)}, u32[]{:S(2)}) collective-permute-start(bf16[16,64,320]{2,1,0:T(8,128)(2,1)} %collective-permute-done.4), channel_id=1, source_target_pairs={{2,0},{4,2},{6,4},{8,6},{10,8},{12,10},{14,12},{3,1},{5,3},{7,5},{... | collective-permute-start | bytes 1966088 | tf_op jit(solution)/shard_map/ppermute | solution.py:15
  88.7 33.5 %collective-permute-start.2 = (bf16[16,64,320]{2,1,0:T(8,128)(2,1)}, bf16[16,64,320]{2,1,0:T(8,128)(2,1)}, u32[]{:S(2)}, u32[]{:S(2)}) collective-permute-start(bf16[16,64,320]{2,1,0:T(8,128)(2,1)} %collective-permute-done.1), channel_id=1, source_target_pairs={{2,0},{4,2},{6,4},{8,6},{10,8},{12,10},{14,12},{3,1},{5,3},{7,5},{... | collective-permute-start | bytes 1966088 | tf_op jit(solution)/shard_map/ppermute | solution.py:15
  131.6 11.5 %copy-start.8 = (f32[16,1280]{1,0:T(8,128)}, f32[16,1280]{1,0:T(8,128)S(1)}, u32[]{:S(2)}) copy-start(f32[16,1280]{1,0:T(8,128)S(1)} %add_rsqrt_fusion) | copy-start | bytes 245764
  143.1 355.6 %copy-start.9 = (f32[16,1280]{1,0:T(8,128)S(1)}, f32[16,1280]{1,0:T(8,128)}, u32[]{:S(2)}) copy-start(f32[16,1280]{1,0:T(8,128)} %copy-done.8) | copy-start | bytes 245764
  143.3 1.2 copy-start.6
  144.5 0.9 copy-start.2
  146.3 2.9 copy-start.3
  300.4 18.2 %copy-start.5 = (bf16[2,8,64,320]{3,2,1,0:T(8,128)(2,1)S(1)}, bf16[2,8,64,320]{3,2,1,0:T(8,128)(2,1)}, u32[]{:S(2)}) copy-start(bf16[2,8,64,320]{3,2,1,0:T(8,128)(2,1)} %copy-done.4) | copy-start | bytes 1966084 | tf_op jit(solution)/shard_map/while
  300.4 18.2 %copy-start.7 = (bf16[2,8,64,320]{3,2,1,0:T(8,128)(2,1)S(1)}, bf16[2,8,64,320]{3,2,1,0:T(8,128)(2,1)}, u32[]{:S(2)}) copy-start(bf16[2,8,64,320]{3,2,1,0:T(8,128)(2,1)} %copy-done.6) | copy-start | bytes 1966084 | tf_op jit(solution)/shard_map/while
  318.8 1.2 copy-start.6
  320.0 0.9 copy-start.2
  321.8 2.9 copy-start.3
  475.7 18.2 %copy-start.5 = (bf16[2,8,64,320]{3,2,1,0:T(8,128)(2,1)S(1)}, bf16[2,8,64,320]{3,2,1,0:T(8,128)(2,1)}, u32[]{:S(2)}) copy-start(bf16[2,8,64,320]{3,2,1,0:T(8,128)(2,1)} %copy-done.4) | copy-start | bytes 1966084 | tf_op jit(solution)/shard_map/while
  475.7 18.2 %copy-start.7 = (bf16[2,8,64,320]{3,2,1,0:T(8,128)(2,1)S(1)}, bf16[2,8,64,320]{3,2,1,0:T(8,128)(2,1)}, u32[]{:S(2)}) copy-start(bf16[2,8,64,320]{3,2,1,0:T(8,128)(2,1)} %copy-done.6) | copy-start | bytes 1966084 | tf_op jit(solution)/shard_map/while
  539.3 47.5 %slice-start = ((f32[16,1280]{1,0:T(8,128)}), f32[16,320]{1,0:T(8,128)S(1)}, s32[]{:S(2)}) async-start(f32[16,1280]{1,0:T(8,128)} %copy-done.8), calls=%async_computation.2 | async-start | bytes 49152 | tf_op jit(solution)/shard_map/slice | solution.py:94
  586.8 30.5 %copy-start.1 = (bf16[32,320,128]{2,1,0:T(8,128)(2,1)S(1)}, bf16[32,320,128]{2,1,0:T(8,128)(2,1)}, u32[]{:S(2)}) copy-start(bf16[32,320,128]{2,1,0:T(8,128)(2,1)} %param.5) | copy-start | bytes 7864324
  (2 other events, 1.7 us)
where the time goes:
time: 624 us; the launch traced here: 617 us
  local copies, waits for them, and re-layouts  434 us (70%)
  waiting for transfers between devices  93.3 us (15%)
  other arithmetic  38.4 us (6%)
  matrix products  29.7 us (5%)
  starting transfers between devices  14.8 us (2%)
    reshape x5, local copies, waits for them, and re-layouts, diagonal_band(): flattened.reshape(bins_here, rows, columns + 1)[:, :, 1:columns - rows + 1]  154 us
    while x32, local copies, waits for them, and re-layouts  131 us
    ppermute x6, waiting for transfers between devices, from_behind(): return lax.ppermute(block, axis, route)  92 us
    pad x5, local copies, waits for them, and re-layouts, diagonal_band(): flattened = jnp.pad(flattened, ((0, 0), (0, rows)))  47.9 us
    dynamic_update_slice x2, local copies, waits for them, and re-layouts, banded_products(): band_real, band_imag = lax.map(tile_band, stacked)  36.4 us
    convert_element_type x1, other arithmetic, body(): (band_imag * factor).astype(jnp.bfloat16)  30.5 us
    unnamed x11, local copies, waits for them, and re-layouts  21.7 us
    dot_general x2, matrix products, tile_band(): jnp.einsum('fwc,fwj->fcj', left_turned, right_both, preferred_element_typ...  15.4 us
  transfers between devices with their start and end apart: 8, of which 8 were waited for; matrix products, arithmetic and copies ran while one was open for 1% of the time, Pallas kernels for 0%

commit v1 on v0

v1 whole, which is shorter than its diff:
```python
import functools
import math

import jax
import jax.numpy as jnp
import ml_dtypes
import numpy as np
from jax import lax
from jax.experimental import pallas as pl
from jax.experimental.pallas import tpu as pltpu
from jax.sharding import PartitionSpec as P

FREQS = 32
FIRST_BIN = 8
LANES = 128
HOPS = 3
ROWS = 64
CHUNKS = 4


def make_table(length, bins, first_bin):
    steps_index = np.arange(length, dtype=np.int32)
    bin_index = np.arange(bins, dtype=np.int32) + first_bin
    products = bin_index[:, None] * steps_index[None, :] % length
    phases = (2.0 * math.pi * products / length).astype(np.float32)
    taper = 0.5 - 0.5 * np.cos((2.0 * math.pi * steps_index / length).astype(np.float32))
    taper = taper.astype(np.float32)
    cosines = taper[None, :] * np.cos(phases)
    sines = -taper[None, :] * np.sin(phases)
    return np.concatenate([cosines, sines], axis=0).astype(ml_dtypes.bfloat16)


def spectra_kernel(place_ref, samples_ref, table_ref, mine_ref, other_ref, raw_ref):
    windows, block, _ = samples_ref.shape
    pairs = mine_ref.shape[0]
    here = place_ref[0]
    tiles = raw_ref.shape[0]
    channel = lax.broadcasted_iota(jnp.int32, (1, block), 1)
    active = (channel < place_ref[1]).astype(jnp.float32)
    for w in range(windows):
        raw = lax.dot_general(
            table_ref[...], samples_ref[w], (((1,), (1,)), ((), ())),
            preferred_element_type=jnp.float32,
        )
        level = jnp.sum(raw * raw, axis=0, keepdims=True) * (1.0 / FREQS)
        white = raw * (lax.rsqrt(level + 1e-06) * active)
        for tile in range(tiles):
            start = tile * LANES
            width = min(LANES, block - start)
            raw_ref[tile, w * 2 * FREQS : (w + 1) * 2 * FREQS, :width] = white[:, start : start + width]
    for out_ref, first in ((mine_ref, here * 2 * pairs), (other_ref, (1 - here) * 2 * pairs)):
        for pair in range(pairs):
            for tile in range(tiles):
                start = tile * LANES
                width = min(LANES, block - start)
                rows = [
                    raw_ref[tile, pl.ds(first + 2 * pair + part, windows, stride=2 * FREQS), :]
                    for part in (0, FREQS, 1, FREQS + 1)
                ]
                turned = jnp.concatenate(rows, axis=0).T
                out_ref[pair, start : start + width, :] = turned[:width].astype(jnp.bfloat16)


def merge_kernel(mine_ref, theirs_ref, *out_refs, total_windows):
    block, lanes = mine_ref.shape[1:]
    half = lanes // 2
    lane = lax.broadcasted_iota(jnp.int32, (block, lanes), 1)
    per_chunk = out_refs[0].shape[0]
    for pair in range(mine_ref.shape[0]):
        mine = mine_ref[pair].astype(jnp.float32)
        theirs = theirs_ref[pair].astype(jnp.float32)
        both = (
            jnp.where(lane < half, mine, pltpu.roll(theirs, half, 1)),
            jnp.where(lane < half, pltpu.roll(mine, half, 1), theirs),
        )
        for step, values in enumerate(both):
            power = jnp.sum(values * values, axis=1, keepdims=True)
            root = lax.rsqrt(power * (1.0 / total_windows) + 1e-06)
            bin_at = 2 * pair + step
            out_refs[bin_at // per_chunk][bin_at % per_chunk] = (values * root).astype(jnp.bfloat16)


def band_kernel(
    even_ref, own_ref, *refs, total_windows
):
    pieces = refs[: 2 * HOPS]
    mask_ref, real_ref, imag_ref, right_ref, left_ref = (*refs[2 * HOPS : 2 * HOPS + 1], *refs[-4:])
    block, depth = own_ref.shape[1:]
    reach = HOPS * block
    right_ref[:block] = own_ref[0]
    is_even = even_ref[0] == 1

    @pl.when(is_even)
    def _():
        for hop in range(HOPS):
            right_ref[(hop + 1) * block : (hop + 2) * block] = pieces[2 * hop][0]

    @pl.when(jnp.logical_not(is_even))
    def _():
        for hop in range(HOPS):
            right_ref[(hop + 1) * block : (hop + 2) * block] = pieces[2 * hop + 1][0]

    wide = own_ref[0].astype(jnp.float32) * (1.0 / math.sqrt(total_windows))
    part = depth // 4
    lane = lax.broadcasted_iota(jnp.int32, (block, depth), 1)
    turned = jnp.where(
        (lane // part) % 2 == 0, pltpu.roll(wide, depth - part, 1), -pltpu.roll(wide, part, 1)
    )
    for group in range(block // ROWS):
        at = slice(group * ROWS, (group + 1) * ROWS)
        left_ref[2 * group * ROWS : (2 * group + 1) * ROWS] = wide[at].astype(jnp.bfloat16)
        left_ref[(2 * group + 1) * ROWS : (2 * group + 2) * ROWS] = turned[at].astype(jnp.bfloat16)
    lane_of = lax.broadcasted_iota(jnp.int32, (ROWS, LANES), 1)
    row_of = lax.broadcasted_iota(jnp.int32, (ROWS, LANES), 0)
    out_tiles = -(-reach // LANES)
    for group in range(block // ROWS):
        first = group * ROWS
        base = (first + 1) // LANES
        shift = first + 1 - base * LANES + row_of
        tiles = (first + ROWS - 1 + reach) // LANES - base + 1
        products = lax.dot_general(
            left_ref[2 * first : 2 * first + 2 * ROWS],
            right_ref[base * LANES : (base + tiles) * LANES],
            (((1,), (1,)), ((), ())),
            preferred_element_type=jnp.float32,
        )
        keep = lane_of >= shift
        source = (lane_of + shift) % LANES
        for out_at, out_ref in enumerate((real_ref, imag_ref)):
            rows = products[out_at * ROWS : (out_at + 1) * ROWS]
            for tile in range(out_tiles):
                start = tile * LANES
                width = min(LANES, reach - start)
                values = rows[:, start : start + LANES]
                if tile + 1 < tiles:
                    values = jnp.where(keep, values, rows[:, start + LANES : start + 2 * LANES])
                moved = jnp.take_along_axis(values, source, axis=1, mode="promise_in_bounds")
                moved = moved.astype(jnp.bfloat16)
                if start + LANES > block:
                    moved = moved * mask_ref[first : first + ROWS, start : start + LANES]
                out_ref[0, first : first + ROWS, start : start + width] = moved[:, :width]


def band(even, own, pieces, mask, so_far, chunk, bins_here, total_windows):
    per_chunk, block, depth = own.shape
    out = jax.ShapeDtypeStruct((bins_here, block, HOPS * block), jnp.bfloat16)
    out_spec = pl.BlockSpec(
        (1, block, HOPS * block), lambda i, even: (chunk * per_chunk + i, 0, 0)
    )
    one = (1, block, depth)
    in_specs = [pl.BlockSpec(one, lambda i, even: (i, 0, 0))]
    operands = [even, own]
    for for_even, for_odd in pieces:
        in_specs.append(pl.BlockSpec(one, lambda i, even: (i * even[0], 0, 0)))
        in_specs.append(pl.BlockSpec(one, lambda i, even: (i * (1 - even[0]), 0, 0)))
        operands += [for_even, for_odd]
    in_specs.append(pl.BlockSpec(mask.shape, lambda i, even: (0, 0)))
    operands.append(mask)
    aliases = {}
    if so_far is not None:
        aliases = {len(operands): 0, len(operands) + 1: 1}
        operands += list(so_far)
        in_specs += [pl.BlockSpec(memory_space=pl.ANY)] * 2
    return pl.pallas_call(
        functools.partial(band_kernel, total_windows=total_windows),
        grid_spec=pltpu.PrefetchScalarGridSpec(
            num_scalar_prefetch=1,
            grid=(per_chunk,),
            in_specs=in_specs,
            out_specs=[out_spec, out_spec],
            scratch_shapes=[
                pltpu.VMEM(((HOPS + 1) * block, depth), jnp.bfloat16),
                pltpu.VMEM((2 * block, depth), jnp.bfloat16),
            ],
        ),
        out_shape=[out, out],
        input_output_aliases=aliases,
        cost_estimate=pl.CostEstimate(
            flops=per_chunk * 4 * block * (HOPS + 1) * block * depth,
            bytes_accessed=per_chunk * 4 * block * HOPS * block * 2,
            transcendentals=0,
        ),
        compiler_params=pltpu.CompilerParams(vmem_limit_bytes=24 << 20),
    )(*operands)


def body(samples, counts, reach_limit):
    windows_here, block, length = samples.shape
    tm_size = lax.axis_size("tm")
    fiber_size = lax.axis_size("fiber")
    total_windows = windows_here * tm_size
    bins_here = FREQS // tm_size
    per_chunk = bins_here // CHUNKS
    lanes = 4 * windows_here
    here = lax.axis_index("tm").astype(jnp.int32)
    is_even = lax.axis_index("fiber") % 2 == 0
    even = is_even.astype(jnp.int32)[None]

    pair_shape = jax.ShapeDtypeStruct((bins_here // 2, block, lanes), jnp.bfloat16)
    mine, other = pl.pallas_call(
        spectra_kernel,
        in_specs=[
            pl.BlockSpec(memory_space=pltpu.SMEM),
            pl.BlockSpec(memory_space=pltpu.VMEM),
            pl.BlockSpec(memory_space=pltpu.VMEM),
        ],
        out_specs=[pl.BlockSpec(memory_space=pltpu.VMEM)] * 2,
        out_shape=[pair_shape, pair_shape],
        scratch_shapes=[
            pltpu.VMEM((-(-block // LANES), windows_here * 2 * FREQS, LANES), jnp.float32)
        ],
        compiler_params=pltpu.CompilerParams(vmem_limit_bytes=32 << 20),
    )(
        jnp.stack([here, counts[0]]),
        samples,
        jnp.asarray(make_table(length, FREQS, FIRST_BIN)),
    )
    theirs = lax.ppermute(other, "tm", [(0, 1), (1, 0)])
    chunk_shape = jax.ShapeDtypeStruct((per_chunk, block, lanes), jnp.bfloat16)
    own = pl.pallas_call(
        functools.partial(merge_kernel, total_windows=total_windows),
        in_specs=[pl.BlockSpec(memory_space=pltpu.VMEM)] * 2,
        out_specs=[pl.BlockSpec(memory_space=pltpu.VMEM)] * CHUNKS,
        out_shape=[chunk_shape] * CHUNKS,
        compiler_params=pltpu.CompilerParams(vmem_limit_bytes=32 << 20),
    )(mine, theirs)

    down = [(i, i - 2) for i in range(2, fiber_size)]
    to_even = [(i, i - 1) for i in range(1, fiber_size, 2)]
    to_odd = [(i - 1, i) for i in range(1, fiber_size, 2)]

    def pick(for_even, for_odd):
        return jnp.where(is_even, for_even, for_odd)

    def move_down(for_even, for_odd):
        return lax.ppermute(pick(for_even, for_odd), "fiber", down)

    def cross(for_even, for_odd):
        return lax.ppermute(pick(for_even, for_odd), "fiber", to_even + to_odd)

    z, y = {}, {}
    z[0] = move_down(own[0], own[2])
    y[0] = lax.ppermute(own[0], "fiber", to_even)
    z[1] = move_down(own[1], own[3])
    y[1] = cross(z[0], own[1])
    z[2] = move_down(own[2], y[1])
    y[2] = cross(z[1], own[2])
    z[3] = move_down(own[3], y[2])
    y[3] = cross(z[2], own[3])
    z[4] = move_down(y[0], y[3])
    y[4] = cross(z[3], z[0])
    z[5] = move_down(y[1], y[4])
    y[5] = cross(z[4], z[1])
    y[6] = lax.ppermute(z[5], "fiber", to_odd)
    blocks = {
        0: ((y[0], y[1]), (z[0], y[5]), (z[4], z[2])),
        1: ((y[1], y[2]), (z[1], y[6]), (z[5], z[3])),
        2: ((y[2], y[3]), (z[2], z[0]), (y[4], z[4])),
        3: ((y[3], y[4]), (z[3], z[1]), (y[5], z[5])),
    }

    offsets = jnp.arange(1, -(-HOPS * block // LANES) * LANES + 1, dtype=jnp.int32)
    mask = (offsets[None, :] <= reach_limit[:, None]).astype(jnp.bfloat16)
    outs = None
    for chunk in (2, 0, 3, 1):
        outs = band(even, own[chunk], blocks[chunk], mask, outs, chunk, bins_here, total_windows)
    return tuple(outs)


def solution(mesh):
    placed = (P("tm", ("grp", "fiber"), None), P(("grp", "fiber")), P(("grp", "fiber")))
    return jax.shard_map(
        body,
        mesh=mesh,
        in_specs=placed,
        out_specs=(P("tm", ("grp", "fiber"), None), P("tm", ("grp", "fiber"), None)),
        check_vma=False,
    )
```

time: 624 us -> 133 us (0.21)
  local copies, waits for them, and re-layouts: 434 us -> 9.29 us
  other arithmetic: 38.4 us -> 1.42 us
  Pallas kernels: 0 us -> 30.5 us
  matrix products: 29.7 us -> 0 us
  waiting for transfers between devices: 93.3 us -> 74.5 us
    reshape x5 -> x0, local copies, waits for them, and re-layouts: 154 us -> none  [diagonal_band(): flattened.reshape(bins_here, rows, columns + 1)[:, :, 1:columns - rows + 1]]
    while x32 -> x0, local copies, waits for them, and re-layouts: 131 us -> none
    pad x5 -> x0, local copies, waits for them, and re-layouts: 47.9 us -> none  [diagonal_band(): flattened = jnp.pad(flattened, ((0, 0), (0, rows)))]
    dynamic_update_slice x2 -> x0, local copies, waits for them, and re-layouts: 36.4 us -> none  [banded_products(): band_real, band_imag = lax.map(tile_band, stacked)]
    convert_element_type x4 -> x1, other arithmetic: 32.2 us -> 0.17 us  [body(): mask = (offsets[None, :] <= reach_limit[:, None]).astype(jnp.bfloat16)]
    pallas_call x0 -> x6, Pallas kernels: none -> 30.5 us  [the longest x4 25.4 us: band(): pl.pallas_call(functools.partial(band_kernel, total_windows=total_windows...]
    dot_general x5 -> x0, matrix products: 29.7 us -> none  [the longest x2 15.4 us: tile_band(): jnp.einsum('fwc,fwj->fcj', left_turned, right_both, preferred_element_typ...]
    concatenate x4 -> x0, local copies, waits for them, and re-layouts: 22.9 us -> none  [the longest x2 11.6 us: body(): jnp.concatenate([imag_part] + [piece[1] for piece in pieces], axis=2)]
  transfers between devices with their start and end apart: 8 -> 14, of which waited for: 8 -> 11; matrix products, arithmetic and copies ran while one was open for 1% -> 0% of each run, Pallas kernels for 0% -> 14%
where the time goes in v1:
time: 133 us; the launch traced here: 132 us
  waiting for transfers between devices  74.5 us (56%)
  Pallas kernels  30.5 us (23%)
  starting transfers between devices  14.9 us (11%)
  local copies, waits for them, and re-layouts  9.29 us (7%)
  between operations  1.48 us (1%)
  other arithmetic  1.42 us (1%)
    ppermute x6, waiting for transfers between devices, move_down(): return lax.ppermute(pick(for_even, for_odd), 'fiber', down)  43.2 us
    ppermute x5, waiting for transfers between devices, cross(): return lax.ppermute(pick(for_even, for_odd), 'fiber', to_even + to_odd)  29.6 us
    pallas_call x4, Pallas kernels, band(): pl.pallas_call(functools.partial(band_kernel, total_windows=total_windows...  25.4 us
    unnamed x38, local copies, waits for them, and re-layouts  9.29 us
    ppermute x6, starting transfers between devices, move_down(): return lax.ppermute(pick(for_even, for_odd), 'fiber', down)  7.74 us
    pallas_call x1, Pallas kernels, body(): pl.pallas_call(spectra_kernel, in_specs=[pl.BlockSpec(memory_space=pltpu....  3.62 us
    ppermute x5, starting transfers between devices, cross(): return lax.ppermute(pick(for_even, for_odd), 'fiber', to_even + to_odd)  2.97 us
  transfers between devices with their start and end apart: 14, of which 11 were waited for; matrix products, arithmetic and copies ran while one was open for 0% of the time, Pallas kernels for 14%

profile of v1, /device:TPU:0, one launch (start us, length us, event | category | flops | bytes accessed | tf_op | source)
XLA Modules:
  0.0 132.0 jit_solution(5519152998346310948)
XLA Ops:
  1.4 1.7 %copy-done = bf16[32,320,128]{2,1,0:T(8,128)(2,1)S(1)} copy-done((bf16[32,320,128]{2,1,0:T(8,128)(2,1)S(1)}, bf16[32,320,128]{2,1,0:T(8,128)(2,1)}, u32[]{:S(2)}) %copy-start) | copy-done | bytes 2621464
  3.8 3.6 %shard_map.59 = (bf16[8,320,128]{2,1,0:T(8,128)(2,1)S(1)}, bf16[8,320,128]{2,1,0:T(8,128)(2,1)S(1)}) custom-call(s32[2]{0:T(128)S(1)} %pad_add_fusion.place_ref, bf16[32,320,128]{2,1,0:T(8,128)(2,1)S(1)} %copy-done, bf16[64,128]{1,0:T(8,128)(2,1)S(1)} %copy-done.17), custom_call_target="tpu_custom_call" | custom-call | tf_op jit(solution)/shard_map/pallas_call | solution.py:200
  8.0 1.7 %collective-permute-done.theirs_ref = bf16[8,320,128]{2,1,0:T(8,128)(2,1)S(1)} collective-permute-done((bf16[8,320,128]{2,1,0:T(8,128)(2,1)S(1)}, bf16[8,320,128]{2,1,0:T(8,128)(2,1)S(1)}, u32[]{:S(2)}, u32[]{:S(2)}) %collective-permute-start) | collective-permute-done | bytes 655392 | tf_op jit(solution)/shard_map/ppermute | solution.py:218
  9.7 1.4 %shard_map.60 = (bf16[4,320,128]{2,1,0:T(8,128)(2,1)S(1)}, bf16[4,320,128]{2,1,0:T(8,128)(2,1)S(1)}, bf16[4,320,128]{2,1,0:T(8,128)(2,1)S(1)}, bf16[4,320,128]{2,1,0:T(8,128)(2,1)S(1)}) custom-call(bf16[8,320,128]{2,1,0:T(8,128)(2,1)S(1)} %get-tuple-element.14.mine_ref, bf16[8,320,128]{2,1,0:T(8,128)(2,1)S(1)} %collective-permute-done.theirs_ref), custom_call_target="tpu_custom_call" | custom-call | tf_op jit(solution)/shard_map/pallas_call | solution.py:220
  11.1 1.3 collective-permute-start.1
  12.4 11.6 %collective-permute-done.1.refs_3_.refs_2_ = bf16[4,320,128]{2,1,0:T(8,128)(2,1)S(1)} collective-permute-done((bf16[4,320,128]{2,1,0:T(8,128)(2,1)S(1)}, bf16[4,320,128]{2,1,0:T(8,128)(2,1)S(1)}, u32[]{:S(2)}, u32[]{:S(2)}) %collective-permute-start.1) | collective-permute-done | bytes 327712 | tf_op jit(solution)/shard_map/ppermute | solution.py:236
  24.0 1.7 %collective-permute-start.2 = (bf16[4,320,128]{2,1,0:T(8,128)(2,1)S(1)}, bf16[4,320,128]{2,1,0:T(8,128)(2,1)S(1)}, u32[]{:S(2)}, u32[]{:S(2)}) collective-permute-start(bf16[4,320,128]{2,1,0:T(8,128)(2,1)S(1)} %broadcast_select_fusion.9), channel_id=1, source_target_pairs={{2,0},{6,4},{10,8},{14,12},{0,2},{4,6},{8,10},{12,14},{3,1},{7,5},... | collective-permute-start | bytes 983048 | tf_op jit(solution)/shard_map/ppermute | solution.py:239
  25.8 7.6 %collective-permute-done.2.refs_1_.refs_0_ = bf16[4,320,128]{2,1,0:T(8,128)(2,1)S(1)} collective-permute-done((bf16[4,320,128]{2,1,0:T(8,128)(2,1)S(1)}, bf16[4,320,128]{2,1,0:T(8,128)(2,1)S(1)}, u32[]{:S(2)}, u32[]{:S(2)}) %collective-permute-start.2) | collective-permute-done | bytes 327712 | tf_op jit(solution)/shard_map/ppermute | solution.py:239
  33.4 1.3 collective-permute-start.9
  34.7 1.3 collective-permute-start.11
  36.0 7.6 %collective-permute-done.9.refs_2_.refs_5_ = bf16[4,320,128]{2,1,0:T(8,128)(2,1)S(1)} collective-permute-done((bf16[4,320,128]{2,1,0:T(8,128)(2,1)S(1)}, bf16[4,320,128]{2,1,0:T(8,128)(2,1)S(1)}, u32[]{:S(2)}, u32[]{:S(2)}) %collective-permute-start.9) | collective-permute-done | bytes 327712 | tf_op jit(solution)/shard_map/ppermute | solution.py:236
  46.1 5.9 %collective-permute-done.10.refs_1_.refs_0_ = bf16[4,320,128]{2,1,0:T(8,128)(2,1)S(1)} collective-permute-done((bf16[4,320,128]{2,1,0:T(8,128)(2,1)S(1)}, bf16[4,320,128]{2,1,0:T(8,128)(2,1)S(1)}, u32[]{:S(2)}, u32[]{:S(2)}) %collective-permute-start.10) | collective-permute-done | bytes 327712 | tf_op jit(solution)/shard_map/ppermute | solution.py:239
  52.0 1.3 collective-permute-start.12
  53.7 8.2 %collective-permute-done.12.refs_5_.refs_4_ = bf16[4,320,128]{2,1,0:T(8,128)(2,1)S(1)} collective-permute-done((bf16[4,320,128]{2,1,0:T(8,128)(2,1)S(1)}, bf16[4,320,128]{2,1,0:T(8,128)(2,1)S(1)}, u32[]{:S(2)}, u32[]{:S(2)}) %collective-permute-start.12) | collective-permute-done | bytes 327712 | tf_op jit(solution)/shard_map/ppermute | solution.py:236
  62.7 7.1 %collective-permute-done.4.refs_0_.refs_1_ = bf16[4,320,128]{2,1,0:T(8,128)(2,1)S(1)} collective-permute-done((bf16[4,320,128]{2,1,0:T(8,128)(2,1)S(1)}, bf16[4,320,128]{2,1,0:T(8,128)(2,1)S(1)}, u32[]{:S(2)}, u32[]{:S(2)}) %collective-permute-start.4) | collective-permute-done | bytes 327712 | tf_op jit(solution)/shard_map/ppermute | solution.py:239
  71.2 7.7 %collective-permute-done.5.refs_2_.refs_5_ = bf16[4,320,128]{2,1,0:T(8,128)(2,1)S(1)} collective-permute-done((bf16[4,320,128]{2,1,0:T(8,128)(2,1)S(1)}, bf16[4,320,128]{2,1,0:T(8,128)(2,1)S(1)}, u32[]{:S(2)}, u32[]{:S(2)}) %collective-permute-start.5) | collective-permute-done | bytes 327712 | tf_op jit(solution)/shard_map/ppermute | solution.py:236
  79.0 9.1 %collective-permute-done.6.refs_4_.refs_1_ = bf16[4,320,128]{2,1,0:T(8,128)(2,1)S(1)} collective-permute-done((bf16[4,320,128]{2,1,0:T(8,128)(2,1)S(1)}, bf16[4,320,128]{2,1,0:T(8,128)(2,1)S(1)}, u32[]{:S(2)}, u32[]{:S(2)}) %collective-permute-start.6) | collective-permute-done | bytes 327712 | tf_op jit(solution)/shard_map/ppermute | solution.py:239
  88.1 1.3 collective-permute-start.7
  89.5 7.7 %collective-permute-done.7.refs_5_.refs_4_ = bf16[4,320,128]{2,1,0:T(8,128)(2,1)} collective-permute-done((bf16[4,320,128]{2,1,0:T(8,128)(2,1)S(1)}, bf16[4,320,128]{2,1,0:T(8,128)(2,1)}, u32[]{:S(2)}, u32[]{:S(2)}) %collective-permute-start.7) | collective-permute-done | bytes 327712 | tf_op jit(solution)/shard_map/ppermute | solution.py:236
  97.2 2.3 %collective-permute-start.8 = (bf16[4,320,128]{2,1,0:T(8,128)(2,1)}, bf16[4,320,128]{2,1,0:T(8,128)(2,1)}, u32[]{:S(2)}, u32[]{:S(2)}) collective-permute-start(bf16[4,320,128]{2,1,0:T(8,128)(2,1)} %collective-permute-done.7.refs_5_.refs_4_), channel_id=1, source_target_pairs={{0,2},{4,6},{8,10},{12,14},{1,3},{5,7},{9,11},{13,15},{16,18},{20,... | collective-permute-start | bytes 983048 | tf_op jit(solution)/shard_map/ppermute | solution.py:254
  104.6 5.6 %shard_map.61 = (bf16[16,320,960]{2,1,0:T(8,128)(2,1)}, bf16[16,320,960]{2,1,0:T(8,128)(2,1)}) custom-call(s32[1]{0:T(128)} %bitcast.even_ref, bf16[4,320,128]{2,1,0:T(8,128)(2,1)S(1)} %get-tuple-element.18.own_ref, bf16[4,320,128]{2,1,0:T(8,128)(2,1)S(1)} %copy-done.7, bf16[4,320,128]{2,1,0:T(8,128)(2,1)S(1)} %copy-done.4, ...), custom_call_target="tpu_custom_call" | custom-call | flops 838860800 | bytes 9830400 | tf_op jit(solution)/shard_map/pallas_call | solution.py:164
  112.1 6.6 %shard_map.62 = (bf16[16,320,960]{2,1,0:T(8,128)(2,1)}, bf16[16,320,960]{2,1,0:T(8,128)(2,1)}) custom-call(s32[1]{0:T(128)} %bitcast.even_ref, bf16[4,320,128]{2,1,0:T(8,128)(2,1)S(1)} %get-tuple-element.17.own_ref, bf16[4,320,128]{2,1,0:T(8,128)(2,1)S(1)} %copy-done.2, ...), custom_call_target="tpu_custom_call", output_to_operand_aliasing={{0}: (9, {}), {1}: (10, {})} | custom-call | flops 838860800 | bytes 9830400 | tf_op jit(solution)/shard_map/pallas_call | solution.py:164
  118.7 6.7 %shard_map.63 = (bf16[16,320,960]{2,1,0:T(8,128)(2,1)}, bf16[16,320,960]{2,1,0:T(8,128)(2,1)}) custom-call(s32[1]{0:T(128)} %bitcast.even_ref, bf16[4,320,128]{2,1,0:T(8,128)(2,1)S(1)} %get-tuple-element.19.own_ref, bf16[4,320,128]{2,1,0:T(8,128)(2,1)S(1)} %copy-done.5, ...), custom_call_target="tpu_custom_call", output_to_operand_aliasing={{0}: (9, {}), {1}: (10, {})} | custom-call | flops 838860800 | bytes 9830400 | tf_op jit(solution)/shard_map/pallas_call | solution.py:164
  125.4 6.6 %shard_map.64 = (bf16[16,320,960]{2,1,0:T(8,128)(2,1)}, bf16[16,320,960]{2,1,0:T(8,128)(2,1)}) custom-call(s32[1]{0:T(128)} %bitcast.even_ref, bf16[4,320,128]{2,1,0:T(8,128)(2,1)S(1)} %get-tuple-element.16.own_ref, bf16[4,320,128]{2,1,0:T(8,128)(2,1)S(1)} %collective-permute-done.2.refs_1_.refs_0_, ...), custom_call_target="tpu_custom_call", output_to_operand_aliasing={{0}: (9, {}), {1}: (10, {})} | custom-call | flops 838860800 | bytes 9830400 | tf_op jit(solution)/shard_map/pallas_call | solution.py:164
  (60 shorter events, 13.7 us)
Async XLA Ops:
  0.6 98.9 %copy-start.18 = (s32[320]{0:T(512)S(1)}, s32[320]{0:T(512)}, u32[]{:S(2)}) copy-start(s32[320]{0:T(512)} %param.6) | copy-start | bytes 3844
  1.4 1.7 %copy-start = (bf16[32,320,128]{2,1,0:T(8,128)(2,1)S(1)}, bf16[32,320,128]{2,1,0:T(8,128)(2,1)}, u32[]{:S(2)}) copy-start(bf16[32,320,128]{2,1,0:T(8,128)(2,1)} %samples_ref.1) | copy-start | bytes 7864324
  7.5 2.2 %collective-permute-start = (bf16[8,320,128]{2,1,0:T(8,128)(2,1)S(1)}, bf16[8,320,128]{2,1,0:T(8,128)(2,1)S(1)}, u32[]{:S(2)}, u32[]{:S(2)}) collective-permute-start(bf16[8,320,128]{2,1,0:T(8,128)(2,1)S(1)} %get-tuple-element.15), channel_id=1, source_target_pairs={{0,1},{1,0},{2,3},{3,2},{4,5},{5,4},{6,7},{7,6},{8,9},{9,8},{10,11... | collective-permute-start | bytes 1966088 | tf_op jit(solution)/shard_map/ppermute | solution.py:218
  11.1 12.9 %collective-permute-start.1 = (bf16[4,320,128]{2,1,0:T(8,128)(2,1)S(1)}, bf16[4,320,128]{2,1,0:T(8,128)(2,1)S(1)}, u32[]{:S(2)}, u32[]{:S(2)}) collective-permute-start(bf16[4,320,128]{2,1,0:T(8,128)(2,1)S(1)} %broadcast_select_fusion.10), channel_id=1, source_target_pairs={{4,0},{6,2},{8,4},{10,6},{12,8},{14,10},{5,1},{7,3},{9,5},{11,7},{... | collective-permute-start | bytes 983048 | tf_op jit(solution)/shard_map/ppermute | solution.py:236
  24.0 9.3 %collective-permute-start.2 = (bf16[4,320,128]{2,1,0:T(8,128)(2,1)S(1)}, bf16[4,320,128]{2,1,0:T(8,128)(2,1)S(1)}, u32[]{:S(2)}, u32[]{:S(2)}) collective-permute-start(bf16[4,320,128]{2,1,0:T(8,128)(2,1)S(1)} %broadcast_select_fusion.9), channel_id=1, source_target_pairs={{2,0},{6,4},{10,8},{14,12},{0,2},{4,6},{8,10},{12,14},{3,1},{7,5},... | collective-permute-start | bytes 983048 | tf_op jit(solution)/shard_map/ppermute | solution.py:239
  33.4 10.2 %collective-permute-start.9 = (bf16[4,320,128]{2,1,0:T(8,128)(2,1)S(1)}, bf16[4,320,128]{2,1,0:T(8,128)(2,1)S(1)}, u32[]{:S(2)}, u32[]{:S(2)}) collective-permute-start(bf16[4,320,128]{2,1,0:T(8,128)(2,1)S(1)} %broadcast_select_fusion.3), channel_id=1, source_target_pairs={{4,0},{6,2},{8,4},{10,6},{12,8},{14,10},{5,1},{7,3},{9,5},{11,7},{... | collective-permute-start | bytes 983048 | tf_op jit(solution)/shard_map/ppermute | solution.py:236
  34.7 11.4 %collective-permute-start.11 = (bf16[4,320,128]{2,1,0:T(8,128)(2,1)S(1)}, bf16[4,320,128]{2,1,0:T(8,128)(2,1)S(1)}, u32[]{:S(2)}, u32[]{:S(2)}) collective-permute-start(bf16[4,320,128]{2,1,0:T(8,128)(2,1)S(1)} %get-tuple-element.17.own_ref), channel_id=1, source_target_pairs={{2,0},{6,4},{10,8},{14,12},{3,1},{7,5},{11,9},{15,13},{18,16},{22,... | collective-permute-start | bytes 983048 | tf_op jit(solution)/shard_map/ppermute | solution.py:243
  43.7 8.3 %collective-permute-start.10 = (bf16[4,320,128]{2,1,0:T(8,128)(2,1)S(1)}, bf16[4,320,128]{2,1,0:T(8,128)(2,1)S(1)}, u32[]{:S(2)}, u32[]{:S(2)}) collective-permute-start(bf16[4,320,128]{2,1,0:T(8,128)(2,1)S(1)} %get-tuple-element.28), channel_id=1, source_target_pairs={{2,0},{6,4},{10,8},{14,12},{0,2},{4,6},{8,10},{12,14},{3,1},{7,5},... | collective-permute-start | bytes 983048 | tf_op jit(solution)/shard_map/ppermute | solution.py:239
  44.8 9.0 %collective-permute-start.3 = (bf16[4,320,128]{2,1,0:T(8,128)(2,1)S(1)}, bf16[4,320,128]{2,1,0:T(8,128)(2,1)S(1)}, u32[]{:S(2)}, u32[]{:S(2)}) collective-permute-start(bf16[4,320,128]{2,1,0:T(8,128)(2,1)S(1)} %get-tuple-element.29), channel_id=1, source_target_pairs={{4,0},{6,2},{8,4},{10,6},{12,8},{14,10},{5,1},{7,3},{9,5},{11,7},{... | collective-permute-start | bytes 983048 | tf_op jit(solution)/shard_map/ppermute | solution.py:236
  46.1 23.8 %copy-start.1 = (bf16[4,320,128]{2,1,0:T(8,128)(2,1)}, bf16[4,320,128]{2,1,0:T(8,128)(2,1)S(1)}, u32[]{:S(2)}) copy-start(bf16[4,320,128]{2,1,0:T(8,128)(2,1)S(1)} %collective-permute-done.11.refs_0_) | copy-start | bytes 983044
  51.9 1.8 %copy-start.3 = (bf16[4,320,128]{2,1,0:T(8,128)(2,1)}, bf16[4,320,128]{2,1,0:T(8,128)(2,1)S(1)}, u32[]{:S(2)}) copy-start(bf16[4,320,128]{2,1,0:T(8,128)(2,1)S(1)} %collective-permute-done.10.refs_1_.refs_0_) | copy-start | bytes 983044
  52.0 9.9 %collective-permute-start.12 = (bf16[4,320,128]{2,1,0:T(8,128)(2,1)S(1)}, bf16[4,320,128]{2,1,0:T(8,128)(2,1)S(1)}, u32[]{:S(2)}, u32[]{:S(2)}) collective-permute-start(bf16[4,320,128]{2,1,0:T(8,128)(2,1)S(1)} %broadcast_select_fusion.1), channel_id=1, source_target_pairs={{4,0},{6,2},{8,4},{10,6},{12,8},{14,10},{5,1},{7,3},{9,5},{11,7},{... | collective-permute-start | bytes 983048 | tf_op jit(solution)/shard_map/ppermute | solution.py:236
  61.9 37.6 %copy-start.14 = (bf16[4,320,128]{2,1,0:T(8,128)(2,1)}, bf16[4,320,128]{2,1,0:T(8,128)(2,1)S(1)}, u32[]{:S(2)}) copy-start(bf16[4,320,128]{2,1,0:T(8,128)(2,1)S(1)} %collective-permute-done.12.refs_5_.refs_4_) | copy-start | bytes 983044
  62.7 7.1 %collective-permute-start.4 = (bf16[4,320,128]{2,1,0:T(8,128)(2,1)S(1)}, bf16[4,320,128]{2,1,0:T(8,128)(2,1)S(1)}, u32[]{:S(2)}, u32[]{:S(2)}) collective-permute-start(bf16[4,320,128]{2,1,0:T(8,128)(2,1)S(1)} %get-tuple-element.27), channel_id=1, source_target_pairs={{2,0},{6,4},{10,8},{14,12},{0,2},{4,6},{8,10},{12,14},{3,1},{7,5},... | collective-permute-start | bytes 983048 | tf_op jit(solution)/shard_map/ppermute | solution.py:239
  69.8 27.4 %copy-start.6 = (bf16[4,320,128]{2,1,0:T(8,128)(2,1)}, bf16[4,320,128]{2,1,0:T(8,128)(2,1)S(1)}, u32[]{:S(2)}) copy-start(bf16[4,320,128]{2,1,0:T(8,128)(2,1)S(1)} %collective-permute-done.4.refs_0_.refs_1_) | copy-start | bytes 983044
  69.9 9.0 %collective-permute-start.5 = (bf16[4,320,128]{2,1,0:T(8,128)(2,1)S(1)}, bf16[4,320,128]{2,1,0:T(8,128)(2,1)S(1)}, u32[]{:S(2)}, u32[]{:S(2)}) collective-permute-start(bf16[4,320,128]{2,1,0:T(8,128)(2,1)S(1)} %broadcast_select_fusion.6), channel_id=1, source_target_pairs={{4,0},{6,2},{8,4},{10,6},{12,8},{14,10},{5,1},{7,3},{9,5},{11,7},{... | collective-permute-start | bytes 983048 | tf_op jit(solution)/shard_map/ppermute | solution.py:236
  78.9 9.2 %collective-permute-start.6 = (bf16[4,320,128]{2,1,0:T(8,128)(2,1)S(1)}, bf16[4,320,128]{2,1,0:T(8,128)(2,1)S(1)}, u32[]{:S(2)}, u32[]{:S(2)}) collective-permute-start(bf16[4,320,128]{2,1,0:T(8,128)(2,1)S(1)} %broadcast_select_fusion.5), channel_id=1, source_target_pairs={{2,0},{6,4},{10,8},{14,12},{0,2},{4,6},{8,10},{12,14},{3,1},{7,5},... | collective-permute-start | bytes 983048 | tf_op jit(solution)/shard_map/ppermute | solution.py:239
  88.1 11.5 %copy-start.9 = (bf16[4,320,128]{2,1,0:T(8,128)(2,1)}, bf16[4,320,128]{2,1,0:T(8,128)(2,1)S(1)}, u32[]{:S(2)}) copy-start(bf16[4,320,128]{2,1,0:T(8,128)(2,1)S(1)} %collective-permute-done.6.refs_4_.refs_1_) | copy-start | bytes 983044
  88.1 9.1 %collective-permute-start.7 = (bf16[4,320,128]{2,1,0:T(8,128)(2,1)S(1)}, bf16[4,320,128]{2,1,0:T(8,128)(2,1)}, u32[]{:S(2)}, u32[]{:S(2)}) collective-permute-start(bf16[4,320,128]{2,1,0:T(8,128)(2,1)S(1)} %broadcast_select_fusion.4), channel_id=1, source_target_pairs={{4,0},{6,2},{8,4},{10,6},{12,8},{14,10},{5,1},{7,3},{9,5},{11,7},{... | collective-permute-start | bytes 983048 | tf_op jit(solution)/shard_map/ppermute | solution.py:236
  89.4 20.8 %collective-permute-start.13 = (bf16[4,320,128]{2,1,0:T(8,128)(2,1)}, bf16[4,320,128]{2,1,0:T(8,128)(2,1)}, u32[]{:S(2)}, u32[]{:S(2)}) collective-permute-start(bf16[4,320,128]{2,1,0:T(8,128)(2,1)} %get-tuple-element.26), channel_id=1, source_target_pairs={{2,0},{6,4},{10,8},{14,12},{0,2},{4,6},{8,10},{12,14},{3,1},{7,5},... | collective-permute-start | bytes 983048 | tf_op jit(solution)/shard_map/ppermute | solution.py:239
  97.2 28.2 %collective-permute-start.8 = (bf16[4,320,128]{2,1,0:T(8,128)(2,1)}, bf16[4,320,128]{2,1,0:T(8,128)(2,1)}, u32[]{:S(2)}, u32[]{:S(2)}) collective-permute-start(bf16[4,320,128]{2,1,0:T(8,128)(2,1)} %collective-permute-done.7.refs_5_.refs_4_), channel_id=1, source_target_pairs={{0,2},{4,6},{8,10},{12,14},{1,3},{5,7},{9,11},{13,15},{16,18},{20,... | collective-permute-start | bytes 983048 | tf_op jit(solution)/shard_map/ppermute | solution.py:254
  112.1 6.6 %copy-start.5 = (bf16[4,320,128]{2,1,0:T(8,128)(2,1)S(1)}, bf16[4,320,128]{2,1,0:T(8,128)(2,1)}, u32[]{:S(2)}) copy-start(bf16[4,320,128]{2,1,0:T(8,128)(2,1)} %copy-done.3) | copy-start | bytes 983044
  112.1 6.6 %copy-start.11 = (bf16[4,320,128]{2,1,0:T(8,128)(2,1)S(1)}, bf16[4,320,128]{2,1,0:T(8,128)(2,1)}, u32[]{:S(2)}) copy-start(bf16[4,320,128]{2,1,0:T(8,128)(2,1)} %copy-done.9) | copy-start | bytes 983044
  118.7 6.7 %copy-start.8 = (bf16[4,320,128]{2,1,0:T(8,128)(2,1)S(1)}, bf16[4,320,128]{2,1,0:T(8,128)(2,1)}, u32[]{:S(2)}) copy-start(bf16[4,320,128]{2,1,0:T(8,128)(2,1)} %copy-done.6) | copy-start | bytes 983044
  (9 other events, 8.7 us)

commit v2 on v1

--- a/solution.py
+++ b/solution.py
@@ -16,6 +16,8 @@
 HOPS = 3
 ROWS = 64
 CHUNKS = 4
+AT_ONCE = 8
+VMEM = 60 << 20
 
 
 def make_table(length, bins, first_bin):
@@ -31,13 +33,14 @@
 
 
 def spectra_kernel(place_ref, samples_ref, table_ref, mine_ref, other_ref, raw_ref):
-    windows, block, _ = samples_ref.shape
+    at_once, block, _ = samples_ref.shape
+    step = pl.program_id(0)
     pairs = mine_ref.shape[0]
     here = place_ref[0]
     tiles = raw_ref.shape[0]
     channel = lax.broadcasted_iota(jnp.int32, (1, block), 1)
     active = (channel < place_ref[1]).astype(jnp.float32)
-    for w in range(windows):
+    for w in range(at_once):
         raw = lax.dot_general(
             table_ref[...], samples_ref[w], (((1,), (1,)), ((), ())),
             preferred_element_type=jnp.float32,
@@ -47,18 +50,23 @@
         for tile in range(tiles):
             start = tile * LANES
             width = min(LANES, block - start)
-            raw_ref[tile, w * 2 * FREQS : (w + 1) * 2 * FREQS, :width] = white[:, start : start + width]
-    for out_ref, first in ((mine_ref, here * 2 * pairs), (other_ref, (1 - here) * 2 * pairs)):
-        for pair in range(pairs):
-            for tile in range(tiles):
-                start = tile * LANES
-                width = min(LANES, block - start)
-                rows = [
-                    raw_ref[tile, pl.ds(first + 2 * pair + part, windows, stride=2 * FREQS), :]
-                    for part in (0, FREQS, 1, FREQS + 1)
-                ]
-                turned = jnp.concatenate(rows, axis=0).T
-                out_ref[pair, start : start + width, :] = turned[:width].astype(jnp.bfloat16)
+            rows = pl.ds(pl.multiple_of((step * at_once + w) * 2 * FREQS, 2 * FREQS), 2 * FREQS)
+            raw_ref[tile, rows, :width] = white[:, start : start + width]
+
+    @pl.when(step == pl.num_programs(0) - 1)
+    def _():
+        windows = raw_ref.shape[1] // (2 * FREQS)
+        for out_ref, first in ((mine_ref, here * 2 * pairs), (other_ref, (1 - here) * 2 * pairs)):
+            for pair in range(pairs):
+                for tile in range(tiles):
+                    start = tile * LANES
+                    width = min(LANES, block - start)
+                    rows = [
+                        raw_ref[tile, pl.ds(first + 2 * pair + part, windows, stride=2 * FREQS), :]
+                        for part in (0, FREQS, 1, FREQS + 1)
+                    ]
+                    turned = jnp.concatenate(rows, axis=0).T
+                    out_ref[pair, start : start + width, :] = turned[:width].astype(jnp.bfloat16)
 
 
 def merge_kernel(mine_ref, theirs_ref, *out_refs, total_windows):
@@ -180,7 +188,7 @@
             bytes_accessed=per_chunk * 4 * block * HOPS * block * 2,
             transcendentals=0,
         ),
-        compiler_params=pltpu.CompilerParams(vmem_limit_bytes=24 << 20),
+        compiler_params=pltpu.CompilerParams(vmem_limit_bytes=VMEM),
     )(*operands)
 
 
@@ -199,17 +207,18 @@
     pair_shape = jax.ShapeDtypeStruct((bins_here // 2, block, lanes), jnp.bfloat16)
     mine, other = pl.pallas_call(
         spectra_kernel,
+        grid=(windows_here // AT_ONCE,),
         in_specs=[
             pl.BlockSpec(memory_space=pltpu.SMEM),
-            pl.BlockSpec(memory_space=pltpu.VMEM),
-            pl.BlockSpec(memory_space=pltpu.VMEM),
+            pl.BlockSpec((AT_ONCE, block, length), lambda i: (i, 0, 0)),
+            pl.BlockSpec((2 * FREQS, length), lambda i: (0, 0)),
         ],
-        out_specs=[pl.BlockSpec(memory_space=pltpu.VMEM)] * 2,
+        out_specs=[pl.BlockSpec(pair_shape.shape, lambda i: (0, 0, 0))] * 2,
         out_shape=[pair_shape, pair_shape],
         scratch_shapes=[
             pltpu.VMEM((-(-block // LANES), windows_here * 2 * FREQS, LANES), jnp.float32)
         ],
-        compiler_params=pltpu.CompilerParams(vmem_limit_bytes=32 << 20),
+        compiler_params=pltpu.CompilerParams(vmem_limit_bytes=VMEM),
     )(
         jnp.stack([here, counts[0]]),
         samples,
@@ -230,7 +239,8 @@
     to_odd = [(i - 1, i) for i in range(1, fiber_size, 2)]
 
     def pick(for_even, for_odd):
-        return jnp.where(is_even, for_even, for_odd)
+        even_one, for_even, for_odd = lax.optimization_barrier((is_even, for_even, for_odd))
+        return lax.optimization_barrier(jnp.where(even_one, for_even, for_odd))
 
     def move_down(for_even, for_odd):
         return lax.ppermute(pick(for_even, for_odd), "fiber", down)
@@ -242,6 +252,7 @@
     z[0] = move_down(own[0], own[2])
     y[0] = lax.ppermute(own[0], "fiber", to_even)
     z[1] = move_down(own[1], own[3])
+    z[0], y[0] = lax.optimization_barrier((z[0], y[0]))
     y[1] = cross(z[0], own[1])
     z[2] = move_down(own[2], y[1])
     y[2] = cross(z[1], own[2])
@@ -251,19 +262,18 @@
     y[4] = cross(z[3], z[0])
     z[5] = move_down(y[1], y[4])
     y[5] = cross(z[4], z[1])
-    y[6] = lax.ppermute(z[5], "fiber", to_odd)
-    blocks = {
-        0: ((y[0], y[1]), (z[0], y[5]), (z[4], z[2])),
-        1: ((y[1], y[2]), (z[1], y[6]), (z[5], z[3])),
-        2: ((y[2], y[3]), (z[2], z[0]), (y[4], z[4])),
-        3: ((y[3], y[4]), (z[3], z[1]), (y[5], z[5])),
-    }
-
     offsets = jnp.arange(1, -(-HOPS * block // LANES) * LANES + 1, dtype=jnp.int32)
     mask = (offsets[None, :] <= reach_limit[:, None]).astype(jnp.bfloat16)
-    outs = None
-    for chunk in (2, 0, 3, 1):
-        outs = band(even, own[chunk], blocks[chunk], mask, outs, chunk, bins_here, total_windows)
+
+    def work(outs, chunk, *pieces):
+        return band(even, own[chunk], pieces, mask, outs, chunk, bins_here, total_windows)
+
+    outs = work(None, 2, (y[2], y[3]), (z[2], z[0]), (y[4], z[4]))
+    z[5], *outs = lax.optimization_barrier((z[5], *outs))
+    y[6] = lax.ppermute(z[5], "fiber", to_odd)
+    outs = work(outs, 0, (y[0], y[1]), (z[0], y[5]), (z[4], z[2]))
+    outs = work(outs, 3, (y[3], y[4]), (z[3], z[1]), (y[5], z[5]))
+    outs = work(outs, 1, (y[1], y[2]), (z[1], y[6]), (z[5], z[3]))
     return tuple(outs)
 
 

time: 133 us -> 104 us (0.78)
  waiting for transfers between devices: 74.5 us -> 38.3 us
  Pallas kernels: 30.5 us -> 37.3 us
  local copies, waits for them, and re-layouts: 9.29 us -> 4.07 us
  starting transfers between devices: 14.9 us -> 17.7 us
  other arithmetic: 1.42 us -> 3.47 us
    ppermute x6, waiting for transfers between devices: 43.2 us -> 24.1 us  [move_down(): return lax.ppermute(pick(for_even, for_odd), 'fiber', down)]
    ppermute x5, waiting for transfers between devices: 29.6 us -> 12.1 us  [cross(): return lax.ppermute(pick(for_even, for_odd), 'fiber', to_even + to_odd)]
    unnamed x38 -> x34, local copies, waits for them, and re-layouts: 9.29 us -> 4.07 us
    pallas_call x4, Pallas kernels: 25.4 us -> 29.7 us  [band(): pl.pallas_call(functools.partial(band_kernel, total_windows=total_windows...]
    ppermute x5, starting transfers between devices: 2.97 us -> 6.23 us  [cross(): return lax.ppermute(pick(for_even, for_odd), 'fiber', to_even + to_odd)]
    pallas_call x1, Pallas kernels: 3.62 us -> 6.17 us  [body(): pl.pallas_call(spectra_kernel, grid=(windows_here // AT_ONCE,), in_specs=...]
  transfers between devices with their start and end apart: 14 -> 14, of which waited for: 11 -> 10; matrix products, arithmetic and copies ran while one was open for 0% -> 3% of each run, Pallas kernels for 14% -> 22%
where the time goes in v2:
time: 104 us; the launch traced here: 102 us
  waiting for transfers between devices  38.3 us (37%)
  Pallas kernels  37.3 us (36%)
  starting transfers between devices  17.7 us (17%)
  local copies, waits for them, and re-layouts  4.07 us (4%)
  other arithmetic  3.47 us (3%)
  between operations  1.55 us (1%)
    pallas_call x4, Pallas kernels, band(): pl.pallas_call(functools.partial(band_kernel, total_windows=total_windows...  29.7 us
    ppermute x6, waiting for transfers between devices, move_down(): return lax.ppermute(pick(for_even, for_odd), 'fiber', down)  24.1 us
    ppermute x5, waiting for transfers between devices, cross(): return lax.ppermute(pick(for_even, for_odd), 'fiber', to_even + to_odd)  12.1 us
    ppermute x6, starting transfers between devices, move_down(): return lax.ppermute(pick(for_even, for_odd), 'fiber', down)  7.74 us
    ppermute x5, starting transfers between devices, cross(): return lax.ppermute(pick(for_even, for_odd), 'fiber', to_even + to_odd)  6.23 us
    pallas_call x1, Pallas kernels, body(): pl.pallas_call(spectra_kernel, grid=(windows_here // AT_ONCE,), in_specs=...  6.17 us
    unnamed x34, local copies, waits for them, and re-layouts  4.07 us
  transfers between devices with their start and end apart: 14, of which 10 were waited for; matrix products, arithmetic and copies ran while one was open for 3% of the time, Pallas kernels for 22%

profile of v2, /device:TPU:0, one launch (start us, length us, event | category | flops | bytes accessed | tf_op | source)
XLA Modules:
  0.0 102.3 jit_solution(7983461067264540928)
XLA Ops:
  1.9 6.2 %shard_map.59 = (bf16[8,320,128]{2,1,0:T(8,128)(2,1)}, bf16[8,320,128]{2,1,0:T(8,128)(2,1)}) custom-call(s32[2]{0:T(128)} %pad_add_fusion.place_ref, bf16[32,320,128]{2,1,0:T(8,128)(2,1)} %samples_ref.1, bf16[64,128]{1,0:T(8,128)(2,1)} %constant.25.clone.table_ref), custom_call_target="tpu_custom_call" | custom-call | tf_op jit(solution)/shard_map/pallas_call | solution.py:208
  8.5 1.9 %collective-permute-done.theirs_ref = bf16[8,320,128]{2,1,0:T(8,128)(2,1)S(1)} collective-permute-done((bf16[8,320,128]{2,1,0:T(8,128)(2,1)}, bf16[8,320,128]{2,1,0:T(8,128)(2,1)S(1)}, u32[]{:S(2)}, u32[]{:S(2)}) %collective-permute-start) | collective-permute-done | bytes 655392 | tf_op jit(solution)/shard_map/ppermute | solution.py:227
  11.5 1.4 %shard_map.60 = (bf16[4,320,128]{2,1,0:T(8,128)(2,1)S(1)}, bf16[4,320,128]{2,1,0:T(8,128)(2,1)S(1)}, bf16[4,320,128]{2,1,0:T(8,128)(2,1)S(1)}, bf16[4,320,128]{2,1,0:T(8,128)(2,1)S(1)}) custom-call(bf16[8,320,128]{2,1,0:T(8,128)(2,1)S(1)} %copy-done.4, bf16[8,320,128]{2,1,0:T(8,128)(2,1)S(1)} %collective-permute-done.theirs_ref), custom_call_target="tpu_custom_call" | custom-call | tf_op jit(solution)/shard_map/pallas_call | solution.py:229
  13.0 1.3 %collective-permute-start.1 = (bf16[4,320,128]{2,1,0:T(8,128)(2,1)S(1)}, bf16[4,320,128]{2,1,0:T(8,128)(2,1)S(1)}, u32[]{:S(2)}, u32[]{:S(2)}) collective-permute-start(bf16[4,320,128]{2,1,0:T(8,128)(2,1)S(1)} %broadcast_select_fusion.10), channel_id=1, source_target_pairs={{4,0},{6,2},{8,4},{10,6},{12,8},{14,10},{5,1},{7,3},{9,5},{11,7},{... | collective-permute-start | bytes 983048 | tf_op jit(solution)/shard_map/ppermute | solution.py:246
  14.3 1.3 %collective-permute-start.2 = (bf16[4,320,128]{2,1,0:T(8,128)(2,1)S(1)}, bf16[4,320,128]{2,1,0:T(8,128)(2,1)S(1)}, u32[]{:S(2)}, u32[]{:S(2)}) collective-permute-start(bf16[4,320,128]{2,1,0:T(8,128)(2,1)S(1)} %get-tuple-element.58.own_ref), channel_id=1, source_target_pairs={{2,0},{6,4},{10,8},{14,12},{3,1},{7,5},{11,9},{15,13},{18,16},{22,... | collective-permute-start | bytes 983048 | tf_op jit(solution)/shard_map/ppermute | solution.py:253
  15.6 1.3 %collective-permute-start.4 = (bf16[4,320,128]{2,1,0:T(8,128)(2,1)S(1)}, bf16[4,320,128]{2,1,0:T(8,128)(2,1)S(1)}, u32[]{:S(2)}, u32[]{:S(2)}) collective-permute-start(bf16[4,320,128]{2,1,0:T(8,128)(2,1)S(1)} %broadcast_select_fusion.8), channel_id=1, source_target_pairs={{4,0},{6,2},{8,4},{10,6},{12,8},{14,10},{5,1},{7,3},{9,5},{11,7},{... | collective-permute-start | bytes 983048 | tf_op jit(solution)/shard_map/ppermute | solution.py:246
  16.9 9.4 %collective-permute-done.1.refs_3_.refs_2_ = bf16[4,320,128]{2,1,0:T(8,128)(2,1)S(1)} collective-permute-done((bf16[4,320,128]{2,1,0:T(8,128)(2,1)S(1)}, bf16[4,320,128]{2,1,0:T(8,128)(2,1)S(1)}, u32[]{:S(2)}, u32[]{:S(2)}) %collective-permute-start.1) | collective-permute-done | bytes 327712 | tf_op jit(solution)/shard_map/ppermute | solution.py:246
  26.5 1.9 %collective-permute-start.3 = (bf16[4,320,128]{2,1,0:T(8,128)(2,1)S(1)}, bf16[4,320,128]{2,1,0:T(8,128)(2,1)S(1)}, u32[]{:S(2)}, u32[]{:S(2)}) collective-permute-start(bf16[4,320,128]{2,1,0:T(8,128)(2,1)S(1)} %broadcast_select_fusion.9), channel_id=1, source_target_pairs={{2,0},{6,4},{10,8},{14,12},{0,2},{4,6},{8,10},{12,14},{3,1},{7,5},... | collective-permute-start | bytes 983048 | tf_op jit(solution)/shard_map/ppermute | solution.py:249
  28.5 4.4 %collective-permute-done.4.refs_3_.refs_2_ = bf16[4,320,128]{2,1,0:T(8,128)(2,1)S(1)} collective-permute-done((bf16[4,320,128]{2,1,0:T(8,128)(2,1)S(1)}, bf16[4,320,128]{2,1,0:T(8,128)(2,1)S(1)}, u32[]{:S(2)}, u32[]{:S(2)}) %collective-permute-start.4) | collective-permute-done | bytes 327712 | tf_op jit(solution)/shard_map/ppermute | solution.py:246
  32.9 1.7 %collective-permute-start.5 = (bf16[4,320,128]{2,1,0:T(8,128)(2,1)S(1)}, bf16[4,320,128]{2,1,0:T(8,128)(2,1)S(1)}, u32[]{:S(2)}, u32[]{:S(2)}) collective-permute-start(bf16[4,320,128]{2,1,0:T(8,128)(2,1)S(1)} %broadcast_select_fusion.7), channel_id=1, source_target_pairs={{2,0},{6,4},{10,8},{14,12},{0,2},{4,6},{8,10},{12,14},{3,1},{7,5},... | collective-permute-start | bytes 983048 | tf_op jit(solution)/shard_map/ppermute | solution.py:249
  34.7 1.7 %collective-permute-done.3.refs_1_.refs_0_ = bf16[4,320,128]{2,1,0:T(8,128)(2,1)S(1)} collective-permute-done((bf16[4,320,128]{2,1,0:T(8,128)(2,1)S(1)}, bf16[4,320,128]{2,1,0:T(8,128)(2,1)S(1)}, u32[]{:S(2)}, u32[]{:S(2)}) %collective-permute-start.3) | collective-permute-done | bytes 327712 | tf_op jit(solution)/shard_map/ppermute | solution.py:249
  36.4 1.3 %collective-permute-start.9 = (bf16[4,320,128]{2,1,0:T(8,128)(2,1)S(1)}, bf16[4,320,128]{2,1,0:T(8,128)(2,1)S(1)}, u32[]{:S(2)}, u32[]{:S(2)}) collective-permute-start(bf16[4,320,128]{2,1,0:T(8,128)(2,1)S(1)} %broadcast_select_fusion.3), channel_id=1, source_target_pairs={{4,0},{6,2},{8,4},{10,6},{12,8},{14,10},{5,1},{7,3},{9,5},{11,7},{... | collective-permute-start | bytes 983048 | tf_op jit(solution)/shard_map/ppermute | solution.py:246
  37.7 5.1 %collective-permute-done.5.refs_0_.refs_1_ = bf16[4,320,128]{2,1,0:T(8,128)(2,1)S(1)} collective-permute-done((bf16[4,320,128]{2,1,0:T(8,128)(2,1)S(1)}, bf16[4,320,128]{2,1,0:T(8,128)(2,1)S(1)}, u32[]{:S(2)}, u32[]{:S(2)}) %collective-permute-start.5) | collective-permute-done | bytes 327712 | tf_op jit(solution)/shard_map/ppermute | solution.py:249
  42.9 1.3 %collective-permute-start.6 = (bf16[4,320,128]{2,1,0:T(8,128)(2,1)S(1)}, bf16[4,320,128]{2,1,0:T(8,128)(2,1)S(1)}, u32[]{:S(2)}, u32[]{:S(2)}) collective-permute-start(bf16[4,320,128]{2,1,0:T(8,128)(2,1)S(1)} %broadcast_select_fusion.6), channel_id=1, source_target_pairs={{4,0},{6,2},{8,4},{10,6},{12,8},{14,10},{5,1},{7,3},{9,5},{11,7},{... | collective-permute-start | bytes 983048 | tf_op jit(solution)/shard_map/ppermute | solution.py:246
  44.2 3.5 %collective-permute-done.9.refs_2_.refs_5_ = bf16[4,320,128]{2,1,0:T(8,128)(2,1)S(1)} collective-permute-done((bf16[4,320,128]{2,1,0:T(8,128)(2,1)S(1)}, bf16[4,320,128]{2,1,0:T(8,128)(2,1)S(1)}, u32[]{:S(2)}, u32[]{:S(2)}) %collective-permute-start.9) | collective-permute-done | bytes 327712 | tf_op jit(solution)/shard_map/ppermute | solution.py:246
  47.8 6.5 %collective-permute-done.6.refs_2_.refs_5_ = bf16[4,320,128]{2,1,0:T(8,128)(2,1)S(1)} collective-permute-done((bf16[4,320,128]{2,1,0:T(8,128)(2,1)S(1)}, bf16[4,320,128]{2,1,0:T(8,128)(2,1)S(1)}, u32[]{:S(2)}, u32[]{:S(2)}) %collective-permute-start.6) | collective-permute-done | bytes 327712 | tf_op jit(solution)/shard_map/ppermute | solution.py:246
  55.7 1.3 %collective-permute-start.11 = (bf16[4,320,128]{2,1,0:T(8,128)(2,1)S(1)}, bf16[4,320,128]{2,1,0:T(8,128)(2,1)S(1)}, u32[]{:S(2)}, u32[]{:S(2)}) collective-permute-start(bf16[4,320,128]{2,1,0:T(8,128)(2,1)S(1)} %broadcast_select_fusion.1), channel_id=1, source_target_pairs={{4,0},{6,2},{8,4},{10,6},{12,8},{14,10},{5,1},{7,3},{9,5},{11,7},{... | collective-permute-start | bytes 983048 | tf_op jit(solution)/shard_map/ppermute | solution.py:246
  57.0 5.3 %collective-permute-done.7.refs_4_.refs_1_ = bf16[4,320,128]{2,1,0:T(8,128)(2,1)S(1)} collective-permute-done((bf16[4,320,128]{2,1,0:T(8,128)(2,1)S(1)}, bf16[4,320,128]{2,1,0:T(8,128)(2,1)S(1)}, u32[]{:S(2)}, u32[]{:S(2)}) %collective-permute-start.7) | collective-permute-done | bytes 327712 | tf_op jit(solution)/shard_map/ppermute | solution.py:249
  66.8 2.0 %collective-permute-start.13 = (bf16[4,320,128]{2,1,0:T(8,128)(2,1)}, bf16[4,320,128]{2,1,0:T(8,128)(2,1)}, u32[]{:S(2)}, u32[]{:S(2)}) collective-permute-start(bf16[4,320,128]{2,1,0:T(8,128)(2,1)} %broadcast_select_fusion), channel_id=1, source_target_pairs={{2,0},{6,4},{10,8},{14,12},{0,2},{4,6},{8,10},{12,14},{3,1},{7,5},... | collective-permute-start | bytes 983048 | tf_op jit(solution)/shard_map/ppermute | solution.py:249
  69.8 7.4 %shard_map.61 = (bf16[16,320,960]{2,1,0:T(8,128)(2,1)}, bf16[16,320,960]{2,1,0:T(8,128)(2,1)}) custom-call(s32[1]{0:T(128)} %bitcast.even_ref, bf16[4,320,128]{2,1,0:T(8,128)(2,1)} %copy-done.1, bf16[4,320,128]{2,1,0:T(8,128)(2,1)} %copy-done.10, bf16[4,320,128]{2,1,0:T(8,128)(2,1)} %copy-done.12, bf16[4,320,128]{2,1,0:T(8,128)(2,1)} %copy-done.11, ...), custom_call_target="tpu_custom_call" | custom-call | flops 838860800 | bytes 9830400 | tf_op jit(solution)/shard_map/pallas_call | solution.py:172
  77.2 1.9 %collective-permute-start.12 = (bf16[4,320,128]{2,1,0:T(8,128)(2,1)}, bf16[4,320,128]{2,1,0:T(8,128)(2,1)S(1)}, u32[]{:S(2)}, u32[]{:S(2)}) collective-permute-start(bf16[4,320,128]{2,1,0:T(8,128)(2,1)} %collective-permute-done.8.refs_5_.refs_4_), channel_id=1, source_target_pairs={{0,2},{4,6},{8,10},{12,14},{1,3},{5,7},{9,11},{13,15},{16,18},{20,... | collective-permute-start | bytes 983048 | tf_op jit(solution)/shard_map/ppermute | solution.py:273
  79.2 7.4 %shard_map.62 = (bf16[16,320,960]{2,1,0:T(8,128)(2,1)}, bf16[16,320,960]{2,1,0:T(8,128)(2,1)}) custom-call(s32[1]{0:T(128)} %bitcast.even_ref, bf16[4,320,128]{2,1,0:T(8,128)(2,1)} %copy-done.3, bf16[4,320,128]{2,1,0:T(8,128)(2,1)} %copy-done.9, bf16[4,320,128]{2,1,0:T(8,128)(2,1)} %copy-done.6, ...), custom_call_target="tpu_custom_call", output_to_operand_aliasing={{0}: (9, {}), {1}: (10, {})} | custom-call | flops 838860800 | bytes 9830400 | tf_op jit(solution)/shard_map/pallas_call | solution.py:172
  86.7 7.4 %shard_map.63 = (bf16[16,320,960]{2,1,0:T(8,128)(2,1)}, bf16[16,320,960]{2,1,0:T(8,128)(2,1)}) custom-call(s32[1]{0:T(128)} %bitcast.even_ref, bf16[4,320,128]{2,1,0:T(8,128)(2,1)} %copy-done, bf16[4,320,128]{2,1,0:T(8,128)(2,1)} %copy-done.12, bf16[4,320,128]{2,1,0:T(8,128)(2,1)} %copy-done.13, ...), custom_call_target="tpu_custom_call", output_to_operand_aliasing={{0}: (9, {}), {1}: (10, {})} | custom-call | flops 838860800 | bytes 9830400 | tf_op jit(solution)/shard_map/pallas_call | solution.py:172
  94.9 7.4 %shard_map.64 = (bf16[16,320,960]{2,1,0:T(8,128)(2,1)}, bf16[16,320,960]{2,1,0:T(8,128)(2,1)}) custom-call(s32[1]{0:T(128)} %bitcast.even_ref, bf16[4,320,128]{2,1,0:T(8,128)(2,1)} %copy-done.2, bf16[4,320,128]{2,1,0:T(8,128)(2,1)} %copy-done.6, bf16[4,320,128]{2,1,0:T(8,128)(2,1)} %copy-done.10, ...), custom_call_target="tpu_custom_call", output_to_operand_aliasing={{0}: (9, {}), {1}: (10, {})} | custom-call | flops 838860800 | bytes 9830400 | tf_op jit(solution)/shard_map/pallas_call | solution.py:172
  (58 shorter events, 10.3 us)
Async XLA Ops:
  0.6 68.1 %copy-start.16 = (s32[320]{0:T(512)S(1)}, s32[320]{0:T(512)}, u32[]{:S(2)}) copy-start(s32[320]{0:T(512)} %param.6) | copy-start | bytes 3844
  8.1 2.4 %collective-permute-start = (bf16[8,320,128]{2,1,0:T(8,128)(2,1)}, bf16[8,320,128]{2,1,0:T(8,128)(2,1)S(1)}, u32[]{:S(2)}, u32[]{:S(2)}) collective-permute-start(bf16[8,320,128]{2,1,0:T(8,128)(2,1)} %get-tuple-element.53), channel_id=1, source_target_pairs={{0,1},{1,0},{2,3},{3,2},{4,5},{5,4},{6,7},{7,6},{8,9},{9,8},{10,11... | collective-permute-start | bytes 1966088 | tf_op jit(solution)/shard_map/ppermute | solution.py:227
  12.9 56.9 %copy-start.1 = (bf16[4,320,128]{2,1,0:T(8,128)(2,1)}, bf16[4,320,128]{2,1,0:T(8,128)(2,1)S(1)}, u32[]{:S(2)}) copy-start(bf16[4,320,128]{2,1,0:T(8,128)(2,1)S(1)} %get-tuple-element.81.own_ref) | copy-start | bytes 983044
  12.9 66.3 %copy-start.3 = (bf16[4,320,128]{2,1,0:T(8,128)(2,1)}, bf16[4,320,128]{2,1,0:T(8,128)(2,1)S(1)}, u32[]{:S(2)}) copy-start(bf16[4,320,128]{2,1,0:T(8,128)(2,1)S(1)} %get-tuple-element.58.own_ref) | copy-start | bytes 983044
  12.9 73.7 %copy-start = (bf16[4,320,128]{2,1,0:T(8,128)(2,1)}, bf16[4,320,128]{2,1,0:T(8,128)(2,1)S(1)}, u32[]{:S(2)}) copy-start(bf16[4,320,128]{2,1,0:T(8,128)(2,1)S(1)} %get-tuple-element.85.own_ref) | copy-start | bytes 983044
  12.9 73.7 %copy-start.2 = (bf16[4,320,128]{2,1,0:T(8,128)(2,1)}, bf16[4,320,128]{2,1,0:T(8,128)(2,1)S(1)}, u32[]{:S(2)}) copy-start(bf16[4,320,128]{2,1,0:T(8,128)(2,1)S(1)} %get-tuple-element.66.own_ref) | copy-start | bytes 983044
  13.0 13.3 %collective-permute-start.1 = (bf16[4,320,128]{2,1,0:T(8,128)(2,1)S(1)}, bf16[4,320,128]{2,1,0:T(8,128)(2,1)S(1)}, u32[]{:S(2)}, u32[]{:S(2)}) collective-permute-start(bf16[4,320,128]{2,1,0:T(8,128)(2,1)S(1)} %broadcast_select_fusion.10), channel_id=1, source_target_pairs={{4,0},{6,2},{8,4},{10,6},{12,8},{14,10},{5,1},{7,3},{9,5},{11,7},{... | collective-permute-start | bytes 983048 | tf_op jit(solution)/shard_map/ppermute | solution.py:246
  14.3 12.2 %collective-permute-start.2 = (bf16[4,320,128]{2,1,0:T(8,128)(2,1)S(1)}, bf16[4,320,128]{2,1,0:T(8,128)(2,1)S(1)}, u32[]{:S(2)}, u32[]{:S(2)}) collective-permute-start(bf16[4,320,128]{2,1,0:T(8,128)(2,1)S(1)} %get-tuple-element.58.own_ref), channel_id=1, source_target_pairs={{2,0},{6,4},{10,8},{14,12},{3,1},{7,5},{11,9},{15,13},{18,16},{22,... | collective-permute-start | bytes 983048 | tf_op jit(solution)/shard_map/ppermute | solution.py:253
  15.6 17.2 %collective-permute-start.4 = (bf16[4,320,128]{2,1,0:T(8,128)(2,1)S(1)}, bf16[4,320,128]{2,1,0:T(8,128)(2,1)S(1)}, u32[]{:S(2)}, u32[]{:S(2)}) collective-permute-start(bf16[4,320,128]{2,1,0:T(8,128)(2,1)S(1)} %broadcast_select_fusion.8), channel_id=1, source_target_pairs={{4,0},{6,2},{8,4},{10,6},{12,8},{14,10},{5,1},{7,3},{9,5},{11,7},{... | collective-permute-start | bytes 983048 | tf_op jit(solution)/shard_map/ppermute | solution.py:246
  26.3 43.4 %copy-start.7 = (bf16[4,320,128]{2,1,0:T(8,128)(2,1)}, bf16[4,320,128]{2,1,0:T(8,128)(2,1)S(1)}, u32[]{:S(2)}) copy-start(bf16[4,320,128]{2,1,0:T(8,128)(2,1)S(1)} %collective-permute-done.1.refs_3_.refs_2_) | copy-start | bytes 983044
  26.5 52.7 %copy-start.9 = (bf16[4,320,128]{2,1,0:T(8,128)(2,1)}, bf16[4,320,128]{2,1,0:T(8,128)(2,1)S(1)}, u32[]{:S(2)}) copy-start(bf16[4,320,128]{2,1,0:T(8,128)(2,1)S(1)} %collective-permute-done.2.refs_0_) | copy-start | bytes 983044
  26.5 9.9 %collective-permute-start.3 = (bf16[4,320,128]{2,1,0:T(8,128)(2,1)S(1)}, bf16[4,320,128]{2,1,0:T(8,128)(2,1)S(1)}, u32[]{:S(2)}, u32[]{:S(2)}) collective-permute-start(bf16[4,320,128]{2,1,0:T(8,128)(2,1)S(1)} %broadcast_select_fusion.9), channel_id=1, source_target_pairs={{2,0},{6,4},{10,8},{14,12},{0,2},{4,6},{8,10},{12,14},{3,1},{7,5},... | collective-permute-start | bytes 983048 | tf_op jit(solution)/shard_map/ppermute | solution.py:249
  32.9 53.8 %copy-start.5 = (bf16[4,320,128]{2,1,0:T(8,128)(2,1)}, bf16[4,320,128]{2,1,0:T(8,128)(2,1)S(1)}, u32[]{:S(2)}) copy-start(bf16[4,320,128]{2,1,0:T(8,128)(2,1)S(1)} %collective-permute-done.4.refs_3_.refs_2_) | copy-start | bytes 983044
  32.9 9.9 %collective-permute-start.5 = (bf16[4,320,128]{2,1,0:T(8,128)(2,1)S(1)}, bf16[4,320,128]{2,1,0:T(8,128)(2,1)S(1)}, u32[]{:S(2)}, u32[]{:S(2)}) collective-permute-start(bf16[4,320,128]{2,1,0:T(8,128)(2,1)S(1)} %broadcast_select_fusion.7), channel_id=1, source_target_pairs={{2,0},{6,4},{10,8},{14,12},{0,2},{4,6},{8,10},{12,14},{3,1},{7,5},... | collective-permute-start | bytes 983048 | tf_op jit(solution)/shard_map/ppermute | solution.py:249
  36.4 42.8 %copy-start.6 = (bf16[4,320,128]{2,1,0:T(8,128)(2,1)}, bf16[4,320,128]{2,1,0:T(8,128)(2,1)S(1)}, u32[]{:S(2)}) copy-start(bf16[4,320,128]{2,1,0:T(8,128)(2,1)S(1)} %collective-permute-done.3.refs_1_.refs_0_) | copy-start | bytes 983044
  36.4 11.3 %collective-permute-start.9 = (bf16[4,320,128]{2,1,0:T(8,128)(2,1)S(1)}, bf16[4,320,128]{2,1,0:T(8,128)(2,1)S(1)}, u32[]{:S(2)}, u32[]{:S(2)}) collective-permute-start(bf16[4,320,128]{2,1,0:T(8,128)(2,1)S(1)} %broadcast_select_fusion.3), channel_id=1, source_target_pairs={{4,0},{6,2},{8,4},{10,6},{12,8},{14,10},{5,1},{7,3},{9,5},{11,7},{... | collective-permute-start | bytes 983048 | tf_op jit(solution)/shard_map/ppermute | solution.py:246
  42.9 11.4 %collective-permute-start.6 = (bf16[4,320,128]{2,1,0:T(8,128)(2,1)S(1)}, bf16[4,320,128]{2,1,0:T(8,128)(2,1)S(1)}, u32[]{:S(2)}, u32[]{:S(2)}) collective-permute-start(bf16[4,320,128]{2,1,0:T(8,128)(2,1)S(1)} %broadcast_select_fusion.6), channel_id=1, source_target_pairs={{4,0},{6,2},{8,4},{10,6},{12,8},{14,10},{5,1},{7,3},{9,5},{11,7},{... | collective-permute-start | bytes 983048 | tf_op jit(solution)/shard_map/ppermute | solution.py:246
  47.8 7.1 %collective-permute-start.10 = (bf16[4,320,128]{2,1,0:T(8,128)(2,1)S(1)}, bf16[4,320,128]{2,1,0:T(8,128)(2,1)S(1)}, u32[]{:S(2)}, u32[]{:S(2)}) collective-permute-start(bf16[4,320,128]{2,1,0:T(8,128)(2,1)S(1)} %broadcast_select_fusion.2), channel_id=1, source_target_pairs={{2,0},{6,4},{10,8},{14,12},{0,2},{4,6},{8,10},{12,14},{3,1},{7,5},... | collective-permute-start | bytes 983048 | tf_op jit(solution)/shard_map/ppermute | solution.py:249
  54.3 32.4 %copy-start.8 = (bf16[4,320,128]{2,1,0:T(8,128)(2,1)}, bf16[4,320,128]{2,1,0:T(8,128)(2,1)S(1)}, u32[]{:S(2)}) copy-start(bf16[4,320,128]{2,1,0:T(8,128)(2,1)S(1)} %collective-permute-done.6.refs_2_.refs_5_) | copy-start | bytes 983044
  54.3 7.9 %collective-permute-start.7 = (bf16[4,320,128]{2,1,0:T(8,128)(2,1)S(1)}, bf16[4,320,128]{2,1,0:T(8,128)(2,1)S(1)}, u32[]{:S(2)}, u32[]{:S(2)}) collective-permute-start(bf16[4,320,128]{2,1,0:T(8,128)(2,1)S(1)} %broadcast_select_fusion.5), channel_id=1, source_target_pairs={{2,0},{6,4},{10,8},{14,12},{0,2},{4,6},{8,10},{12,14},{3,1},{7,5},... | collective-permute-start | bytes 983048 | tf_op jit(solution)/shard_map/ppermute | solution.py:249
  55.7 9.6 %collective-permute-start.11 = (bf16[4,320,128]{2,1,0:T(8,128)(2,1)S(1)}, bf16[4,320,128]{2,1,0:T(8,128)(2,1)S(1)}, u32[]{:S(2)}, u32[]{:S(2)}) collective-permute-start(bf16[4,320,128]{2,1,0:T(8,128)(2,1)S(1)} %broadcast_select_fusion.1), channel_id=1, source_target_pairs={{4,0},{6,2},{8,4},{10,6},{12,8},{14,10},{5,1},{7,3},{9,5},{11,7},{... | collective-permute-start | bytes 983048 | tf_op jit(solution)/shard_map/ppermute | solution.py:246
  63.8 13.4 %collective-permute-start.8 = (bf16[4,320,128]{2,1,0:T(8,128)(2,1)}, bf16[4,320,128]{2,1,0:T(8,128)(2,1)}, u32[]{:S(2)}, u32[]{:S(2)}) collective-permute-start(bf16[4,320,128]{2,1,0:T(8,128)(2,1)} %broadcast_select_fusion.4), channel_id=1, source_target_pairs={{4,0},{6,2},{8,4},{10,6},{12,8},{14,10},{5,1},{7,3},{9,5},{11,7},{... | collective-permute-start | bytes 983048 | tf_op jit(solution)/shard_map/ppermute | solution.py:246
  66.8 12.4 %collective-permute-start.13 = (bf16[4,320,128]{2,1,0:T(8,128)(2,1)}, bf16[4,320,128]{2,1,0:T(8,128)(2,1)}, u32[]{:S(2)}, u32[]{:S(2)}) collective-permute-start(bf16[4,320,128]{2,1,0:T(8,128)(2,1)} %broadcast_select_fusion), channel_id=1, source_target_pairs={{2,0},{6,4},{10,8},{14,12},{0,2},{4,6},{8,10},{12,14},{3,1},{7,5},... | collective-permute-start | bytes 983048 | tf_op jit(solution)/shard_map/ppermute | solution.py:249
  77.2 16.9 %collective-permute-start.12 = (bf16[4,320,128]{2,1,0:T(8,128)(2,1)}, bf16[4,320,128]{2,1,0:T(8,128)(2,1)S(1)}, u32[]{:S(2)}, u32[]{:S(2)}) collective-permute-start(bf16[4,320,128]{2,1,0:T(8,128)(2,1)} %collective-permute-done.8.refs_5_.refs_4_), channel_id=1, source_target_pairs={{0,2},{4,6},{8,10},{12,14},{1,3},{5,7},{9,11},{13,15},{16,18},{20,... | collective-permute-start | bytes 983048 | tf_op jit(solution)/shard_map/ppermute | solution.py:273
  (7 other events, 37.6 us)

commit v3 on v1

--- a/solution.py
+++ b/solution.py
@@ -16,6 +16,7 @@
 HOPS = 3
 ROWS = 64
 CHUNKS = 4
+VMEM = 16 << 20
 
 
 def make_table(length, bins, first_bin):
@@ -80,44 +81,50 @@
             out_refs[bin_at // per_chunk][bin_at % per_chunk] = (values * root).astype(jnp.bfloat16)
 
 
-def band_kernel(
-    even_ref, own_ref, *refs, total_windows
-):
-    pieces = refs[: 2 * HOPS]
-    mask_ref, real_ref, imag_ref, right_ref, left_ref = (*refs[2 * HOPS : 2 * HOPS + 1], *refs[-4:])
-    block, depth = own_ref.shape[1:]
-    reach = HOPS * block
-    right_ref[:block] = own_ref[0]
+def band_kernel(even_ref, own_ref, *refs, hops, first_tile, total_windows):
+    at = pl.program_id(0)
+    far = [hop for hop in hops if hop]
+    pieces = refs[: 2 * len(far)]
+    mask_ref, real_ref, imag_ref = (refs[2 * len(far)], *refs[-4:-2])
+    right_ref, left_ref = refs[-2:]
+    _, block, depth = own_ref.shape
+    reach = min(HOPS * block - first_tile * LANES, real_ref.shape[2])
     is_even = even_ref[0] == 1
-
-    @pl.when(is_even)
-    def _():
-        for hop in range(HOPS):
-            right_ref[(hop + 1) * block : (hop + 2) * block] = pieces[2 * hop][0]
-
-    @pl.when(jnp.logical_not(is_even))
-    def _():
-        for hop in range(HOPS):
-            right_ref[(hop + 1) * block : (hop + 2) * block] = pieces[2 * hop + 1][0]
-
-    wide = own_ref[0].astype(jnp.float32) * (1.0 / math.sqrt(total_windows))
+    origin = hops[0] * block
+    if hops[0] == 0:
+        right_ref[:block] = own_ref[at]
+
+    def gather(parity):
+        for place, hop in enumerate(far):
+            start = hop * block - origin
+            right_ref[start : start + block] = pieces[2 * place + parity][at]
+
+    filled = len(hops) * block
+    if right_ref.shape[0] > filled:
+        right_ref[filled:] = jnp.zeros((right_ref.shape[0] - filled, depth), jnp.bfloat16)
+    pl.when(is_even)(lambda: gather(0))
+    pl.when(jnp.logical_not(is_even))(lambda: gather(1))
+
+    wide = own_ref[at].astype(jnp.float32) * (1.0 / math.sqrt(total_windows))
     part = depth // 4
     lane = lax.broadcasted_iota(jnp.int32, (block, depth), 1)
     turned = jnp.where(
         (lane // part) % 2 == 0, pltpu.roll(wide, depth - part, 1), -pltpu.roll(wide, part, 1)
     )
     for group in range(block // ROWS):
-        at = slice(group * ROWS, (group + 1) * ROWS)
-        left_ref[2 * group * ROWS : (2 * group + 1) * ROWS] = wide[at].astype(jnp.bfloat16)
-        left_ref[(2 * group + 1) * ROWS : (2 * group + 2) * ROWS] = turned[at].astype(jnp.bfloat16)
+        rows = slice(group * ROWS, (group + 1) * ROWS)
+        left_ref[2 * group * ROWS : (2 * group + 1) * ROWS] = wide[rows].astype(jnp.bfloat16)
+        left_ref[(2 * group + 1) * ROWS : (2 * group + 2) * ROWS] = turned[rows].astype(jnp.bfloat16)
     lane_of = lax.broadcasted_iota(jnp.int32, (ROWS, LANES), 1)
     row_of = lax.broadcasted_iota(jnp.int32, (ROWS, LANES), 0)
     out_tiles = -(-reach // LANES)
+    mask_from = 2 if first_tile == 0 else 0
     for group in range(block // ROWS):
         first = group * ROWS
-        base = (first + 1) // LANES
-        shift = first + 1 - base * LANES + row_of
-        tiles = (first + ROWS - 1 + reach) // LANES - base + 1
+        begin = first + 1 + first_tile * LANES - origin
+        base = begin // LANES
+        shift = begin - base * LANES + row_of
+        tiles = (begin + ROWS - 2 + reach) // LANES - base + 1
         products = lax.dot_general(
             left_ref[2 * first : 2 * first + 2 * ROWS],
             right_ref[base * LANES : (base + tiles) * LANES],
@@ -136,51 +143,54 @@
                     values = jnp.where(keep, values, rows[:, start + LANES : start + 2 * LANES])
                 moved = jnp.take_along_axis(values, source, axis=1, mode="promise_in_bounds")
                 moved = moved.astype(jnp.bfloat16)
-                if start + LANES > block:
-                    moved = moved * mask_ref[first : first + ROWS, start : start + LANES]
+                if tile >= mask_from:
+                    column = (tile - mask_from) * LANES
+                    moved = moved * mask_ref[first : first + ROWS, column : column + LANES]
                 out_ref[0, first : first + ROWS, start : start + width] = moved[:, :width]
 
 
-def band(even, own, pieces, mask, so_far, chunk, bins_here, total_windows):
+def band(even, own, pieces, mask, so_far, chunk, bins_here, total_windows, far):
     per_chunk, block, depth = own.shape
     out = jax.ShapeDtypeStruct((bins_here, block, HOPS * block), jnp.bfloat16)
+    near_width = 2 * block
+    hops = (2, 3) if far else (0, 1, 2)
     out_spec = pl.BlockSpec(
-        (1, block, HOPS * block), lambda i, even: (chunk * per_chunk + i, 0, 0)
-    )
-    one = (1, block, depth)
-    in_specs = [pl.BlockSpec(one, lambda i, even: (i, 0, 0))]
+        (1, block, near_width), lambda i: (chunk * per_chunk + i, 0, 1 if far else 0)
+    )
     operands = [even, own]
-    for for_even, for_odd in pieces:
-        in_specs.append(pl.BlockSpec(one, lambda i, even: (i * even[0], 0, 0)))
-        in_specs.append(pl.BlockSpec(one, lambda i, even: (i * (1 - even[0]), 0, 0)))
-        operands += [for_even, for_odd]
-    in_specs.append(pl.BlockSpec(mask.shape, lambda i, even: (0, 0)))
+    for piece in pieces:
+        operands += piece
     operands.append(mask)
+    in_specs = [pl.BlockSpec(memory_space=pltpu.SMEM)]
+    in_specs += [pl.BlockSpec(memory_space=pltpu.VMEM)] * (len(operands) - 1)
     aliases = {}
     if so_far is not None:
         aliases = {len(operands): 0, len(operands) + 1: 1}
         operands += list(so_far)
         in_specs += [pl.BlockSpec(memory_space=pl.ANY)] * 2
+    wide = block if far else near_width
     return pl.pallas_call(
-        functools.partial(band_kernel, total_windows=total_windows),
-        grid_spec=pltpu.PrefetchScalarGridSpec(
-            num_scalar_prefetch=1,
-            grid=(per_chunk,),
-            in_specs=in_specs,
-            out_specs=[out_spec, out_spec],
-            scratch_shapes=[
-                pltpu.VMEM(((HOPS + 1) * block, depth), jnp.bfloat16),
-                pltpu.VMEM((2 * block, depth), jnp.bfloat16),
-            ],
+        functools.partial(
+            band_kernel,
+            hops=hops,
+            first_tile=near_width // LANES if far else 0,
+            total_windows=total_windows,
         ),
+        grid=(per_chunk,),
+        in_specs=in_specs,
+        out_specs=[out_spec, out_spec],
+        scratch_shapes=[
+            pltpu.VMEM((-(-len(hops) * block // LANES) * LANES, depth), jnp.bfloat16),
+            pltpu.VMEM((2 * block, depth), jnp.bfloat16),
+        ],
         out_shape=[out, out],
         input_output_aliases=aliases,
         cost_estimate=pl.CostEstimate(
-            flops=per_chunk * 4 * block * (HOPS + 1) * block * depth,
-            bytes_accessed=per_chunk * 4 * block * HOPS * block * 2,
+            flops=per_chunk * 4 * block * wide * depth,
+            bytes_accessed=per_chunk * 4 * block * wide,
             transcendentals=0,
         ),
-        compiler_params=pltpu.CompilerParams(vmem_limit_bytes=24 << 20),
+        compiler_params=pltpu.CompilerParams(vmem_limit_bytes=VMEM),
     )(*operands)
 
 
@@ -209,7 +219,7 @@
         scratch_shapes=[
             pltpu.VMEM((-(-block // LANES), windows_here * 2 * FREQS, LANES), jnp.float32)
         ],
-        compiler_params=pltpu.CompilerParams(vmem_limit_bytes=32 << 20),
+        compiler_params=pltpu.CompilerParams(vmem_limit_bytes=VMEM),
     )(
         jnp.stack([here, counts[0]]),
         samples,
@@ -230,18 +240,30 @@
     to_odd = [(i - 1, i) for i in range(1, fiber_size, 2)]
 
     def pick(for_even, for_odd):
-        return jnp.where(is_even, for_even, for_odd)
+        even_one, for_even, for_odd = lax.optimization_barrier((is_even, for_even, for_odd))
+        return lax.optimization_barrier(jnp.where(even_one, for_even, for_odd))
 
     def move_down(for_even, for_odd):
         return lax.ppermute(pick(for_even, for_odd), "fiber", down)
 
     def cross(for_even, for_odd):
         return lax.ppermute(pick(for_even, for_odd), "fiber", to_even + to_odd)
+
+    near = 2 * block
+    offsets = jnp.arange(1, near + HOPS * LANES + 1, dtype=jnp.int32)
+    mask = (offsets[None, :] <= reach_limit[:, None]).astype(jnp.bfloat16)
+    masks = (mask[:, 2 * LANES : near], mask[:, near:])
+
+    def work(outs, chunk, far, *pieces):
+        return band(
+            even, own[chunk], pieces, masks[far], outs, chunk, bins_here, total_windows, far
+        )
 
     z, y = {}, {}
     z[0] = move_down(own[0], own[2])
     y[0] = lax.ppermute(own[0], "fiber", to_even)
     z[1] = move_down(own[1], own[3])
+    z[0], y[0], *masks = lax.optimization_barrier((z[0], y[0], *masks))
     y[1] = cross(z[0], own[1])
     z[2] = move_down(own[2], y[1])
     y[2] = cross(z[1], own[2])
@@ -249,21 +271,19 @@
     y[3] = cross(z[2], own[3])
     z[4] = move_down(y[0], y[3])
     y[4] = cross(z[3], z[0])
+    outs = work(None, 2, 0, (y[2], y[3]), (z[2], z[0]))
+    z[4], *outs = lax.optimization_barrier((z[4], *outs))
     z[5] = move_down(y[1], y[4])
     y[5] = cross(z[4], z[1])
+    outs = work(outs, 3, 0, (y[3], y[4]), (z[3], z[1]))
+    outs = work(outs, 2, 1, (z[2], z[0]), (y[4], z[4]))
+    z[5], *outs = lax.optimization_barrier((z[5], *outs))
     y[6] = lax.ppermute(z[5], "fiber", to_odd)
-    blocks = {
-        0: ((y[0], y[1]), (z[0], y[5]), (z[4], z[2])),
-        1: ((y[1], y[2]), (z[1], y[6]), (z[5], z[3])),
-        2: ((y[2], y[3]), (z[2], z[0]), (y[4], z[4])),
-        3: ((y[3], y[4]), (z[3], z[1]), (y[5], z[5])),
-    }
-
-    offsets = jnp.arange(1, -(-HOPS * block // LANES) * LANES + 1, dtype=jnp.int32)
-    mask = (offsets[None, :] <= reach_limit[:, None]).astype(jnp.bfloat16)
-    outs = None
-    for chunk in (2, 0, 3, 1):
-        outs = band(even, own[chunk], blocks[chunk], mask, outs, chunk, bins_here, total_windows)
+    outs = work(outs, 3, 1, (z[3], z[1]), (y[5], z[5]))
+    outs = work(outs, 0, 0, (y[0], y[1]), (z[0], y[5]))
+    outs = work(outs, 0, 1, (z[0], y[5]), (z[4], z[2]))
+    outs = work(outs, 1, 0, (y[1], y[2]), (z[1], y[6]))
+    outs = work(outs, 1, 1, (z[1], y[6]), (z[5], z[3]))
     return tuple(outs)
 
 

time: 133 us -> 103 us (0.77)
  waiting for transfers between devices: 74.5 us -> 33.6 us
  Pallas kernels: 30.5 us -> 38.9 us
  starting transfers between devices: 14.9 us -> 20.6 us
  local copies, waits for them, and re-layouts: 9.29 us -> 4.22 us
  other arithmetic: 1.42 us -> 3.75 us
    ppermute x6, waiting for transfers between devices: 43.2 us -> 23.1 us  [move_down(): return lax.ppermute(pick(for_even, for_odd), 'fiber', down)]
    ppermute x5, waiting for transfers between devices: 29.6 us -> 9.67 us  [cross(): return lax.ppermute(pick(for_even, for_odd), 'fiber', to_even + to_odd)]
    pallas_call x4 -> x8, Pallas kernels: 25.4 us -> 33.9 us  [band(): pl.pallas_call(functools.partial(band_kernel, hops=hops, first_tile=near_...]
    unnamed x38 -> x16, local copies, waits for them, and re-layouts: 9.29 us -> 4.16 us
    ppermute x5, starting transfers between devices: 2.97 us -> 7.66 us  [cross(): return lax.ppermute(pick(for_even, for_odd), 'fiber', to_even + to_odd)]
    select_n x9 -> x11, other arithmetic: 1.17 us -> 2.82 us  [pick(): return lax.optimization_barrier(jnp.where(even_one, for_even, for_odd))]
  transfers between devices with their start and end apart: 14 -> 14, of which waited for: 11 -> 9; matrix products, arithmetic and copies ran while one was open for 0% -> 4% of each run, Pallas kernels for 14% -> 26%
where the time goes in v3:
time: 103 us
  Pallas kernels  38.9 us (38%)
  waiting for transfers between devices  33.6 us (33%)
  starting transfers between devices  20.6 us (20%)
  local copies, waits for them, and re-layouts  4.22 us (4%)
  other arithmetic  3.75 us (4%)
  between operations  1.46 us (1%)
    pallas_call x8, Pallas kernels, band(): pl.pallas_call(functools.partial(band_kernel, hops=hops, first_tile=near_...  33.9 us
    ppermute x6, waiting for transfers between devices, move_down(): return lax.ppermute(pick(for_even, for_odd), 'fiber', down)  23.1 us
    ppermute x5, waiting for transfers between devices, cross(): return lax.ppermute(pick(for_even, for_odd), 'fiber', to_even + to_odd)  9.67 us
    ppermute x6, starting transfers between devices, move_down(): return lax.ppermute(pick(for_even, for_odd), 'fiber', down)  7.74 us
    ppermute x5, starting transfers between devices, cross(): return lax.ppermute(pick(for_even, for_odd), 'fiber', to_even + to_odd)  7.66 us
    unnamed x16, local copies, waits for them, and re-layouts  4.16 us
    pallas_call x1, Pallas kernels, body(): pl.pallas_call(spectra_kernel, in_specs=[pl.BlockSpec(memory_space=pltpu....  3.62 us
    ppermute x1, starting transfers between devices, body(): y[6] = lax.ppermute(z[5], 'fiber', to_odd)  3.38 us
  transfers between devices with their start and end apart: 14, of which 9 were waited for; matrix products, arithmetic and copies ran while one was open for 4% of the time, Pallas kernels for 26%

profile of v3, /device:TPU:0, one launch (start us, length us, event | category | flops | bytes accessed | tf_op | source)
XLA Modules:
  0.0 102.5 jit_solution(1226755335719118767)
XLA Ops:
  1.4 1.7 %copy-done.4 = bf16[32,320,128]{2,1,0:T(8,128)(2,1)S(1)} copy-done((bf16[32,320,128]{2,1,0:T(8,128)(2,1)S(1)}, bf16[32,320,128]{2,1,0:T(8,128)(2,1)}, u32[]{:S(2)}) %copy-start.4) | copy-done | bytes 2621464
  3.8 3.6 %shard_map.59 = (bf16[8,320,128]{2,1,0:T(8,128)(2,1)S(1)}, bf16[8,320,128]{2,1,0:T(8,128)(2,1)S(1)}) custom-call(s32[2]{0:T(128)S(1)} %pad_add_fusion.place_ref, bf16[32,320,128]{2,1,0:T(8,128)(2,1)S(1)} %copy-done.4, bf16[64,128]{1,0:T(8,128)(2,1)S(1)} %copy-done.7), custom_call_target="tpu_custom_call" | custom-call | tf_op jit(solution)/shard_map/pallas_call | solution.py:210
  9.7 1.4 %shard_map.60 = (bf16[4,320,128]{2,1,0:T(8,128)(2,1)S(1)}, bf16[4,320,128]{2,1,0:T(8,128)(2,1)S(1)}, bf16[4,320,128]{2,1,0:T(8,128)(2,1)S(1)}, bf16[4,320,128]{2,1,0:T(8,128)(2,1)S(1)}) custom-call(bf16[8,320,128]{2,1,0:T(8,128)(2,1)S(1)} %get-tuple-element.65.mine_ref, bf16[8,320,128]{2,1,0:T(8,128)(2,1)S(1)} %collective-permute-done.theirs_ref), custom_call_target="tpu_custom_call" | custom-call | tf_op jit(solution)/shard_map/pallas_call | solution.py:230
  11.1 1.3 %collective-permute-start.3 = (bf16[4,320,128]{2,1,0:T(8,128)(2,1)S(1)}, bf16[4,320,128]{2,1,0:T(8,128)(2,1)S(1)}, u32[]{:S(2)}, u32[]{:S(2)}) collective-permute-start(bf16[4,320,128]{2,1,0:T(8,128)(2,1)S(1)} %get-tuple-element.75.own_ref), channel_id=1, source_target_pairs={{2,0},{6,4},{10,8},{14,12},{3,1},{7,5},{11,9},{15,13},{18,16},{22,... | collective-permute-start | bytes 983048 | tf_op jit(solution)/shard_map/ppermute | solution.py:264
  12.4 1.3 %collective-permute-start.2 = (bf16[4,320,128]{2,1,0:T(8,128)(2,1)S(1)}, bf16[4,320,128]{2,1,0:T(8,128)(2,1)S(1)}, u32[]{:S(2)}, u32[]{:S(2)}) collective-permute-start(bf16[4,320,128]{2,1,0:T(8,128)(2,1)S(1)} %broadcast_select_fusion.9), channel_id=1, source_target_pairs={{4,0},{6,2},{8,4},{10,6},{12,8},{14,10},{5,1},{7,3},{9,5},{11,7},{... | collective-permute-start | bytes 983048 | tf_op jit(solution)/shard_map/ppermute | solution.py:247
  13.8 1.3 %collective-permute-start.1 = (bf16[4,320,128]{2,1,0:T(8,128)(2,1)S(1)}, bf16[4,320,128]{2,1,0:T(8,128)(2,1)S(1)}, u32[]{:S(2)}, u32[]{:S(2)}) collective-permute-start(bf16[4,320,128]{2,1,0:T(8,128)(2,1)S(1)} %broadcast_select_fusion.10), channel_id=1, source_target_pairs={{4,0},{6,2},{8,4},{10,6},{12,8},{14,10},{5,1},{7,3},{9,5},{11,7},{... | collective-permute-start | bytes 983048 | tf_op jit(solution)/shard_map/ppermute | solution.py:247
  15.1 10.6 %collective-permute-done.2.refs_3_.refs_1_.refs_2_.refs_0_ = bf16[4,320,128]{2,1,0:T(8,128)(2,1)S(1)} collective-permute-done((bf16[4,320,128]{2,1,0:T(8,128)(2,1)S(1)}, bf16[4,320,128]{2,1,0:T(8,128)(2,1)S(1)}, u32[]{:S(2)}, u32[]{:S(2)}) %collective-permute-start.2) | collective-permute-done | bytes 327712 | tf_op jit(solution)/shard_map/ppermute | solution.py:247
  25.8 2.8 %collective-permute-start.4 = (bf16[4,320,128]{2,1,0:T(8,128)(2,1)S(1)}, bf16[4,320,128]{2,1,0:T(8,128)(2,1)S(1)}, u32[]{:S(2)}, u32[]{:S(2)}) collective-permute-start(bf16[4,320,128]{2,1,0:T(8,128)(2,1)S(1)} %broadcast_select_fusion.8), channel_id=1, source_target_pairs={{2,0},{6,4},{10,8},{14,12},{0,2},{4,6},{8,10},{12,14},{3,1},{7,5},... | collective-permute-start | bytes 983048 | tf_op jit(solution)/shard_map/ppermute | solution.py:250
  28.6 3.7 %collective-permute-done.1.refs_3_.refs_1_.refs_2_.refs_0_ = bf16[4,320,128]{2,1,0:T(8,128)(2,1)S(1)} collective-permute-done((bf16[4,320,128]{2,1,0:T(8,128)(2,1)S(1)}, bf16[4,320,128]{2,1,0:T(8,128)(2,1)S(1)}, u32[]{:S(2)}, u32[]{:S(2)}) %collective-permute-start.1) | collective-permute-done | bytes 327712 | tf_op jit(solution)/shard_map/ppermute | solution.py:247
  32.3 2.4 %collective-permute-start.5 = (bf16[4,320,128]{2,1,0:T(8,128)(2,1)S(1)}, bf16[4,320,128]{2,1,0:T(8,128)(2,1)S(1)}, u32[]{:S(2)}, u32[]{:S(2)}) collective-permute-start(bf16[4,320,128]{2,1,0:T(8,128)(2,1)S(1)} %broadcast_select_fusion.7), channel_id=1, source_target_pairs={{2,0},{6,4},{10,8},{14,12},{0,2},{4,6},{8,10},{12,14},{3,1},{7,5},... | collective-permute-start | bytes 983048 | tf_op jit(solution)/shard_map/ppermute | solution.py:250
  35.0 1.3 %collective-permute-start.9 = (bf16[4,320,128]{2,1,0:T(8,128)(2,1)S(1)}, bf16[4,320,128]{2,1,0:T(8,128)(2,1)S(1)}, u32[]{:S(2)}, u32[]{:S(2)}) collective-permute-start(bf16[4,320,128]{2,1,0:T(8,128)(2,1)S(1)} %broadcast_select_fusion.3), channel_id=1, source_target_pairs={{4,0},{6,2},{8,4},{10,6},{12,8},{14,10},{5,1},{7,3},{9,5},{11,7},{... | collective-permute-start | bytes 983048 | tf_op jit(solution)/shard_map/ppermute | solution.py:247
  36.3 5.7 %collective-permute-done.5.refs_0_.refs_1_ = bf16[4,320,128]{2,1,0:T(8,128)(2,1)S(1)} collective-permute-done((bf16[4,320,128]{2,1,0:T(8,128)(2,1)S(1)}, bf16[4,320,128]{2,1,0:T(8,128)(2,1)S(1)}, u32[]{:S(2)}, u32[]{:S(2)}) %collective-permute-start.5) | collective-permute-done | bytes 327712 | tf_op jit(solution)/shard_map/ppermute | solution.py:250
  43.3 2.2 %collective-permute-done.9.refs_2_.refs_0_.refs_3_ = bf16[4,320,128]{2,1,0:T(8,128)(2,1)S(1)} collective-permute-done((bf16[4,320,128]{2,1,0:T(8,128)(2,1)S(1)}, bf16[4,320,128]{2,1,0:T(8,128)(2,1)S(1)}, u32[]{:S(2)}, u32[]{:S(2)}) %collective-permute-start.9) | collective-permute-done | bytes 327712 | tf_op jit(solution)/shard_map/ppermute | solution.py:247
  45.9 6.5 %collective-permute-done.6.refs_2_.refs_0_.refs_3_ = bf16[4,320,128]{2,1,0:T(8,128)(2,1)S(1)} collective-permute-done((bf16[4,320,128]{2,1,0:T(8,128)(2,1)S(1)}, bf16[4,320,128]{2,1,0:T(8,128)(2,1)S(1)}, u32[]{:S(2)}, u32[]{:S(2)}) %collective-permute-start.6) | collective-permute-done | bytes 327712 | tf_op jit(solution)/shard_map/ppermute | solution.py:247
  57.2 3.8 %collective-permute-done.7.refs_1_.refs_2_ = bf16[4,320,128]{2,1,0:T(8,128)(2,1)} collective-permute-done((bf16[4,320,128]{2,1,0:T(8,128)(2,1)}, bf16[4,320,128]{2,1,0:T(8,128)(2,1)}, u32[]{:S(2)}, u32[]{:S(2)}) %collective-permute-start.7) | collective-permute-done | bytes 327712 | tf_op jit(solution)/shard_map/ppermute | solution.py:250
  63.3 4.3 %shard_map.61 = (bf16[16,320,960]{2,1,0:T(8,128)(2,1)}, bf16[16,320,960]{2,1,0:T(8,128)(2,1)}) custom-call(s32[1]{0:T(128)} %bitcast.even_ref, bf16[4,320,128]{2,1,0:T(8,128)(2,1)S(1)} %get-tuple-element.94.own_ref, bf16[4,320,128]{2,1,0:T(8,128)(2,1)S(1)} %collective-permute-done.5.refs_0_.refs_1_, bf16[4,320,128]{2,1,0:T(8,128)(2,1)S(1)} %copy-done.1, ...), custom_call_target="tpu_custom_call" | custom-call | flops 419430400 | bytes 3276800 | tf_op jit(solution)/shard_map/pallas_call | solution.py:172
  69.5 5.2 %shard_map.62 = (bf16[16,320,960]{2,1,0:T(8,128)(2,1)}, bf16[16,320,960]{2,1,0:T(8,128)(2,1)}) custom-call(s32[1]{0:T(128)} %bitcast.even_ref, bf16[4,320,128]{2,1,0:T(8,128)(2,1)S(1)} %get-tuple-element.99.own_ref, bf16[4,320,128]{2,1,0:T(8,128)(2,1)S(1)} %copy-done.1, ...), custom_call_target="tpu_custom_call", output_to_operand_aliasing={{0}: (7, {}), {1}: (8, {})} | custom-call | flops 419430400 | bytes 3276800 | tf_op jit(solution)/shard_map/pallas_call | solution.py:172
  74.7 4.5 %shard_map.63 = (bf16[16,320,960]{2,1,0:T(8,128)(2,1)}, bf16[16,320,960]{2,1,0:T(8,128)(2,1)}) custom-call(s32[1]{0:T(128)} %bitcast.even_ref, bf16[4,320,128]{2,1,0:T(8,128)(2,1)S(1)} %get-tuple-element.94.own_ref, bf16[4,320,128]{2,1,0:T(8,128)(2,1)S(1)} %collective-permute-done.9.refs_2_.refs_0_.refs_3_, ...), custom_call_target="tpu_custom_call", output_to_operand_aliasing={{0}: (7, {}), {1}: (8, {})} | custom-call | flops 209715200 | bytes 1638400 | tf_op jit(solution)/shard_map/pallas_call | solution.py:172
  79.2 3.4 %collective-permute-start.12 = (bf16[4,320,128]{2,1,0:T(8,128)(2,1)S(1)}, bf16[4,320,128]{2,1,0:T(8,128)(2,1)S(1)}, u32[]{:S(2)}, u32[]{:S(2)}) collective-permute-start(bf16[4,320,128]{2,1,0:T(8,128)(2,1)S(1)} %collective-permute-done.8.refs_3_.refs_2_), channel_id=1, source_target_pairs={{0,2},{4,6},{8,10},{12,14},{1,3},{5,7},{9,11},{13,15},{16,18},{20,... | collective-permute-start | bytes 983048 | tf_op jit(solution)/shard_map/ppermute | solution.py:281
  82.6 3.5 %shard_map.64 = (bf16[16,320,960]{2,1,0:T(8,128)(2,1)}, bf16[16,320,960]{2,1,0:T(8,128)(2,1)}) custom-call(s32[1]{0:T(128)} %bitcast.even_ref, bf16[4,320,128]{2,1,0:T(8,128)(2,1)S(1)} %get-tuple-element.99.own_ref, bf16[4,320,128]{2,1,0:T(8,128)(2,1)S(1)} %collective-permute-done.6.refs_2_.refs_0_.refs_3_, ...), custom_call_target="tpu_custom_call", output_to_operand_aliasing={{0}: (7, {}), {1}: (8, {})} | custom-call | flops 209715200 | bytes 1638400 | tf_op jit(solution)/shard_map/pallas_call | solution.py:172
  86.1 4.3 %shard_map.65 = (bf16[16,320,960]{2,1,0:T(8,128)(2,1)}, bf16[16,320,960]{2,1,0:T(8,128)(2,1)}) custom-call(s32[1]{0:T(128)} %bitcast.even_ref, bf16[4,320,128]{2,1,0:T(8,128)(2,1)S(1)} %copy-done.3, bf16[4,320,128]{2,1,0:T(8,128)(2,1)S(1)} %copy-done.6, ...), custom_call_target="tpu_custom_call", output_to_operand_aliasing={{0}: (7, {}), {1}: (8, {})} | custom-call | flops 419430400 | bytes 3276800 | tf_op jit(solution)/shard_map/pallas_call | solution.py:172
  90.4 4.4 %shard_map.66 = (bf16[16,320,960]{2,1,0:T(8,128)(2,1)}, bf16[16,320,960]{2,1,0:T(8,128)(2,1)}) custom-call(s32[1]{0:T(128)} %bitcast.even_ref, bf16[4,320,128]{2,1,0:T(8,128)(2,1)S(1)} %copy-done.3, bf16[4,320,128]{2,1,0:T(8,128)(2,1)S(1)} %collective-permute-done.2.refs_3_.refs_1_.refs_2_.refs_0_, ...), custom_call_target="tpu_custom_call", output_to_operand_aliasing={{0}: (7, {}), {1}: (8, {})} | custom-call | flops 209715200 | bytes 1638400 | tf_op jit(solution)/shard_map/pallas_call | solution.py:172
  94.8 4.3 %shard_map.67 = (bf16[16,320,960]{2,1,0:T(8,128)(2,1)}, bf16[16,320,960]{2,1,0:T(8,128)(2,1)}) custom-call(s32[1]{0:T(128)} %bitcast.even_ref, bf16[4,320,128]{2,1,0:T(8,128)(2,1)S(1)} %get-tuple-element.80.own_ref, bf16[4,320,128]{2,1,0:T(8,128)(2,1)S(1)} %collective-permute-done.4.refs_1_.refs_0_, ...), custom_call_target="tpu_custom_call", output_to_operand_aliasing={{0}: (7, {}), {1}: (8, {})} | custom-call | flops 419430400 | bytes 3276800 | tf_op jit(solution)/shard_map/pallas_call | solution.py:172
  99.1 3.4 %shard_map.68 = (bf16[16,320,960]{2,1,0:T(8,128)(2,1)}, bf16[16,320,960]{2,1,0:T(8,128)(2,1)}) custom-call(s32[1]{0:T(128)} %bitcast.even_ref, bf16[4,320,128]{2,1,0:T(8,128)(2,1)S(1)} %get-tuple-element.80.own_ref, bf16[4,320,128]{2,1,0:T(8,128)(2,1)S(1)} %collective-permute-done.1.refs_3_.refs_1_.refs_2_.refs_0_, ...), custom_call_target="tpu_custom_call", output_to_operand_aliasing={{0}: (7, {}), {1}: (8, {})} | custom-call | flops 209715200 | bytes 1638400 | tf_op jit(solution)/shard_map/pallas_call | solution.py:172
  (45 shorter events, 14.2 us)
Async XLA Ops:
  1.4 1.7 %copy-start.4 = (bf16[32,320,128]{2,1,0:T(8,128)(2,1)S(1)}, bf16[32,320,128]{2,1,0:T(8,128)(2,1)}, u32[]{:S(2)}) copy-start(bf16[32,320,128]{2,1,0:T(8,128)(2,1)} %samples_ref.1) | copy-start | bytes 7864324
  3.1 0.7 copy-start.7
  7.4 2.2 %collective-permute-start = (bf16[8,320,128]{2,1,0:T(8,128)(2,1)S(1)}, bf16[8,320,128]{2,1,0:T(8,128)(2,1)S(1)}, u32[]{:S(2)}, u32[]{:S(2)}) collective-permute-start(bf16[8,320,128]{2,1,0:T(8,128)(2,1)S(1)} %get-tuple-element.66), channel_id=1, source_target_pairs={{0,1},{1,0},{2,3},{3,2},{4,5},{5,4},{6,7},{7,6},{8,9},{9,8},{10,11... | collective-permute-start | bytes 1966088 | tf_op jit(solution)/shard_map/ppermute | solution.py:228
  11.1 44.1 %copy-start.2 = (bf16[4,320,128]{2,1,0:T(8,128)(2,1)}, bf16[4,320,128]{2,1,0:T(8,128)(2,1)S(1)}, u32[]{:S(2)}) copy-start(bf16[4,320,128]{2,1,0:T(8,128)(2,1)S(1)} %get-tuple-element.75.own_ref) | copy-start | bytes 983044
  11.1 14.7 %collective-permute-start.3 = (bf16[4,320,128]{2,1,0:T(8,128)(2,1)S(1)}, bf16[4,320,128]{2,1,0:T(8,128)(2,1)S(1)}, u32[]{:S(2)}, u32[]{:S(2)}) collective-permute-start(bf16[4,320,128]{2,1,0:T(8,128)(2,1)S(1)} %get-tuple-element.75.own_ref), channel_id=1, source_target_pairs={{2,0},{6,4},{10,8},{14,12},{3,1},{7,5},{11,9},{15,13},{18,16},{22,... | collective-permute-start | bytes 983048 | tf_op jit(solution)/shard_map/ppermute | solution.py:264
  12.4 13.3 %collective-permute-start.2 = (bf16[4,320,128]{2,1,0:T(8,128)(2,1)S(1)}, bf16[4,320,128]{2,1,0:T(8,128)(2,1)S(1)}, u32[]{:S(2)}, u32[]{:S(2)}) collective-permute-start(bf16[4,320,128]{2,1,0:T(8,128)(2,1)S(1)} %broadcast_select_fusion.9), channel_id=1, source_target_pairs={{4,0},{6,2},{8,4},{10,6},{12,8},{14,10},{5,1},{7,3},{9,5},{11,7},{... | collective-permute-start | bytes 983048 | tf_op jit(solution)/shard_map/ppermute | solution.py:247
  13.8 18.5 %collective-permute-start.1 = (bf16[4,320,128]{2,1,0:T(8,128)(2,1)S(1)}, bf16[4,320,128]{2,1,0:T(8,128)(2,1)S(1)}, u32[]{:S(2)}, u32[]{:S(2)}) collective-permute-start(bf16[4,320,128]{2,1,0:T(8,128)(2,1)S(1)} %broadcast_select_fusion.10), channel_id=1, source_target_pairs={{4,0},{6,2},{8,4},{10,6},{12,8},{14,10},{5,1},{7,3},{9,5},{11,7},{... | collective-permute-start | bytes 983048 | tf_op jit(solution)/shard_map/ppermute | solution.py:247
  25.8 29.4 %copy-start.5 = (bf16[4,320,128]{2,1,0:T(8,128)(2,1)}, bf16[4,320,128]{2,1,0:T(8,128)(2,1)S(1)}, u32[]{:S(2)}) copy-start(bf16[4,320,128]{2,1,0:T(8,128)(2,1)S(1)} %collective-permute-done.3.refs_0_) | copy-start | bytes 983044
  25.8 9.1 %collective-permute-start.4 = (bf16[4,320,128]{2,1,0:T(8,128)(2,1)S(1)}, bf16[4,320,128]{2,1,0:T(8,128)(2,1)S(1)}, u32[]{:S(2)}, u32[]{:S(2)}) collective-permute-start(bf16[4,320,128]{2,1,0:T(8,128)(2,1)S(1)} %broadcast_select_fusion.8), channel_id=1, source_target_pairs={{2,0},{6,4},{10,8},{14,12},{0,2},{4,6},{8,10},{12,14},{3,1},{7,5},... | collective-permute-start | bytes 983048 | tf_op jit(solution)/shard_map/ppermute | solution.py:250
  32.3 9.6 %collective-permute-start.5 = (bf16[4,320,128]{2,1,0:T(8,128)(2,1)S(1)}, bf16[4,320,128]{2,1,0:T(8,128)(2,1)S(1)}, u32[]{:S(2)}, u32[]{:S(2)}) collective-permute-start(bf16[4,320,128]{2,1,0:T(8,128)(2,1)S(1)} %broadcast_select_fusion.7), channel_id=1, source_target_pairs={{2,0},{6,4},{10,8},{14,12},{0,2},{4,6},{8,10},{12,14},{3,1},{7,5},... | collective-permute-start | bytes 983048 | tf_op jit(solution)/shard_map/ppermute | solution.py:250
  35.0 10.5 %collective-permute-start.9 = (bf16[4,320,128]{2,1,0:T(8,128)(2,1)S(1)}, bf16[4,320,128]{2,1,0:T(8,128)(2,1)S(1)}, u32[]{:S(2)}, u32[]{:S(2)}) collective-permute-start(bf16[4,320,128]{2,1,0:T(8,128)(2,1)S(1)} %broadcast_select_fusion.3), channel_id=1, source_target_pairs={{4,0},{6,2},{8,4},{10,6},{12,8},{14,10},{5,1},{7,3},{9,5},{11,7},{... | collective-permute-start | bytes 983048 | tf_op jit(solution)/shard_map/ppermute | solution.py:247
  42.0 10.4 %collective-permute-start.6 = (bf16[4,320,128]{2,1,0:T(8,128)(2,1)S(1)}, bf16[4,320,128]{2,1,0:T(8,128)(2,1)S(1)}, u32[]{:S(2)}, u32[]{:S(2)}) collective-permute-start(bf16[4,320,128]{2,1,0:T(8,128)(2,1)S(1)} %broadcast_select_fusion.6), channel_id=1, source_target_pairs={{4,0},{6,2},{8,4},{10,6},{12,8},{14,10},{5,1},{7,3},{9,5},{11,7},{... | collective-permute-start | bytes 983048 | tf_op jit(solution)/shard_map/ppermute | solution.py:247
  45.5 8.9 %collective-permute-start.10 = (bf16[4,320,128]{2,1,0:T(8,128)(2,1)S(1)}, bf16[4,320,128]{2,1,0:T(8,128)(2,1)S(1)}, u32[]{:S(2)}, u32[]{:S(2)}) collective-permute-start(bf16[4,320,128]{2,1,0:T(8,128)(2,1)S(1)} %broadcast_select_fusion.2), channel_id=1, source_target_pairs={{2,0},{6,4},{10,8},{14,12},{0,2},{4,6},{8,10},{12,14},{3,1},{7,5},... | collective-permute-start | bytes 983048 | tf_op jit(solution)/shard_map/ppermute | solution.py:250
  53.2 7.9 %collective-permute-start.7 = (bf16[4,320,128]{2,1,0:T(8,128)(2,1)}, bf16[4,320,128]{2,1,0:T(8,128)(2,1)}, u32[]{:S(2)}, u32[]{:S(2)}) collective-permute-start(bf16[4,320,128]{2,1,0:T(8,128)(2,1)} %broadcast_select_fusion.5), channel_id=1, source_target_pairs={{2,0},{6,4},{10,8},{14,12},{0,2},{4,6},{8,10},{12,14},{3,1},{7,5},... | collective-permute-start | bytes 983048 | tf_op jit(solution)/shard_map/ppermute | solution.py:250
  55.2 0.7 copy-start
  55.9 11.8 %collective-permute-start.11 = (bf16[4,320,128]{2,1,0:T(8,128)(2,1)}, bf16[4,320,128]{2,1,0:T(8,128)(2,1)}, u32[]{:S(2)}, u32[]{:S(2)}) collective-permute-start(bf16[4,320,128]{2,1,0:T(8,128)(2,1)} %broadcast_select_fusion.1), channel_id=1, source_target_pairs={{4,0},{6,2},{8,4},{10,6},{12,8},{14,10},{5,1},{7,3},{9,5},{11,7},{... | collective-permute-start | bytes 983048 | tf_op jit(solution)/shard_map/ppermute | solution.py:247
  61.1 18.2 %collective-permute-start.8 = (bf16[4,320,128]{2,1,0:T(8,128)(2,1)S(1)}, bf16[4,320,128]{2,1,0:T(8,128)(2,1)S(1)}, u32[]{:S(2)}, u32[]{:S(2)}) collective-permute-start(bf16[4,320,128]{2,1,0:T(8,128)(2,1)S(1)} %broadcast_select_fusion.4), channel_id=1, source_target_pairs={{4,0},{6,2},{8,4},{10,6},{12,8},{14,10},{5,1},{7,3},{9,5},{11,7},{... | collective-permute-start | bytes 983048 | tf_op jit(solution)/shard_map/ppermute | solution.py:247
  62.4 1.0 copy-start.1
  68.7 13.9 %collective-permute-start.13 = (bf16[4,320,128]{2,1,0:T(8,128)(2,1)S(1)}, bf16[4,320,128]{2,1,0:T(8,128)(2,1)S(1)}, u32[]{:S(2)}, u32[]{:S(2)}) collective-permute-start(bf16[4,320,128]{2,1,0:T(8,128)(2,1)S(1)} %broadcast_select_fusion), channel_id=1, source_target_pairs={{2,0},{6,4},{10,8},{14,12},{0,2},{4,6},{8,10},{12,14},{3,1},{7,5},... | collective-permute-start | bytes 983048 | tf_op jit(solution)/shard_map/ppermute | solution.py:250
  79.2 6.9 %copy-start.3 = (bf16[4,320,128]{2,1,0:T(8,128)(2,1)S(1)}, bf16[4,320,128]{2,1,0:T(8,128)(2,1)}, u32[]{:S(2)}) copy-start(bf16[4,320,128]{2,1,0:T(8,128)(2,1)} %copy-done.2) | copy-start | bytes 983044
  79.2 6.9 %copy-start.6 = (bf16[4,320,128]{2,1,0:T(8,128)(2,1)S(1)}, bf16[4,320,128]{2,1,0:T(8,128)(2,1)}, u32[]{:S(2)}) copy-start(bf16[4,320,128]{2,1,0:T(8,128)(2,1)} %copy-done.5) | copy-start | bytes 983044
  79.2 15.6 %collective-permute-start.12 = (bf16[4,320,128]{2,1,0:T(8,128)(2,1)S(1)}, bf16[4,320,128]{2,1,0:T(8,128)(2,1)S(1)}, u32[]{:S(2)}, u32[]{:S(2)}) collective-permute-start(bf16[4,320,128]{2,1,0:T(8,128)(2,1)S(1)} %collective-permute-done.8.refs_3_.refs_2_), channel_id=1, source_target_pairs={{0,2},{4,6},{8,10},{12,14},{1,3},{5,7},{9,11},{13,15},{16,18},{20,... | collective-permute-start | bytes 983048 | tf_op jit(solution)/shard_map/ppermute | solution.py:281

commit v4 on v3

v4 whole, which is shorter than its diff:
```python
import functools
import math

import jax
import jax.numpy as jnp
import ml_dtypes
import numpy as np
from jax import lax
from jax.experimental import pallas as pl
from jax.experimental.pallas import tpu as pltpu
from jax.sharding import PartitionSpec as P

FREQS = 32
FIRST_BIN = 8
LANES = 128
HOPS = 3
ROWS = 64
CHUNKS = 4
VMEM = 16 << 20


def make_table(length, bins, first_bin):
    steps_index = np.arange(length, dtype=np.int32)
    bin_index = np.arange(bins, dtype=np.int32) + first_bin
    products = bin_index[:, None] * steps_index[None, :] % length
    phases = (2.0 * math.pi * products / length).astype(np.float32)
    taper = 0.5 - 0.5 * np.cos((2.0 * math.pi * steps_index / length).astype(np.float32))
    taper = taper.astype(np.float32)
    cosines = taper[None, :] * np.cos(phases)
    sines = -taper[None, :] * np.sin(phases)
    return np.concatenate([cosines, sines], axis=0).astype(ml_dtypes.bfloat16)


def spectra_kernel(place_ref, samples_ref, table_ref, mine_ref, other_ref, raw_ref):
    windows, block, _ = samples_ref.shape
    pairs = mine_ref.shape[0]
    here = place_ref[0]
    tiles = raw_ref.shape[0]
    channel = lax.broadcasted_iota(jnp.int32, (1, block), 1)
    active = (channel < place_ref[1]).astype(jnp.float32)
    for w in range(windows):
        raw = lax.dot_general(
            table_ref[...], samples_ref[w], (((1,), (1,)), ((), ())),
            preferred_element_type=jnp.float32,
        )
        level = jnp.sum(raw * raw, axis=0, keepdims=True) * (1.0 / FREQS)
        white = raw * (lax.rsqrt(level + 1e-06) * active)
        for tile in range(tiles):
            start = tile * LANES
            width = min(LANES, block - start)
            raw_ref[tile, w * 2 * FREQS : (w + 1) * 2 * FREQS, :width] = white[:, start : start + width]
    for out_ref, first in ((mine_ref, here * 2 * pairs), (other_ref, (1 - here) * 2 * pairs)):
        for pair in range(pairs):
            for tile in range(tiles):
                start = tile * LANES
                width = min(LANES, block - start)
                rows = [
                    raw_ref[tile, pl.ds(first + 2 * pair + part, windows, stride=2 * FREQS), :]
                    for part in (0, FREQS, 1, FREQS + 1)
                ]
                turned = jnp.concatenate(rows, axis=0).T
                out_ref[pair, start : start + width, :] = turned[:width].astype(jnp.bfloat16)


def merge_kernel(mine_ref, theirs_ref, *out_refs, total_windows):
    block, lanes = mine_ref.shape[1:]
    chunk_refs, half_refs, left_refs = out_refs[:CHUNKS], out_refs[CHUNKS:-CHUNKS], out_refs[-CHUNKS:]
    half = lanes // 2
    part = lanes // 4
    lane = lax.broadcasted_iota(jnp.int32, (block, lanes), 1)
    is_real = (lane // part) % 2 == 0
    per_chunk = chunk_refs[0].shape[0]
    per_half = half_refs[0].shape[0]
    for pair in range(mine_ref.shape[0]):
        mine = mine_ref[pair].astype(jnp.float32)
        theirs = theirs_ref[pair].astype(jnp.float32)
        both = (
            jnp.where(lane < half, mine, pltpu.roll(theirs, half, 1)),
            jnp.where(lane < half, pltpu.roll(mine, half, 1), theirs),
        )
        for step, values in enumerate(both):
            power = jnp.sum(values * values, axis=1, keepdims=True)
            root = lax.rsqrt(power * (1.0 / total_windows) + 1e-06)
            bin_at = 2 * pair + step
            scaled = values * root
            rounded = scaled.astype(jnp.bfloat16)
            chunk_refs[bin_at // per_chunk][bin_at % per_chunk] = rounded
            half_refs[bin_at // per_half][bin_at % per_half] = rounded
            straight = scaled * (1.0 / math.sqrt(total_windows))
            turned = jnp.where(
                is_real, pltpu.roll(straight, lanes - part, 1), -pltpu.roll(straight, part, 1)
            )
            left_ref = left_refs[bin_at // per_chunk]
            for group in range(block // ROWS):
                rows = slice(group * ROWS, (group + 1) * ROWS)
                for place, operand in enumerate((straight, turned)):
                    start = (2 * group + place) * ROWS
                    left_ref[bin_at % per_chunk, start : start + ROWS] = operand[rows].astype(
                        jnp.bfloat16
                    )


def band_kernel(*refs, chunks, sources, hops, first_tile):
    step = pl.program_id(0)
    mask_ref, real_ref, imag_ref, right_ref, left_ref = (refs[0], *refs[-4:])
    _, block, width = real_ref.shape
    depth = right_ref.shape[1]
    reach = min(HOPS * block - first_tile * LANES, width)
    origin = hops[0] * block
    filled = len(hops) * block
    per_chunk = pl.num_programs(0) // chunks
    parity = lax.rem(lax.axis_index("fiber"), 2)
    if right_ref.shape[0] > filled:
        right_ref[filled:] = jnp.zeros((right_ref.shape[0] - filled, depth), jnp.bfloat16)

    def gather(at, places, odd):
        for hop, place in zip(hops, places):
            operand, first_bin = place[odd]
            start = hop * block - origin
            right_ref[start : start + block] = refs[operand][first_bin + at]

    for chunk, (left, places) in enumerate(sources):
        at = step - chunk * per_chunk
        here = jnp.logical_and(at >= 0, at < per_chunk)

        @pl.when(jnp.logical_and(here, parity == 0))
        def _(at=at, places=places):
            gather(at, places, 0)

        @pl.when(jnp.logical_and(here, parity == 1))
        def _(at=at, places=places):
            gather(at, places, 1)

        if chunks > 1:
            @pl.when(here)
            def _(at=at, left=left):
                left_ref[...] = refs[left][at]

    def left_rows(start, size):
        if chunks > 1:
            return left_ref[start : start + size]
        return refs[sources[0][0]][step, start : start + size]

    lane_of = lax.broadcasted_iota(jnp.int32, (ROWS, LANES), 1)
    row_of = lax.broadcasted_iota(jnp.int32, (ROWS, LANES), 0)
    out_tiles = -(-reach // LANES)
    mask_from = 2 if first_tile == 0 else 0
    for group in range(block // ROWS):
        first = group * ROWS
        begin = first + 1 + first_tile * LANES - origin
        base = begin // LANES
        shift = begin - base * LANES + row_of
        tiles = (begin + ROWS - 2 + reach) // LANES - base + 1
        products = lax.dot_general(
            left_rows(2 * first, 2 * ROWS),
            right_ref[base * LANES : (base + tiles) * LANES],
            (((1,), (1,)), ((), ())),
            preferred_element_type=jnp.float32,
        )
        keep = lane_of >= shift
        source = (lane_of + shift) % LANES
        for out_at, out_ref in enumerate((real_ref, imag_ref)):
            rows = products[out_at * ROWS : (out_at + 1) * ROWS]
            for tile in range(out_tiles):
                start = tile * LANES
                wide = min(LANES, reach - start)
                values = rows[:, start : start + LANES]
                if tile + 1 < tiles:
                    values = jnp.where(keep, values, rows[:, start + LANES : start + 2 * LANES])
                moved = jnp.take_along_axis(values, source, axis=1, mode="promise_in_bounds")
                moved = moved.astype(jnp.bfloat16)
                if tile >= mask_from:
                    column = (tile - mask_from) * LANES
                    moved = moved * mask_ref[first : first + ROWS, column : column + LANES]
                out_ref[0, first : first + ROWS, start : start + wide] = moved[:, :wide]


def band(first_chunk, far, parts, mask, so_far, bins_here):
    per_chunk, _, depth = parts[0][0].shape
    block = mask.shape[0]
    chunks = len(parts)
    out = jax.ShapeDtypeStruct((bins_here, block, HOPS * block), jnp.bfloat16)
    near_width = 2 * block
    hops = (2, 3) if far else (0, 1, 2)
    first_bin = first_chunk * per_chunk
    out_spec = pl.BlockSpec((1, block, near_width), lambda i: (first_bin + i, 0, 1 if far else 0))
    operands = [mask]

    def index_of(array):
        for at, operand in enumerate(operands):
            if operand is array:
                return at
        operands.append(array)
        return len(operands) - 1

    sources = [
        (
            index_of(left),
            [tuple((index_of(array), offset) for array, offset in place) for place in places],
        )
        for left, places in parts
    ]
    in_specs = [pl.BlockSpec(memory_space=pltpu.VMEM)] * len(operands)
    aliases = {}
    if so_far is not None:
        aliases = {len(operands): 0, len(operands) + 1: 1}
        operands += list(so_far)
        in_specs += [pl.BlockSpec(memory_space=pl.ANY)] * 2
    wide = block if far else near_width
    return pl.pallas_call(
        functools.partial(
            band_kernel,
            chunks=chunks,
            sources=sources,
            hops=hops,
            first_tile=near_width // LANES if far else 0,
        ),
        grid=(chunks * per_chunk,),
        in_specs=in_specs,
        out_specs=[out_spec, out_spec],
        scratch_shapes=[
            pltpu.VMEM((-(-len(hops) * block // LANES) * LANES, depth), jnp.bfloat16),
            pltpu.VMEM((2 * block, depth), jnp.bfloat16),
        ],
        out_shape=[out, out],
        input_output_aliases=aliases,
        cost_estimate=pl.CostEstimate(
            flops=chunks * per_chunk * 4 * block * wide * depth,
            bytes_accessed=chunks * per_chunk * 4 * block * wide,
            transcendentals=0,
        ),
        compiler_params=pltpu.CompilerParams(vmem_limit_bytes=VMEM),
    )(*operands)


def body(samples, counts, reach_limit):
    windows_here, block, length = samples.shape
    tm_size = lax.axis_size("tm")
    fiber_size = lax.axis_size("fiber")
    total_windows = windows_here * tm_size
    bins_here = FREQS // tm_size
    per_chunk = bins_here // CHUNKS
    lanes = 4 * windows_here
    here = lax.axis_index("tm").astype(jnp.int32)
    is_even = lax.axis_index("fiber") % 2 == 0

    pair_shape = jax.ShapeDtypeStruct((bins_here // 2, block, lanes), jnp.bfloat16)
    mine, other = pl.pallas_call(
        spectra_kernel,
        in_specs=[
            pl.BlockSpec(memory_space=pltpu.SMEM),
            pl.BlockSpec(memory_space=pltpu.VMEM),
            pl.BlockSpec(memory_space=pltpu.VMEM),
        ],
        out_specs=[pl.BlockSpec(memory_space=pltpu.VMEM)] * 2,
        out_shape=[pair_shape, pair_shape],
        scratch_shapes=[
            pltpu.VMEM((-(-block // LANES), windows_here * 2 * FREQS, LANES), jnp.float32)
        ],
        compiler_params=pltpu.CompilerParams(vmem_limit_bytes=VMEM),
    )(
        jnp.stack([here, counts[0]]),
        samples,
        jnp.asarray(make_table(length, FREQS, FIRST_BIN)),
    )
    theirs = lax.ppermute(other, "tm", [(0, 1), (1, 0)])
    chunk_shape = jax.ShapeDtypeStruct((per_chunk, block, lanes), jnp.bfloat16)
    half_shape = jax.ShapeDtypeStruct((bins_here // 2, block, lanes), jnp.bfloat16)
    left_shape = jax.ShapeDtypeStruct((per_chunk, 2 * block, lanes), jnp.bfloat16)
    shapes = [chunk_shape] * CHUNKS + [half_shape] * 2 + [left_shape] * CHUNKS
    merged = pl.pallas_call(
        functools.partial(merge_kernel, total_windows=total_windows),
        in_specs=[pl.BlockSpec(memory_space=pltpu.VMEM)] * 2,
        out_specs=[pl.BlockSpec(memory_space=pltpu.VMEM)] * len(shapes),
        out_shape=shapes,
        compiler_params=pltpu.CompilerParams(vmem_limit_bytes=32 << 20),
    )(mine, theirs)
    own, halves, left = merged[:CHUNKS], merged[CHUNKS:-CHUNKS], merged[-CHUNKS:]

    down = [(i, i - 2) for i in range(2, fiber_size)]
    down_odd = [(i, i - 2) for i in range(3, fiber_size, 2)]
    to_even = [(i, i - 1) for i in range(1, fiber_size, 2)]
    to_odd = [(i - 1, i) for i in range(1, fiber_size, 2)]

    def pick(for_even, for_odd):
        even_one, for_even, for_odd = lax.optimization_barrier((is_even, for_even, for_odd))
        return lax.optimization_barrier(jnp.where(even_one, for_even, for_odd))

    def send(payload, route):
        return lax.ppermute(payload, "fiber", route)

    def after(payload, *others):
        return lax.optimization_barrier((payload, *others))

    near_reach = 2 * block
    offsets = jnp.arange(1, near_reach + HOPS * LANES + 1, dtype=jnp.int32)
    mask = (offsets[None, :] <= reach_limit[:, None]).astype(jnp.bfloat16)
    masks = (mask[:, 2 * LANES : near_reach], mask[:, near_reach:])

    def near(outs, chunk):
        first = chunk % 2 * per_chunk
        places = [
            ((own[chunk], 0), (own[chunk], 0)),
            ((ahead[chunk // 2], first), (up[chunk], 0)),
            ((z[chunk], 0), (z[chunk], 0)),
        ]
        return band(chunk, 0, [(left[chunk], places)], masks[0], outs, bins_here)

    def far(outs, first_chunk, count):
        last = [(z[5], up[4]), (back[1], z[4]), (back[2], z[5]), (back[3], z[6])]
        parts = []
        for chunk in range(first_chunk, first_chunk + count):
            places = [
                ((z[chunk], 0), (z[chunk], 0)),
                ((last[chunk][0], 0), (last[chunk][1], 0)),
            ]
            parts.append((left[chunk], places))
        return band(first_chunk, 1, parts, masks[1], outs, bins_here)

    z, up, ahead, back = {}, {}, {}, {}
    ahead[0] = send(halves[0], to_even)
    z[0] = send(own[0], down)
    z[1] = send(own[1], down)
    own_two, z[0] = after(own[2], z[0])
    z[2] = send(own_two, down)
    up[0] = send(z[0], to_odd)
    own_three, z[1] = after(own[3], z[1])
    z[3] = send(own_three, down)
    up[1] = send(z[1], to_odd)
    own_high, ahead[0], z[1], *masks = after(halves[1], ahead[0], z[1], *masks)
    ahead[1] = send(own_high, to_even)
    outs = near(None, 0)
    up[2] = send(z[2], to_odd)
    up[1], *outs = after(up[1], *outs)
    z[4] = send(pick(z[0], up[1]), down)
    outs = near(outs, 1)
    up[3] = send(z[3], to_odd)
    z_one, ahead[1] = after(z[1], ahead[1])
    back[1] = send(z_one, to_even)
    up[2], *outs = after(up[2], *outs)
    z[5] = send(pick(ahead[0][:per_chunk], up[2]), down)
    up[4] = send(z[4], to_odd)
    z_two, back[1] = after(z[2], back[1])
    back[2] = send(z_two, to_even)
    outs = near(outs, 2)
    up[3], *outs = after(up[3], *outs)
    z[6] = send(up[3], down_odd)
    outs = near(outs, 3)
    z_three, back[2], *outs = after(z[3], back[2], *outs)
    back[3] = send(z_three, to_even)
    outs = far(outs, 1, 1)
    outs = far(outs, 2, 1)
    outs = far(outs, 0, 1)
    outs = far(outs, 3, 1)
    return tuple(outs)


def solution(mesh):
    placed = (P("tm", ("grp", "fiber"), None), P(("grp", "fiber")), P(("grp", "fiber")))
    return jax.shard_map(
        body,
        mesh=mesh,
        in_specs=placed,
        out_specs=(P("tm", ("grp", "fiber"), None), P("tm", ("grp", "fiber"), None)),
        check_vma=False,
    )
```

time: 103 us -> 113 us (1.097)
  the two profiles are of different devices: /device:TPU:0 before, /device:TPU:30 now
where the time goes in v4:
time: 113 us
  Pallas kernels  44.5 us (39%)
  starting transfers between devices  41.2 us (36%)
  waiting for transfers between devices  17.7 us (16%)
  local copies, waits for them, and re-layouts  5.58 us (5%)
  other arithmetic  1.98 us (2%)
  between operations  1.55 us (1%)
    ppermute x17, starting transfers between devices, send(): return lax.ppermute(payload, 'fiber', route)  41.2 us
    pallas_call x8, Pallas kernels, band(): pl.pallas_call(functools.partial(band_kernel, chunks=chunks, sources=sour...  36.5 us
    ppermute x17, waiting for transfers between devices, send(): return lax.ppermute(payload, 'fiber', route)  15.6 us
    unnamed x22, local copies, waits for them, and re-layouts  5.5 us
    pallas_call x1, Pallas kernels, body(): pl.pallas_call(functools.partial(merge_kernel, total_windows=total_window...  4.32 us
    pallas_call x1, Pallas kernels, body(): pl.pallas_call(spectra_kernel, in_specs=[pl.BlockSpec(memory_space=pltpu....  3.62 us
  transfers between devices with their start and end apart: 18, of which 5 were waited for; matrix products, arithmetic and copies ran while one was open for 2% of the time, Pallas kernels for 29%

profile of v4, /device:TPU:30, one launch (start us, length us, event | category | flops | bytes accessed | tf_op | source)
XLA Modules:
  0.0 112.5 jit_solution(4118155948852177366)
XLA Ops:
  3.8 3.6 %shard_map.59 = (bf16[8,320,128]{2,1,0:T(8,128)(2,1)S(1)}, bf16[8,320,128]{2,1,0:T(8,128)(2,1)S(1)}) custom-call(s32[2]{0:T(128)S(1)} %pad_add_fusion.place_ref, bf16[32,320,128]{2,1,0:T(8,128)(2,1)S(1)} %copy-done.3, bf16[64,128]{1,0:T(8,128)(2,1)S(1)} %copy-done.10), custom_call_target="tpu_custom_call" | custom-call | tf_op jit(solution)/shard_map/pallas_call | solution.py:248
  7.5 2.1 %collective-permute-done.theirs_ref = bf16[8,320,128]{2,1,0:T(8,128)(2,1)S(1)} collective-permute-done((bf16[8,320,128]{2,1,0:T(8,128)(2,1)S(1)}, bf16[8,320,128]{2,1,0:T(8,128)(2,1)S(1)}, u32[]{:S(2)}, u32[]{:S(2)}) %collective-permute-start) | collective-permute-done | bytes 655392 | tf_op jit(solution)/shard_map/ppermute | solution.py:266
  9.6 4.3 %shard_map.60 = (bf16[4,320,128]{2,1,0:T(8,128)(2,1)S(1)}, bf16[4,320,128]{2,1,0:T(8,128)(2,1)S(1)}, bf16[4,320,128]{2,1,0:T(8,128)(2,1)}, bf16[4,320,128]{2,1,0...) custom-call(bf16[8,320,128]{2,1,0:T(8,128)(2,1)S(1)} %get-tuple-elem, ...), custom_call_target="tpu_custom_call" | custom-call | tf_op jit(solution)/shard_map/pallas_call | solution.py:271
  13.9 2.5 %collective-permute-start.1 = (bf16[8,320,128]{2,1,0:T(8,128)(2,1)S(1)}, bf16[8,320,128]{2,1,0:T(8,128)(2,1)S(1)}, u32[]{:S(2)}, u32[]{:S(2)}) collective-permute-start(bf16[8,320,128]{2,1,0:T(8,128)(2,1)S(1)} %get-tuple-element.63), channel_id=1, source_target_pairs={{2,0},{6,4},{10,8},{14,12},{3,1},{7,5},{11,9},{15,13},{18,16},{22,... | collective-permute-start | bytes 1966088 | tf_op jit(solution)/shard_map/ppermute | solution.py:290
  16.4 3.1 %collective-permute-start.2 = (bf16[4,320,128]{2,1,0:T(8,128)(2,1)S(1)}, bf16[4,320,128]{2,1,0:T(8,128)(2,1)}, u32[]{:S(2)}, u32[]{:S(2)}) collective-permute-start(bf16[4,320,128]{2,1,0:T(8,128)(2,1)S(1)} %get-tuple-element.65.refs_2_), channel_id=1, source_target_pairs={{4,0},{6,2},{8,4},{10,6},{12,8},{14,10},{5,1},{7,3},{9,5},{11,7},{... | collective-permute-start | bytes 983048 | tf_op jit(solution)/shard_map/ppermute | solution.py:290
  22.1 4.8 %collective-permute-done.2.refs_5_.refs_2_ = bf16[4,320,128]{2,1,0:T(8,128)(2,1)} collective-permute-done((bf16[4,320,128]{2,1,0:T(8,128)(2,1)S(1)}, bf16[4,320,128]{2,1,0:T(8,128)(2,1)}, u32[]{:S(2)}, u32[]{:S(2)}) %collective-permute-start.2) | collective-permute-done | bytes 327712 | tf_op jit(solution)/shard_map/ppermute | solution.py:290
  26.9 3.8 %collective-permute-done.1.refs_3_ = bf16[8,320,128]{2,1,0:T(8,128)(2,1)S(1)} collective-permute-done((bf16[8,320,128]{2,1,0:T(8,128)(2,1)S(1)}, bf16[8,320,128]{2,1,0:T(8,128)(2,1)S(1)}, u32[]{:S(2)}, u32[]{:S(2)}) %collective-permute-start.1) | collective-permute-done | bytes 655392 | tf_op jit(solution)/shard_map/ppermute | solution.py:290
  30.6 5.2 %collective-permute-start.6 = (bf16[8,320,128]{2,1,0:T(8,128)(2,1)}, bf16[8,320,128]{2,1,0:T(8,128)(2,1)}, u32[]{:S(2)}, u32[]{:S(2)}) collective-permute-start(bf16[8,320,128]{2,1,0:T(8,128)(2,1)} %get-tuple-element.74), channel_id=1, source_target_pairs={{2,0},{6,4},{10,8},{14,12},{3,1},{7,5},{11,9},{15,13},{18,16},{22,... | collective-permute-start | bytes 1966088 | tf_op jit(solution)/shard_map/ppermute | solution.py:290
  35.8 3.1 %collective-permute-start.5 = (bf16[4,320,128]{2,1,0:T(8,128)(2,1)}, bf16[4,320,128]{2,1,0:T(8,128)(2,1)}, u32[]{:S(2)}, u32[]{:S(2)}) collective-permute-start(bf16[4,320,128]{2,1,0:T(8,128)(2,1)} %get-tuple-element.72.refs_2_), channel_id=1, source_target_pairs={{4,0},{6,2},{8,4},{10,6},{12,8},{14,10},{5,1},{7,3},{9,5},{11,7},{... | collective-permute-start | bytes 983048 | tf_op jit(solution)/shard_map/ppermute | solution.py:290
  43.2 3.4 %collective-permute-done.5.refs_5_.refs_2_ = bf16[4,320,128]{2,1,0:T(8,128)(2,1)} collective-permute-done((bf16[4,320,128]{2,1,0:T(8,128)(2,1)}, bf16[4,320,128]{2,1,0:T(8,128)(2,1)}, u32[]{:S(2)}, u32[]{:S(2)}) %collective-permute-start.5) | collective-permute-done | bytes 327712 | tf_op jit(solution)/shard_map/ppermute | solution.py:290
  47.9 3.6 %collective-permute-done.12.refs_4_ = bf16[4,320,128]{2,1,0:T(8,128)(2,1)} collective-permute-done((bf16[4,320,128]{2,1,0:T(8,128)(2,1)S(1)}, bf16[4,320,128]{2,1,0:T(8,128)(2,1)}, u32[]{:S(2)}, u32[]{:S(2)}) %collective-permute-start.12) | collective-permute-done | bytes 327712 | tf_op jit(solution)/shard_map/ppermute | solution.py:290
  53.6 5.1 %shard_map.61 = (bf16[16,320,960]{2,1,0:T(8,128)(2,1)}, bf16[16,320,960]{2,1,0:T(8,128)(2,1)}) custom-call(bf16[320,384]{1,0:T(8,128)(2,1)S(1)} %get-tuple-element.77.refs_0_, bf16[4,640,128]{2,1,0:T(8,128)(2,1)S(1)} %copy-done.1, bf16[4,320,128]{2,1,0:T(8,128)(2,1)S(1)} %copy-done.5, bf16[8,320,128]{2,1,0:T(8,128)(2,1)S(1)} %collective-permute-done.1.refs_3_, ...), custom_call_target="tpu_custom_call" | custom-call | flops 419430400 | bytes 3276800 | tf_op jit(solution)/shard_map/pallas_call | solution.py:210
  61.1 4.0 %collective-permute-start.16 = (bf16[4,320,128]{2,1,0:T(8,128)(2,1)S(1)}, bf16[4,320,128]{2,1,0:T(8,128)(2,1)S(1)}, u32[]{:S(2)}, u32[]{:S(2)}) collective-permute-start(bf16[4,320,128]{2,1,0:T(8,128)(2,1)S(1)} %broadcast_select_fusion), channel_id=1, source_target_pairs={{4,0},{6,2},{8,4},{10,6},{12,8},{14,10},{5,1},{7,3},{9,5},{11,7},{... | collective-permute-start | bytes 983048 | tf_op jit(solution)/shard_map/ppermute | solution.py:290
  67.5 5.2 %shard_map.62 = (bf16[16,320,960]{2,1,0:T(8,128)(2,1)}, bf16[16,320,960]{2,1,0:T(8,128)(2,1)}) custom-call(bf16[320,384]{1,0:T(8,128)(2,1)S(1)} %get-tuple-element.77.refs_0_, bf16[4,640,128]{2,1,0:T(8,128)(2,1)S(1)} %get-tuple-element.80.refs_1_, bf16[4,320,128]{2,1,0:T(8,128)(2,1)S(1)} %copy-done.9, ...), custom_call_target="tpu_custom_call", output_to_operand_aliasing={{0}: (6, {}), {1}: (7, {})} | custom-call | flops 419430400 | bytes 3276800 | tf_op jit(solution)/shard_map/pallas_call | solution.py:210
  72.7 4.6 %collective-permute-start.8 = (bf16[4,320,128]{2,1,0:T(8,128)(2,1)}, bf16[4,320,128]{2,1,0:T(8,128)(2,1)S(1)}, u32[]{:S(2)}, u32[]{:S(2)}) collective-permute-start(bf16[4,320,128]{2,1,0:T(8,128)(2,1)} %collective-permute-done.5.refs_5_.refs_2_), channel_id=1, source_target_pairs={{2,0},{6,4},{10,8},{14,12},{3,1},{7,5},{11,9},{15,13},{18,16},{22,... | collective-permute-start | bytes 983048 | tf_op jit(solution)/shard_map/ppermute | solution.py:290
  77.3 2.4 %collective-permute-start.15 = (bf16[4,320,128]{2,1,0:T(8,128)(2,1)S(1)}, bf16[4,320,128]{2,1,0:T(8,128)(2,1)S(1)}, u32[]{:S(2)}, u32[]{:S(2)}) collective-permute-start(bf16[4,320,128]{2,1,0:T(8,128)(2,1)S(1)} %broadcast_select_fusion.1), channel_id=1, source_target_pairs={{4,0},{6,2},{8,4},{10,6},{12,8},{14,10},{5,1},{7,3},{9,5},{11,7},{... | collective-permute-start | bytes 983048 | tf_op jit(solution)/shard_map/ppermute | solution.py:290
  81.0 5.5 %shard_map.63 = (bf16[16,320,960]{2,1,0:T(8,128)(2,1)}, bf16[16,320,960]{2,1,0:T(8,128)(2,1)}) custom-call(bf16[320,384]{1,0:T(8,128)(2,1)S(1)} %get-tuple-element.77.refs_0_, bf16[4,640,128]{2,1,0:T(8,128)(2,1)S(1)} %get-tuple-element.79.refs_1_, bf16[4,320,128]{2,1,0:T(8,128)(2,1)} %get-tuple-element.72.refs_2_, ...), custom_call_target="tpu_custom_call", output_to_operand_aliasing={{0}: (6, {}), {1}: (7, {})} | custom-call | flops 419430400 | bytes 3276800 | tf_op jit(solution)/shard_map/pallas_call | solution.py:210
  86.5 2.3 %collective-permute-start.14 = (bf16[4,320,128]{2,1,0:T(8,128)(2,1)S(1)}, bf16[4,320,128]{2,1,0:T(8,128)(2,1)S(1)}, u32[]{:S(2)}, u32[]{:S(2)}) collective-permute-start(bf16[4,320,128]{2,1,0:T(8,128)(2,1)S(1)} %collective-permute-done.9.refs_4_), channel_id=1, source_target_pairs={{6,2},{10,6},{14,10},{7,3},{11,7},{15,11},{22,18},{26,22},{30,26},... | collective-permute-start | bytes 983048 | tf_op jit(solution)/shard_map/ppermute | solution.py:290
  88.9 5.3 %shard_map.64 = (bf16[16,320,960]{2,1,0:T(8,128)(2,1)}, bf16[16,320,960]{2,1,0:T(8,128)(2,1)}) custom-call(bf16[320,384]{1,0:T(8,128)(2,1)S(1)} %get-tuple-element.77.refs_0_, bf16[4,640,128]{2,1,0:T(8,128)(2,1)S(1)} %get-tuple-element.68.refs_1_, bf16[4,320,128]{2,1,0:T(8,128)(2,1)S(1)} %copy-done.7, ...), custom_call_target="tpu_custom_call", output_to_operand_aliasing={{0}: (6, {}), {1}: (7, {})} | custom-call | flops 419430400 | bytes 3276800 | tf_op jit(solution)/shard_map/pallas_call | solution.py:210
  94.2 2.9 %collective-permute-start.13 = (bf16[4,320,128]{2,1,0:T(8,128)(2,1)S(1)}, bf16[4,320,128]{2,1,0:T(8,128)(2,1)S(1)}, u32[]{:S(2)}, u32[]{:S(2)}) collective-permute-start(bf16[4,320,128]{2,1,0:T(8,128)(2,1)S(1)} %collective-permute-done.3.refs_5_.refs_2_), channel_id=1, source_target_pairs={{2,0},{6,4},{10,8},{14,12},{3,1},{7,5},{11,9},{15,13},{18,16},{22,... | collective-permute-start | bytes 983048 | tf_op jit(solution)/shard_map/ppermute | solution.py:290
  97.1 4.3 %shard_map.65 = (bf16[16,320,960]{2,1,0:T(8,128)(2,1)}, bf16[16,320,960]{2,1,0:T(8,128)(2,1)}) custom-call(bf16[320,384]{1,0:T(8,128)(2,1)S(1)} %get-tuple-element.67.refs_0_, bf16[4,640,128]{2,1,0:T(8,128)(2,1)S(1)} %get-tuple-element.80.refs_1_, ...), custom_call_target="tpu_custom_call", output_to_operand_aliasing={{0}: (5, {}), {1}: (6, {})} | custom-call | flops 209715200 | bytes 1638400 | tf_op jit(solution)/shard_map/pallas_call | solution.py:210
  101.4 4.4 %shard_map.66 = (bf16[16,320,960]{2,1,0:T(8,128)(2,1)}, bf16[16,320,960]{2,1,0:T(8,128)(2,1)}) custom-call(bf16[320,384]{1,0:T(8,128)(2,1)S(1)} %get-tuple-element.67.refs_0_, bf16[4,640,128]{2,1,0:T(8,128)(2,1)S(1)} %get-tuple-element.79.refs_1_, ...), custom_call_target="tpu_custom_call", output_to_operand_aliasing={{0}: (5, {}), {1}: (6, {})} | custom-call | flops 209715200 | bytes 1638400 | tf_op jit(solution)/shard_map/pallas_call | solution.py:210
  105.8 3.4 %shard_map.67 = (bf16[16,320,960]{2,1,0:T(8,128)(2,1)}, bf16[16,320,960]{2,1,0:T(8,128)(2,1)}) custom-call(bf16[320,384]{1,0:T(8,128)(2,1)S(1)} %get-tuple-element.67.refs_0_, bf16[4,640,128]{2,1,0:T(8,128)(2,1)S(1)} %copy-done.2, bf16[4,320,128]{2,1,0:T(8,128)(2,1)S(1)} %collective-permute-done.4.refs_5_.refs_2_, ...), custom_call_target="tpu_custom_call", output_to_operand_aliasing={{0}: (5, {}), {1}: (6, {})} | custom-call | flops 209715200 | bytes 1638400 | tf_op jit(solution)/shard_map/pallas_call | solution.py:210
  109.2 3.4 %shard_map.68 = (bf16[16,320,960]{2,1,0:T(8,128)(2,1)}, bf16[16,320,960]{2,1,0:T(8,128)(2,1)}) custom-call(bf16[320,384]{1,0:T(8,128)(2,1)S(1)} %get-tuple-element.67.refs_0_, bf16[4,640,128]{2,1,0:T(8,128)(2,1)S(1)} %get-tuple-element.68.refs_1_, ...), custom_call_target="tpu_custom_call", output_to_operand_aliasing={{0}: (5, {}), {1}: (6, {})} | custom-call | flops 209715200 | bytes 1638400 | tf_op jit(solution)/shard_map/pallas_call | solution.py:210
  (51 shorter events, 18.8 us)
Async XLA Ops:
  7.4 2.2 %collective-permute-start = (bf16[8,320,128]{2,1,0:T(8,128)(2,1)S(1)}, bf16[8,320,128]{2,1,0:T(8,128)(2,1)S(1)}, u32[]{:S(2)}, u32[]{:S(2)}) collective-permute-start(bf16[8,320,128]{2,1,0:T(8,128)(2,1)S(1)} %get-tuple-element.61), channel_id=1, source_target_pairs={{0,1},{1,0},{2,3},{3,2},{4,5},{5,4},{6,7},{7,6},{8,9},{9,8},{10,11... | collective-permute-start | bytes 1966088 | tf_op jit(solution)/shard_map/ppermute | solution.py:266
  13.9 21.9 %copy-start = (bf16[4,640,128]{2,1,0:T(8,128)(2,1)}, bf16[4,640,128]{2,1,0:T(8,128)(2,1)S(1)}, u32[]{:S(2)}) copy-start(bf16[4,640,128]{2,1,0:T(8,128)(2,1)S(1)} %get-tuple-element.82.refs_1_) | copy-start | bytes 1966084
  13.9 25.0 %copy-start.4 = (bf16[4,320,128]{2,1,0:T(8,128)(2,1)}, bf16[4,320,128]{2,1,0:T(8,128)(2,1)S(1)}, u32[]{:S(2)}) copy-start(bf16[4,320,128]{2,1,0:T(8,128)(2,1)S(1)} %get-tuple-element.71.refs_2_) | copy-start | bytes 983044
  13.9 26.3 %copy-start.6 = (bf16[4,320,128]{2,1,0:T(8,128)(2,1)}, bf16[4,320,128]{2,1,0:T(8,128)(2,1)S(1)}, u32[]{:S(2)}) copy-start(bf16[4,320,128]{2,1,0:T(8,128)(2,1)S(1)} %get-tuple-element.69.refs_2_) | copy-start | bytes 983044
  13.9 26.3 %copy-start.8 = (bf16[4,320,128]{2,1,0:T(8,128)(2,1)}, bf16[4,320,128]{2,1,0:T(8,128)(2,1)S(1)}, u32[]{:S(2)}) copy-start(bf16[4,320,128]{2,1,0:T(8,128)(2,1)S(1)} %get-tuple-element.65.refs_2_) | copy-start | bytes 983044
  13.9 16.7 %collective-permute-start.1 = (bf16[8,320,128]{2,1,0:T(8,128)(2,1)S(1)}, bf16[8,320,128]{2,1,0:T(8,128)(2,1)S(1)}, u32[]{:S(2)}, u32[]{:S(2)}) collective-permute-start(bf16[8,320,128]{2,1,0:T(8,128)(2,1)S(1)} %get-tuple-element.63), channel_id=1, source_target_pairs={{2,0},{6,4},{10,8},{14,12},{3,1},{7,5},{11,9},{15,13},{18,16},{22,... | collective-permute-start | bytes 1966088 | tf_op jit(solution)/shard_map/ppermute | solution.py:290
  16.4 10.5 %collective-permute-start.2 = (bf16[4,320,128]{2,1,0:T(8,128)(2,1)S(1)}, bf16[4,320,128]{2,1,0:T(8,128)(2,1)}, u32[]{:S(2)}, u32[]{:S(2)}) collective-permute-start(bf16[4,320,128]{2,1,0:T(8,128)(2,1)S(1)} %get-tuple-element.65.refs_2_), channel_id=1, source_target_pairs={{4,0},{6,2},{8,4},{10,6},{12,8},{14,10},{5,1},{7,3},{9,5},{11,7},{... | collective-permute-start | bytes 983048 | tf_op jit(solution)/shard_map/ppermute | solution.py:290
  20.3 15.5 %collective-permute-start.4 = (bf16[4,320,128]{2,1,0:T(8,128)(2,1)S(1)}, bf16[4,320,128]{2,1,0:T(8,128)(2,1)S(1)}, u32[]{:S(2)}, u32[]{:S(2)}) collective-permute-start(bf16[4,320,128]{2,1,0:T(8,128)(2,1)S(1)} %get-tuple-element.71.refs_2_), channel_id=1, source_target_pairs={{4,0},{6,2},{8,4},{10,6},{12,8},{14,10},{5,1},{7,3},{9,5},{11,7},{... | collective-permute-start | bytes 983048 | tf_op jit(solution)/shard_map/ppermute | solution.py:290
  30.6 28.1 %collective-permute-start.6 = (bf16[8,320,128]{2,1,0:T(8,128)(2,1)}, bf16[8,320,128]{2,1,0:T(8,128)(2,1)}, u32[]{:S(2)}, u32[]{:S(2)}) collective-permute-start(bf16[8,320,128]{2,1,0:T(8,128)(2,1)} %get-tuple-element.74), channel_id=1, source_target_pairs={{2,0},{6,4},{10,8},{14,12},{3,1},{7,5},{11,9},{15,13},{18,16},{22,... | collective-permute-start | bytes 1966088 | tf_op jit(solution)/shard_map/ppermute | solution.py:290
  35.8 10.8 %collective-permute-start.5 = (bf16[4,320,128]{2,1,0:T(8,128)(2,1)}, bf16[4,320,128]{2,1,0:T(8,128)(2,1)}, u32[]{:S(2)}, u32[]{:S(2)}) collective-permute-start(bf16[4,320,128]{2,1,0:T(8,128)(2,1)} %get-tuple-element.72.refs_2_), channel_id=1, source_target_pairs={{4,0},{6,2},{8,4},{10,6},{12,8},{14,10},{5,1},{7,3},{9,5},{11,7},{... | collective-permute-start | bytes 983048 | tf_op jit(solution)/shard_map/ppermute | solution.py:290
  38.9 12.6 %collective-permute-start.12 = (bf16[4,320,128]{2,1,0:T(8,128)(2,1)S(1)}, bf16[4,320,128]{2,1,0:T(8,128)(2,1)}, u32[]{:S(2)}, u32[]{:S(2)}) collective-permute-start(bf16[4,320,128]{2,1,0:T(8,128)(2,1)S(1)} %collective-permute-done.4.refs_5_.refs_2_), channel_id=1, source_target_pairs={{0,2},{4,6},{8,10},{12,14},{1,3},{5,7},{9,11},{13,15},{16,18},{20,... | collective-permute-start | bytes 983048 | tf_op jit(solution)/shard_map/ppermute | solution.py:290
  40.2 19.9 %collective-permute-start.11 = (bf16[4,320,128]{2,1,0:T(8,128)(2,1)}, bf16[4,320,128]{2,1,0:T(8,128)(2,1)}, u32[]{:S(2)}, u32[]{:S(2)}) collective-permute-start(bf16[4,320,128]{2,1,0:T(8,128)(2,1)} %collective-permute-done.2.refs_5_.refs_2_), channel_id=1, source_target_pairs={{0,2},{4,6},{8,10},{12,14},{1,3},{5,7},{9,11},{13,15},{16,18},{20,... | collective-permute-start | bytes 983048 | tf_op jit(solution)/shard_map/ppermute | solution.py:290
  41.5 23.6 %collective-permute-start.3 = (bf16[4,320,128]{2,1,0:T(8,128)(2,1)}, bf16[4,320,128]{2,1,0:T(8,128)(2,1)S(1)}, u32[]{:S(2)}, u32[]{:S(2)}) collective-permute-start(bf16[4,320,128]{2,1,0:T(8,128)(2,1)} %copy-done.6), channel_id=1, source_target_pairs={{4,0},{6,2},{8,4},{10,6},{12,8},{14,10},{5,1},{7,3},{9,5},{11,7},{... | collective-permute-start | bytes 983048 | tf_op jit(solution)/shard_map/ppermute | solution.py:290
  46.7 26.0 %collective-permute-start.10 = (bf16[4,320,128]{2,1,0:T(8,128)(2,1)}, bf16[4,320,128]{2,1,0:T(8,128)(2,1)S(1)}, u32[]{:S(2)}, u32[]{:S(2)}) collective-permute-start(bf16[4,320,128]{2,1,0:T(8,128)(2,1)} %collective-permute-done.5.refs_5_.refs_2_), channel_id=1, source_target_pairs={{0,2},{4,6},{8,10},{12,14},{1,3},{5,7},{9,11},{13,15},{16,18},{20,... | collective-permute-start | bytes 983048 | tf_op jit(solution)/shard_map/ppermute | solution.py:290
  58.7 14.0 %collective-permute-start.7 = (bf16[4,320,128]{2,1,0:T(8,128)(2,1)}, bf16[4,320,128]{2,1,0:T(8,128)(2,1)S(1)}, u32[]{:S(2)}, u32[]{:S(2)}) collective-permute-start(bf16[4,320,128]{2,1,0:T(8,128)(2,1)} %collective-permute-done.2.refs_5_.refs_2_), channel_id=1, source_target_pairs={{2,0},{6,4},{10,8},{14,12},{3,1},{7,5},{11,9},{15,13},{18,16},{22,... | collective-permute-start | bytes 983048 | tf_op jit(solution)/shard_map/ppermute | solution.py:290
  61.1 18.6 %collective-permute-start.16 = (bf16[4,320,128]{2,1,0:T(8,128)(2,1)S(1)}, bf16[4,320,128]{2,1,0:T(8,128)(2,1)S(1)}, u32[]{:S(2)}, u32[]{:S(2)}) collective-permute-start(bf16[4,320,128]{2,1,0:T(8,128)(2,1)S(1)} %broadcast_select_fusion), channel_id=1, source_target_pairs={{4,0},{6,2},{8,4},{10,6},{12,8},{14,10},{5,1},{7,3},{9,5},{11,7},{... | collective-permute-start | bytes 983048 | tf_op jit(solution)/shard_map/ppermute | solution.py:290
  65.2 21.3 %collective-permute-start.9 = (bf16[4,320,128]{2,1,0:T(8,128)(2,1)S(1)}, bf16[4,320,128]{2,1,0:T(8,128)(2,1)S(1)}, u32[]{:S(2)}, u32[]{:S(2)}) collective-permute-start(bf16[4,320,128]{2,1,0:T(8,128)(2,1)S(1)} %collective-permute-done.3.refs_5_.refs_2_), channel_id=1, source_target_pairs={{0,2},{4,6},{8,10},{12,14},{1,3},{5,7},{9,11},{13,15},{16,18},{20,... | collective-permute-start | bytes 983048 | tf_op jit(solution)/shard_map/ppermute | solution.py:290
  72.7 21.5 %collective-permute-start.8 = (bf16[4,320,128]{2,1,0:T(8,128)(2,1)}, bf16[4,320,128]{2,1,0:T(8,128)(2,1)S(1)}, u32[]{:S(2)}, u32[]{:S(2)}) collective-permute-start(bf16[4,320,128]{2,1,0:T(8,128)(2,1)} %collective-permute-done.5.refs_5_.refs_2_), channel_id=1, source_target_pairs={{2,0},{6,4},{10,8},{14,12},{3,1},{7,5},{11,9},{15,13},{18,16},{22,... | collective-permute-start | bytes 983048 | tf_op jit(solution)/shard_map/ppermute | solution.py:290
  77.3 24.1 %collective-permute-start.15 = (bf16[4,320,128]{2,1,0:T(8,128)(2,1)S(1)}, bf16[4,320,128]{2,1,0:T(8,128)(2,1)S(1)}, u32[]{:S(2)}, u32[]{:S(2)}) collective-permute-start(bf16[4,320,128]{2,1,0:T(8,128)(2,1)S(1)} %broadcast_select_fusion.1), channel_id=1, source_target_pairs={{4,0},{6,2},{8,4},{10,6},{12,8},{14,10},{5,1},{7,3},{9,5},{11,7},{... | collective-permute-start | bytes 983048 | tf_op jit(solution)/shard_map/ppermute | solution.py:290
  79.7 26.1 %collective-permute-start.17 = (bf16[4,320,128]{2,1,0:T(8,128)(2,1)S(1)}, bf16[4,320,128]{2,1,0:T(8,128)(2,1)S(1)}, u32[]{:S(2)}, u32[]{:S(2)}) collective-permute-start(bf16[4,320,128]{2,1,0:T(8,128)(2,1)S(1)} %collective-permute-done.16.refs_4_), channel_id=1, source_target_pairs={{0,2},{4,6},{8,10},{12,14},{1,3},{5,7},{9,11},{13,15},{16,18},{20,... | collective-permute-start | bytes 983048 | tf_op jit(solution)/shard_map/ppermute | solution.py:290
  81.0 7.9 %copy-start.7 = (bf16[4,320,128]{2,1,0:T(8,128)(2,1)S(1)}, bf16[4,320,128]{2,1,0:T(8,128)(2,1)}, u32[]{:S(2)}) copy-start(bf16[4,320,128]{2,1,0:T(8,128)(2,1)} %copy-done.6) | copy-start | bytes 983044
  86.5 22.7 %collective-permute-start.14 = (bf16[4,320,128]{2,1,0:T(8,128)(2,1)S(1)}, bf16[4,320,128]{2,1,0:T(8,128)(2,1)S(1)}, u32[]{:S(2)}, u32[]{:S(2)}) collective-permute-start(bf16[4,320,128]{2,1,0:T(8,128)(2,1)S(1)} %collective-permute-done.9.refs_4_), channel_id=1, source_target_pairs={{6,2},{10,6},{14,10},{7,3},{11,7},{15,11},{22,18},{26,22},{30,26},... | collective-permute-start | bytes 983048 | tf_op jit(solution)/shard_map/ppermute | solution.py:290
  94.2 15.0 %collective-permute-start.13 = (bf16[4,320,128]{2,1,0:T(8,128)(2,1)S(1)}, bf16[4,320,128]{2,1,0:T(8,128)(2,1)S(1)}, u32[]{:S(2)}, u32[]{:S(2)}) collective-permute-start(bf16[4,320,128]{2,1,0:T(8,128)(2,1)S(1)} %collective-permute-done.3.refs_5_.refs_2_), channel_id=1, source_target_pairs={{2,0},{6,4},{10,8},{14,12},{3,1},{7,5},{11,9},{15,13},{18,16},{22,... | collective-permute-start | bytes 983048 | tf_op jit(solution)/shard_map/ppermute | solution.py:290
  101.4 4.4 %copy-start.2 = (bf16[4,640,128]{2,1,0:T(8,128)(2,1)S(1)}, bf16[4,640,128]{2,1,0:T(8,128)(2,1)}, u32[]{:S(2)}) copy-start(bf16[4,640,128]{2,1,0:T(8,128)(2,1)} %copy-done) | copy-start | bytes 1966084
  (5 other events, 5.5 us)

commit v5 on v3

--- a/solution.py
+++ b/solution.py
@@ -15,7 +15,6 @@
 LANES = 128
 HOPS = 3
 ROWS = 64
-CHUNKS = 4
 VMEM = 16 << 20
 
 
@@ -81,31 +80,31 @@
             out_refs[bin_at // per_chunk][bin_at % per_chunk] = (values * root).astype(jnp.bfloat16)
 
 
-def band_kernel(even_ref, own_ref, *refs, hops, first_tile, total_windows):
-    at = pl.program_id(0)
-    far = [hop for hop in hops if hop]
-    pieces = refs[: 2 * len(far)]
-    mask_ref, real_ref, imag_ref = (refs[2 * len(far)], *refs[-4:-2])
-    right_ref, left_ref = refs[-2:]
+def band_kernel(*refs, own_first, places, hops, first_tile, total_windows):
+    step = pl.program_id(0)
+    own_ref, mask_ref = refs[:2]
+    real_ref, imag_ref, right_ref, left_ref = refs[-4:]
     _, block, depth = own_ref.shape
     reach = min(HOPS * block - first_tile * LANES, real_ref.shape[2])
-    is_even = even_ref[0] == 1
     origin = hops[0] * block
+    filled = len(hops) * block
+    parity = lax.rem(lax.axis_index("fiber"), 2)
+    own = own_ref[own_first + step]
     if hops[0] == 0:
-        right_ref[:block] = own_ref[at]
-
-    def gather(parity):
-        for place, hop in enumerate(far):
-            start = hop * block - origin
-            right_ref[start : start + block] = pieces[2 * place + parity][at]
-
-    filled = len(hops) * block
+        right_ref[:block] = own
     if right_ref.shape[0] > filled:
         right_ref[filled:] = jnp.zeros((right_ref.shape[0] - filled, depth), jnp.bfloat16)
-    pl.when(is_even)(lambda: gather(0))
-    pl.when(jnp.logical_not(is_even))(lambda: gather(1))
-
-    wide = own_ref[at].astype(jnp.float32) * (1.0 / math.sqrt(total_windows))
+
+    def gather(odd):
+        for hop, place in zip([hop for hop in hops if hop], places):
+            operand, first_bin = place[odd]
+            start = hop * block - origin
+            right_ref[start : start + block] = refs[operand][first_bin + step]
+
+    pl.when(parity == 0)(lambda: gather(0))
+    pl.when(parity == 1)(lambda: gather(1))
+
+    wide = own.astype(jnp.float32) * (1.0 / math.sqrt(total_windows))
     part = depth // 4
     lane = lax.broadcasted_iota(jnp.int32, (block, depth), 1)
     turned = jnp.where(
@@ -149,20 +148,23 @@
                 out_ref[0, first : first + ROWS, start : start + width] = moved[:, :width]
 
 
-def band(even, own, pieces, mask, so_far, chunk, bins_here, total_windows, far):
-    per_chunk, block, depth = own.shape
+def band(first_bin, bins, far, own, places, mask, so_far, bins_here, total_windows):
+    _, block, depth = own[0].shape
     out = jax.ShapeDtypeStruct((bins_here, block, HOPS * block), jnp.bfloat16)
     near_width = 2 * block
     hops = (2, 3) if far else (0, 1, 2)
-    out_spec = pl.BlockSpec(
-        (1, block, near_width), lambda i: (chunk * per_chunk + i, 0, 1 if far else 0)
-    )
-    operands = [even, own]
-    for piece in pieces:
-        operands += piece
-    operands.append(mask)
-    in_specs = [pl.BlockSpec(memory_space=pltpu.SMEM)]
-    in_specs += [pl.BlockSpec(memory_space=pltpu.VMEM)] * (len(operands) - 1)
+    out_spec = pl.BlockSpec((1, block, near_width), lambda i: (first_bin + i, 0, 1 if far else 0))
+    operands = [own[0], mask]
+
+    def index_of(array):
+        for at, operand in enumerate(operands):
+            if operand is array:
+                return at
+        operands.append(array)
+        return len(operands) - 1
+
+    places = [tuple((index_of(array), offset) for array, offset in place) for place in places]
+    in_specs = [pl.BlockSpec(memory_space=pltpu.VMEM)] * len(operands)
     aliases = {}
     if so_far is not None:
         aliases = {len(operands): 0, len(operands) + 1: 1}
@@ -172,11 +174,13 @@
     return pl.pallas_call(
         functools.partial(
             band_kernel,
+            own_first=own[1],
+            places=places,
             hops=hops,
             first_tile=near_width // LANES if far else 0,
             total_windows=total_windows,
         ),
-        grid=(per_chunk,),
+        grid=(bins,),
         in_specs=in_specs,
         out_specs=[out_spec, out_spec],
         scratch_shapes=[
@@ -186,8 +190,8 @@
         out_shape=[out, out],
         input_output_aliases=aliases,
         cost_estimate=pl.CostEstimate(
-            flops=per_chunk * 4 * block * wide * depth,
-            bytes_accessed=per_chunk * 4 * block * wide,
+            flops=bins * 4 * block * wide * depth,
+            bytes_accessed=bins * 4 * block * wide,
             transcendentals=0,
         ),
         compiler_params=pltpu.CompilerParams(vmem_limit_bytes=VMEM),
@@ -200,11 +204,9 @@
     fiber_size = lax.axis_size("fiber")
     total_windows = windows_here * tm_size
     bins_here = FREQS // tm_size
-    per_chunk = bins_here // CHUNKS
     lanes = 4 * windows_here
     here = lax.axis_index("tm").astype(jnp.int32)
     is_even = lax.axis_index("fiber") % 2 == 0
-    even = is_even.astype(jnp.int32)[None]
 
     pair_shape = jax.ShapeDtypeStruct((bins_here // 2, block, lanes), jnp.bfloat16)
     mine, other = pl.pallas_call(
@@ -226,16 +228,19 @@
         jnp.asarray(make_table(length, FREQS, FIRST_BIN)),
     )
     theirs = lax.ppermute(other, "tm", [(0, 1), (1, 0)])
-    chunk_shape = jax.ShapeDtypeStruct((per_chunk, block, lanes), jnp.bfloat16)
+    half = bins_here // 2
+    quarter = half // 2
+    half_shape = jax.ShapeDtypeStruct((half, block, lanes), jnp.bfloat16)
     own = pl.pallas_call(
         functools.partial(merge_kernel, total_windows=total_windows),
         in_specs=[pl.BlockSpec(memory_space=pltpu.VMEM)] * 2,
-        out_specs=[pl.BlockSpec(memory_space=pltpu.VMEM)] * CHUNKS,
-        out_shape=[chunk_shape] * CHUNKS,
+        out_specs=[pl.BlockSpec(memory_space=pltpu.VMEM)] * 2,
+        out_shape=[half_shape] * 2,
         compiler_params=pltpu.CompilerParams(vmem_limit_bytes=32 << 20),
     )(mine, theirs)
 
     down = [(i, i - 2) for i in range(2, fiber_size)]
+    down_odd = [(i, i - 2) for i in range(3, fiber_size, 2)]
     to_even = [(i, i - 1) for i in range(1, fiber_size, 2)]
     to_odd = [(i - 1, i) for i in range(1, fiber_size, 2)]
 
@@ -243,47 +248,49 @@
         even_one, for_even, for_odd = lax.optimization_barrier((is_even, for_even, for_odd))
         return lax.optimization_barrier(jnp.where(even_one, for_even, for_odd))
 
-    def move_down(for_even, for_odd):
-        return lax.ppermute(pick(for_even, for_odd), "fiber", down)
-
-    def cross(for_even, for_odd):
-        return lax.ppermute(pick(for_even, for_odd), "fiber", to_even + to_odd)
-
-    near = 2 * block
-    offsets = jnp.arange(1, near + HOPS * LANES + 1, dtype=jnp.int32)
+    def send(payload, route):
+        return lax.ppermute(payload, "fiber", route)
+
+    def after(payload, *others):
+        return lax.optimization_barrier((payload, *others))
+
+    near_reach = 2 * block
+    offsets = jnp.arange(1, near_reach + HOPS * LANES + 1, dtype=jnp.int32)
     mask = (offsets[None, :] <= reach_limit[:, None]).astype(jnp.bfloat16)
-    masks = (mask[:, 2 * LANES : near], mask[:, near:])
-
-    def work(outs, chunk, far, *pieces):
+    masks = (mask[:, 2 * LANES : near_reach], mask[:, near_reach:])
+
+    def near(outs, at, one, two):
         return band(
-            even, own[chunk], pieces, masks[far], outs, chunk, bins_here, total_windows, far
-        )
-
-    z, y = {}, {}
-    z[0] = move_down(own[0], own[2])
-    y[0] = lax.ppermute(own[0], "fiber", to_even)
-    z[1] = move_down(own[1], own[3])
-    z[0], y[0], *masks = lax.optimization_barrier((z[0], y[0], *masks))
-    y[1] = cross(z[0], own[1])
-    z[2] = move_down(own[2], y[1])
-    y[2] = cross(z[1], own[2])
-    z[3] = move_down(own[3], y[2])
-    y[3] = cross(z[2], own[3])
-    z[4] = move_down(y[0], y[3])
-    y[4] = cross(z[3], z[0])
-    outs = work(None, 2, 0, (y[2], y[3]), (z[2], z[0]))
-    z[4], *outs = lax.optimization_barrier((z[4], *outs))
-    z[5] = move_down(y[1], y[4])
-    y[5] = cross(z[4], z[1])
-    outs = work(outs, 3, 0, (y[3], y[4]), (z[3], z[1]))
-    outs = work(outs, 2, 1, (z[2], z[0]), (y[4], z[4]))
-    z[5], *outs = lax.optimization_barrier((z[5], *outs))
-    y[6] = lax.ppermute(z[5], "fiber", to_odd)
-    outs = work(outs, 3, 1, (z[3], z[1]), (y[5], z[5]))
-    outs = work(outs, 0, 0, (y[0], y[1]), (z[0], y[5]))
-    outs = work(outs, 0, 1, (z[0], y[5]), (z[4], z[2]))
-    outs = work(outs, 1, 0, (y[1], y[2]), (z[1], y[6]))
-    outs = work(outs, 1, 1, (z[1], y[6]), (z[5], z[3]))
+            at * half, half, 0, (own[at], 0), (one, two), masks[0], outs, bins_here, total_windows
+        )
+
+    def far(outs, at, first, bins, two, three):
+        return band(
+            at * half + first, bins, 1, (own[at], first), (two, three), masks[1], outs, bins_here,
+            total_windows,
+        )
+
+    ahead_low = send(own[0], to_even)
+    z_low = send(own[0], down)
+    own_high, ahead_low, *masks = after(own[1], ahead_low, *masks)
+    z_high = send(own_high, down)
+    y_low = send(z_low, to_even + to_odd)
+    up_high = send(z_high, to_odd)
+    own_high, y_low = after(own[1], y_low)
+    ahead_high = send(own_high, to_even)
+    z_next = send(y_low, down_odd)
+    outs = near(None, 0, ((ahead_low, 0), (y_low, 0)), ((z_low, 0), (z_low, 0)))
+    up_high, *outs = after(up_high, *outs)
+    last = [
+        send(pick(ahead_high[at : at + quarter], up_high[at : at + quarter]), down)
+        for at in (0, quarter)
+    ]
+    outs = near(outs, 1, ((ahead_high, 0), (up_high, 0)), ((z_high, 0), (z_high, 0)))
+    outs = far(outs, 0, 0, half, ((z_low, 0), (z_low, 0)), ((y_low, 0), (z_next, 0)))
+    for part, at in enumerate((0, quarter)):
+        outs = far(
+            outs, 1, at, quarter, ((z_high, at), (z_high, at)), ((last[part], 0), (last[part], 0))
+        )
     return tuple(outs)
 
 

time: 103 us -> 94.1 us (0.914)
  starting transfers between devices: 20.6 us -> 12.8 us
  Pallas kernels: 38.9 us -> 33.6 us
  local copies, waits for them, and re-layouts: 4.22 us -> 9.49 us
  other arithmetic: 3.75 us -> 1.01 us
    ppermute x13 -> x9, starting transfers between devices: 20.1 us -> 12.3 us  [send(): return lax.ppermute(payload, 'fiber', route)]
    pallas_call x8 -> x5, Pallas kernels: 33.9 us -> 28.6 us  [band(): pl.pallas_call(functools.partial(band_kernel, own_first=own[1], places=pl...]
    unnamed x16 -> x22, local copies, waits for them, and re-layouts: 4.16 us -> 9.35 us
    select_n x11 -> x2, other arithmetic: 2.82 us -> 0.07 us  [pick(): return lax.optimization_barrier(jnp.where(even_one, for_even, for_odd))]
    ppermute x13 -> x9, waiting for transfers between devices: 32.7 us -> 32.7 us  [send(): return lax.ppermute(payload, 'fiber', route)]
  transfers between devices with their start and end apart: 14 -> 10, of which waited for: 9 -> 4; matrix products, arithmetic and copies ran while one was open for 4% -> 1% of each run, Pallas kernels for 26% -> 27%
where the time goes in v5:
time: 94.1 us; the launch traced here: 92.8 us
  waiting for transfers between devices  34.4 us (37%)
  Pallas kernels  33.6 us (36%)
  starting transfers between devices  12.8 us (14%)
  local copies, waits for them, and re-layouts  9.49 us (10%)
  between operations  1.48 us (2%)
  other arithmetic  1.01 us (1%)
    ppermute x9, waiting for transfers between devices, send(): return lax.ppermute(payload, 'fiber', route)  32.7 us
    pallas_call x5, Pallas kernels, band(): pl.pallas_call(functools.partial(band_kernel, own_first=own[1], places=pl...  28.6 us
    ppermute x9, starting transfers between devices, send(): return lax.ppermute(payload, 'fiber', route)  12.3 us
    unnamed x22, local copies, waits for them, and re-layouts  9.35 us
    pallas_call x1, Pallas kernels, body(): pl.pallas_call(spectra_kernel, in_specs=[pl.BlockSpec(memory_space=pltpu....  3.62 us
  transfers between devices with their start and end apart: 10, of which 4 were waited for; matrix products, arithmetic and copies ran while one was open for 1% of the time, Pallas kernels for 27%

profile of v5, /device:TPU:0, one launch (start us, length us, event | category | flops | bytes accessed | tf_op | source)
XLA Modules:
  0.0 92.8 jit_solution(7749673059346144607)
XLA Ops:
  1.4 1.7 %copy-done = bf16[32,320,128]{2,1,0:T(8,128)(2,1)S(1)} copy-done((bf16[32,320,128]{2,1,0:T(8,128)(2,1)S(1)}, bf16[32,320,128]{2,1,0:T(8,128)(2,1)}, u32[]{:S(2)}) %copy-start) | copy-done | bytes 2621464
  3.8 3.6 %shard_map.59 = (bf16[8,320,128]{2,1,0:T(8,128)(2,1)S(1)}, bf16[8,320,128]{2,1,0:T(8,128)(2,1)S(1)}) custom-call(s32[2]{0:T(128)S(1)} %pad_add_fusion.place_ref, bf16[32,320,128]{2,1,0:T(8,128)(2,1)S(1)} %copy-done, bf16[64,128]{1,0:T(8,128)(2,1)S(1)} %copy-done.8), custom_call_target="tpu_custom_call" | custom-call | tf_op jit(solution)/shard_map/pallas_call | solution.py:212
  8.0 1.7 %collective-permute-done.theirs_ref = bf16[8,320,128]{2,1,0:T(8,128)(2,1)S(1)} collective-permute-done((bf16[8,320,128]{2,1,0:T(8,128)(2,1)S(1)}, bf16[8,320,128]{2,1,0:T(8,128)(2,1)S(1)}, u32[]{:S(2)}, u32[]{:S(2)}) %collective-permute-start) | collective-permute-done | bytes 655392 | tf_op jit(solution)/shard_map/ppermute | solution.py:230
  9.7 1.4 %shard_map.60 = (bf16[8,320,128]{2,1,0:T(8,128)(2,1)S(1)}, bf16[8,320,128]{2,1,0:T(8,128)(2,1)S(1)}) custom-call(bf16[8,320,128]{2,1,0:T(8,128)(2,1)S(1)} %get-tuple-element.29.mine_ref, bf16[8,320,128]{2,1,0:T(8,128)(2,1)S(1)} %collective-permute-done.theirs_ref), custom_call_target="tpu_custom_call" | custom-call | tf_op jit(solution)/shard_map/pallas_call | solution.py:234
  11.1 1.3 %collective-permute-start.1 = (bf16[8,320,128]{2,1,0:T(8,128)(2,1)S(1)}, bf16[8,320,128]{2,1,0:T(8,128)(2,1)S(1)}, u32[]{:S(2)}, u32[]{:S(2)}) collective-permute-start(bf16[8,320,128]{2,1,0:T(8,128)(2,1)S(1)} %get-tuple-element.32.refs_0_), channel_id=1, source_target_pairs={{2,0},{6,4},{10,8},{14,12},{3,1},{7,5},{11,9},{15,13},{18,16},{22,... | collective-permute-start | bytes 1966088 | tf_op jit(solution)/shard_map/ppermute | solution.py:252
  12.4 1.3 %collective-permute-start.3 = (bf16[8,320,128]{2,1,0:T(8,128)(2,1)S(1)}, bf16[8,320,128]{2,1,0:T(8,128)(2,1)S(1)}, u32[]{:S(2)}, u32[]{:S(2)}) collective-permute-start(bf16[8,320,128]{2,1,0:T(8,128)(2,1)S(1)} %get-tuple-element.32.refs_0_), channel_id=1, source_target_pairs={{4,0},{6,2},{8,4},{10,6},{12,8},{14,10},{5,1},{7,3},{9,5},{11,7},{... | collective-permute-start | bytes 1966088 | tf_op jit(solution)/shard_map/ppermute | solution.py:252
  14.6 15.7 %collective-permute-done.1.refs_2_ = bf16[8,320,128]{2,1,0:T(8,128)(2,1)S(1)} collective-permute-done((bf16[8,320,128]{2,1,0:T(8,128)(2,1)S(1)}, bf16[8,320,128]{2,1,0:T(8,128)(2,1)S(1)}, u32[]{:S(2)}, u32[]{:S(2)}) %collective-permute-start.1) | collective-permute-done | bytes 655392 | tf_op jit(solution)/shard_map/ppermute | solution.py:252
  31.1 1.3 %collective-permute-start.2 = (bf16[8,320,128]{2,1,0:T(8,128)(2,1)S(1)}, bf16[8,320,128]{2,1,0:T(8,128)(2,1)S(1)}, u32[]{:S(2)}, u32[]{:S(2)}) collective-permute-start(bf16[8,320,128]{2,1,0:T(8,128)(2,1)S(1)} %get-tuple-element.35.refs_0_), channel_id=1, source_target_pairs={{4,0},{6,2},{8,4},{10,6},{12,8},{14,10},{5,1},{7,3},{9,5},{11,7},{... | collective-permute-start | bytes 1966088 | tf_op jit(solution)/shard_map/ppermute | solution.py:252
  32.4 2.3 %collective-permute-start.4 = (bf16[8,320,128]{2,1,0:T(8,128)(2,1)S(1)}, bf16[8,320,128]{2,1,0:T(8,128)(2,1)S(1)}, u32[]{:S(2)}, u32[]{:S(2)}) collective-permute-start(bf16[8,320,128]{2,1,0:T(8,128)(2,1)S(1)} %collective-permute-done.3.refs_4_.refs_2_), channel_id=1, source_target_pairs={{2,0},{6,4},{10,8},{14,12},{0,2},{4,6},{8,10},{12,14},{3,1},{7,5},... | collective-permute-start | bytes 1966088 | tf_op jit(solution)/shard_map/ppermute | solution.py:252
  35.5 14.1 %collective-permute-done.2.refs_4_.refs_2_ = bf16[8,320,128]{2,1,0:T(8,128)(2,1)S(1)} collective-permute-done((bf16[8,320,128]{2,1,0:T(8,128)(2,1)S(1)}, bf16[8,320,128]{2,1,0:T(8,128)(2,1)S(1)}, u32[]{:S(2)}, u32[]{:S(2)}) %collective-permute-start.2) | collective-permute-done | bytes 655392 | tf_op jit(solution)/shard_map/ppermute | solution.py:252
  49.6 1.5 %collective-permute-start.6 = (bf16[8,320,128]{2,1,0:T(8,128)(2,1)S(1)}, bf16[8,320,128]{2,1,0:T(8,128)(2,1)S(1)}, u32[]{:S(2)}, u32[]{:S(2)}) collective-permute-start(bf16[8,320,128]{2,1,0:T(8,128)(2,1)S(1)} %collective-permute-done.2.refs_4_.refs_2_), channel_id=1, source_target_pairs={{0,2},{4,6},{8,10},{12,14},{1,3},{5,7},{9,11},{13,15},{16,18},{20,... | collective-permute-start | bytes 1966088 | tf_op jit(solution)/shard_map/ppermute | solution.py:252
  52.0 1.3 %collective-permute-start.5 = (bf16[8,320,128]{2,1,0:T(8,128)(2,1)S(1)}, bf16[8,320,128]{2,1,0:T(8,128)(2,1)S(1)}, u32[]{:S(2)}, u32[]{:S(2)}) collective-permute-start(bf16[8,320,128]{2,1,0:T(8,128)(2,1)S(1)} %get-tuple-element.35.refs_0_), channel_id=1, source_target_pairs={{2,0},{6,4},{10,8},{14,12},{3,1},{7,5},{11,9},{15,13},{18,16},{22,... | collective-permute-start | bytes 1966088 | tf_op jit(solution)/shard_map/ppermute | solution.py:252
  54.0 1.1 %copy-done.2 = bf16[8,320,128]{2,1,0:T(8,128)(2,1)S(1)} copy-done((bf16[8,320,128]{2,1,0:T(8,128)(2,1)S(1)}, bf16[8,320,128]{2,1,0:T(8,128)(2,1)}, u32[]{:S(2)}) %copy-start.2) | copy-done | bytes 655384
  55.1 1.1 %copy-done.4 = bf16[8,320,128]{2,1,0:T(8,128)(2,1)S(1)} copy-done((bf16[8,320,128]{2,1,0:T(8,128)(2,1)S(1)}, bf16[8,320,128]{2,1,0:T(8,128)(2,1)}, u32[]{:S(2)}) %copy-start.4) | copy-done | bytes 655384
  56.2 1.1 %copy-done.7 = bf16[8,320,128]{2,1,0:T(8,128)(2,1)S(1)} copy-done((bf16[8,320,128]{2,1,0:T(8,128)(2,1)S(1)}, bf16[8,320,128]{2,1,0:T(8,128)(2,1)}, u32[]{:S(2)}) %copy-start.7) | copy-done | bytes 655384
  57.3 1.1 %copy-done.10 = bf16[8,320,128]{2,1,0:T(8,128)(2,1)S(1)} copy-done((bf16[8,320,128]{2,1,0:T(8,128)(2,1)S(1)}, bf16[8,320,128]{2,1,0:T(8,128)(2,1)}, u32[]{:S(2)}) %copy-start.10) | copy-done | bytes 655384
  58.4 7.7 %shard_map.61 = (bf16[16,320,960]{2,1,0:T(8,128)(2,1)}, bf16[16,320,960]{2,1,0:T(8,128)(2,1)}) custom-call(bf16[8,320,128]{2,1,0:T(8,128)(2,1)S(1)} %copy-done.2, bf16[320,384]{1,0:T(8,128)(2,1)S(1)} %get-tuple-element.36.refs_1_, bf16[8,320,128]{2,1,0:T(8,128)(2,1)S(1)} %copy-done.10, bf16[8,320,128]{2,1,0:T(8,128)(2,1)S(1)} %copy-done.7, ...), custom_call_target="tpu_custom_call" | custom-call | flops 838860800 | bytes 6553600 | tf_op jit(solution)/shard_map/pallas_call | solution.py:174
  66.1 2.9 %collective-permute-done.5.refs_2_ = bf16[8,320,128]{2,1,0:T(8,128)(2,1)S(1)} collective-permute-done((bf16[8,320,128]{2,1,0:T(8,128)(2,1)S(1)}, bf16[8,320,128]{2,1,0:T(8,128)(2,1)S(1)}, u32[]{:S(2)}, u32[]{:S(2)}) %collective-permute-start.5) | collective-permute-done | bytes 655392 | tf_op jit(solution)/shard_map/ppermute | solution.py:252
  69.1 1.3 %collective-permute-start.8 = (bf16[4,320,128]{2,1,0:T(8,128)(2,1)S(1)}, bf16[4,320,128]{2,1,0:T(8,128)(2,1)S(1)}, u32[]{:S(2)}, u32[]{:S(2)}) collective-permute-start(bf16[4,320,128]{2,1,0:T(8,128)(2,1)S(1)} %broadcast_select_fusion), channel_id=1, source_target_pairs={{4,0},{6,2},{8,4},{10,6},{12,8},{14,10},{5,1},{7,3},{9,5},{11,7},{... | collective-permute-start | bytes 983048 | tf_op jit(solution)/shard_map/ppermute | solution.py:252
  70.5 1.4 %collective-permute-start.7 = (bf16[4,320,128]{2,1,0:T(8,128)(2,1)S(1)}, bf16[4,320,128]{2,1,0:T(8,128)(2,1)S(1)}, u32[]{:S(2)}, u32[]{:S(2)}) collective-permute-start(bf16[4,320,128]{2,1,0:T(8,128)(2,1)S(1)} %broadcast_select_fusion.1), channel_id=1, source_target_pairs={{4,0},{6,2},{8,4},{10,6},{12,8},{14,10},{5,1},{7,3},{9,5},{11,7},{... | collective-permute-start | bytes 983048 | tf_op jit(solution)/shard_map/ppermute | solution.py:252
  71.9 7.7 %shard_map.62 = (bf16[16,320,960]{2,1,0:T(8,128)(2,1)}, bf16[16,320,960]{2,1,0:T(8,128)(2,1)}) custom-call(bf16[8,320,128]{2,1,0:T(8,128)(2,1)S(1)} %get-tuple-element.35.refs_0_, bf16[320,384]{1,0:T(8,128)(2,1)S(1)} %get-tuple-element.36.refs_1_, ...), custom_call_target="tpu_custom_call", output_to_operand_aliasing={{0}: (5, {}), {1}: (6, {})} | custom-call | flops 838860800 | bytes 6553600 | tf_op jit(solution)/shard_map/pallas_call | solution.py:174
  79.7 6.2 %shard_map.63 = (bf16[16,320,960]{2,1,0:T(8,128)(2,1)}, bf16[16,320,960]{2,1,0:T(8,128)(2,1)}) custom-call(bf16[8,320,128]{2,1,0:T(8,128)(2,1)S(1)} %copy-done.2, bf16[320,384]{1,0:T(8,128)(2,1)S(1)} %get-tuple-element.33.refs_1_, bf16[8,320,128]{2,1,0:T(8,128)(2,1)S(1)} %copy-done.5, ...), custom_call_target="tpu_custom_call", output_to_operand_aliasing={{0}: (5, {}), {1}: (6, {})} | custom-call | flops 419430400 | bytes 3276800 | tf_op jit(solution)/shard_map/pallas_call | solution.py:174
  85.9 3.4 %shard_map.64 = (bf16[16,320,960]{2,1,0:T(8,128)(2,1)}, bf16[16,320,960]{2,1,0:T(8,128)(2,1)}) custom-call(bf16[8,320,128]{2,1,0:T(8,128)(2,1)S(1)} %get-tuple-element.35.refs_0_, bf16[320,384]{1,0:T(8,128)(2,1)S(1)} %get-tuple-element.33.refs_1_, ...), custom_call_target="tpu_custom_call", output_to_operand_aliasing={{0}: (4, {}), {1}: (5, {})} | custom-call | flops 209715200 | bytes 1638400 | tf_op jit(solution)/shard_map/pallas_call | solution.py:174
  89.4 3.4 %shard_map.65 = (bf16[16,320,960]{2,1,0:T(8,128)(2,1)}, bf16[16,320,960]{2,1,0:T(8,128)(2,1)}) custom-call(bf16[8,320,128]{2,1,0:T(8,128)(2,1)S(1)} %get-tuple-element.35.refs_0_, bf16[320,384]{1,0:T(8,128)(2,1)S(1)} %get-tuple-element.33.refs_1_, ...), custom_call_target="tpu_custom_call", output_to_operand_aliasing={{0}: (4, {}), {1}: (5, {})} | custom-call | flops 209715200 | bytes 1638400 | tf_op jit(solution)/shard_map/pallas_call | solution.py:174
  (33 shorter events, 5.7 us)
Async XLA Ops:
  1.4 1.7 %copy-start = (bf16[32,320,128]{2,1,0:T(8,128)(2,1)S(1)}, bf16[32,320,128]{2,1,0:T(8,128)(2,1)}, u32[]{:S(2)}) copy-start(bf16[32,320,128]{2,1,0:T(8,128)(2,1)} %samples_ref.1) | copy-start | bytes 7864324
  3.1 0.7 copy-start.8
  7.4 2.2 %collective-permute-start = (bf16[8,320,128]{2,1,0:T(8,128)(2,1)S(1)}, bf16[8,320,128]{2,1,0:T(8,128)(2,1)S(1)}, u32[]{:S(2)}, u32[]{:S(2)}) collective-permute-start(bf16[8,320,128]{2,1,0:T(8,128)(2,1)S(1)} %get-tuple-element.30), channel_id=1, source_target_pairs={{0,1},{1,0},{2,3},{3,2},{4,5},{5,4},{6,7},{7,6},{8,9},{9,8},{10,11... | collective-permute-start | bytes 1966088 | tf_op jit(solution)/shard_map/ppermute | solution.py:230
  11.1 23.6 %copy-start.1 = (bf16[8,320,128]{2,1,0:T(8,128)(2,1)}, bf16[8,320,128]{2,1,0:T(8,128)(2,1)S(1)}, u32[]{:S(2)}) copy-start(bf16[8,320,128]{2,1,0:T(8,128)(2,1)S(1)} %get-tuple-element.32.refs_0_) | copy-start | bytes 1966084
  11.1 19.2 %collective-permute-start.1 = (bf16[8,320,128]{2,1,0:T(8,128)(2,1)S(1)}, bf16[8,320,128]{2,1,0:T(8,128)(2,1)S(1)}, u32[]{:S(2)}, u32[]{:S(2)}) collective-permute-start(bf16[8,320,128]{2,1,0:T(8,128)(2,1)S(1)} %get-tuple-element.32.refs_0_), channel_id=1, source_target_pairs={{2,0},{6,4},{10,8},{14,12},{3,1},{7,5},{11,9},{15,13},{18,16},{22,... | collective-permute-start | bytes 1966088 | tf_op jit(solution)/shard_map/ppermute | solution.py:252
  12.4 20.0 %collective-permute-start.3 = (bf16[8,320,128]{2,1,0:T(8,128)(2,1)S(1)}, bf16[8,320,128]{2,1,0:T(8,128)(2,1)S(1)}, u32[]{:S(2)}, u32[]{:S(2)}) collective-permute-start(bf16[8,320,128]{2,1,0:T(8,128)(2,1)S(1)} %get-tuple-element.32.refs_0_), channel_id=1, source_target_pairs={{4,0},{6,2},{8,4},{10,6},{12,8},{14,10},{5,1},{7,3},{9,5},{11,7},{... | collective-permute-start | bytes 1966088 | tf_op jit(solution)/shard_map/ppermute | solution.py:252
  30.3 0.8 copy-start.9
  31.1 18.5 %collective-permute-start.2 = (bf16[8,320,128]{2,1,0:T(8,128)(2,1)S(1)}, bf16[8,320,128]{2,1,0:T(8,128)(2,1)S(1)}, u32[]{:S(2)}, u32[]{:S(2)}) collective-permute-start(bf16[8,320,128]{2,1,0:T(8,128)(2,1)S(1)} %get-tuple-element.35.refs_0_), channel_id=1, source_target_pairs={{4,0},{6,2},{8,4},{10,6},{12,8},{14,10},{5,1},{7,3},{9,5},{11,7},{... | collective-permute-start | bytes 1966088 | tf_op jit(solution)/shard_map/ppermute | solution.py:252
  32.4 18.7 %collective-permute-start.4 = (bf16[8,320,128]{2,1,0:T(8,128)(2,1)S(1)}, bf16[8,320,128]{2,1,0:T(8,128)(2,1)S(1)}, u32[]{:S(2)}, u32[]{:S(2)}) collective-permute-start(bf16[8,320,128]{2,1,0:T(8,128)(2,1)S(1)} %collective-permute-done.3.refs_4_.refs_2_), channel_id=1, source_target_pairs={{2,0},{6,4},{10,8},{14,12},{0,2},{4,6},{8,10},{12,14},{3,1},{7,5},... | collective-permute-start | bytes 1966088 | tf_op jit(solution)/shard_map/ppermute | solution.py:252
  34.7 0.8 copy-start.3
  49.6 16.5 %collective-permute-start.6 = (bf16[8,320,128]{2,1,0:T(8,128)(2,1)S(1)}, bf16[8,320,128]{2,1,0:T(8,128)(2,1)S(1)}, u32[]{:S(2)}, u32[]{:S(2)}) collective-permute-start(bf16[8,320,128]{2,1,0:T(8,128)(2,1)S(1)} %collective-permute-done.2.refs_4_.refs_2_), channel_id=1, source_target_pairs={{0,2},{4,6},{8,10},{12,14},{1,3},{5,7},{9,11},{13,15},{16,18},{20,... | collective-permute-start | bytes 1966088 | tf_op jit(solution)/shard_map/ppermute | solution.py:252
  51.1 0.9 copy-start.6
  52.0 17.0 %collective-permute-start.5 = (bf16[8,320,128]{2,1,0:T(8,128)(2,1)S(1)}, bf16[8,320,128]{2,1,0:T(8,128)(2,1)S(1)}, u32[]{:S(2)}, u32[]{:S(2)}) collective-permute-start(bf16[8,320,128]{2,1,0:T(8,128)(2,1)S(1)} %get-tuple-element.35.refs_0_), channel_id=1, source_target_pairs={{2,0},{6,4},{10,8},{14,12},{3,1},{7,5},{11,9},{15,13},{18,16},{22,... | collective-permute-start | bytes 1966088 | tf_op jit(solution)/shard_map/ppermute | solution.py:252
  53.3 26.4 %collective-permute-start.9 = (bf16[8,320,128]{2,1,0:T(8,128)(2,1)}, bf16[8,320,128]{2,1,0:T(8,128)(2,1)S(1)}, u32[]{:S(2)}, u32[]{:S(2)}) collective-permute-start(bf16[8,320,128]{2,1,0:T(8,128)(2,1)} %copy-done.6), channel_id=1, source_target_pairs={{6,2},{10,6},{14,10},{7,3},{11,7},{15,11},{22,18},{26,22},{30,26},... | collective-permute-start | bytes 1966088 | tf_op jit(solution)/shard_map/ppermute | solution.py:252
  54.0 1.1 %copy-start.2 = (bf16[8,320,128]{2,1,0:T(8,128)(2,1)S(1)}, bf16[8,320,128]{2,1,0:T(8,128)(2,1)}, u32[]{:S(2)}) copy-start(bf16[8,320,128]{2,1,0:T(8,128)(2,1)} %copy-done.1) | copy-start | bytes 1966084
  55.1 1.1 %copy-start.4 = (bf16[8,320,128]{2,1,0:T(8,128)(2,1)S(1)}, bf16[8,320,128]{2,1,0:T(8,128)(2,1)}, u32[]{:S(2)}) copy-start(bf16[8,320,128]{2,1,0:T(8,128)(2,1)} %copy-done.3) | copy-start | bytes 1966084
  56.2 1.1 %copy-start.7 = (bf16[8,320,128]{2,1,0:T(8,128)(2,1)S(1)}, bf16[8,320,128]{2,1,0:T(8,128)(2,1)}, u32[]{:S(2)}) copy-start(bf16[8,320,128]{2,1,0:T(8,128)(2,1)} %copy-done.6) | copy-start | bytes 1966084
  57.3 1.1 %copy-start.10 = (bf16[8,320,128]{2,1,0:T(8,128)(2,1)S(1)}, bf16[8,320,128]{2,1,0:T(8,128)(2,1)}, u32[]{:S(2)}) copy-start(bf16[8,320,128]{2,1,0:T(8,128)(2,1)} %copy-done.9) | copy-start | bytes 1966084
  69.1 16.8 %collective-permute-start.8 = (bf16[4,320,128]{2,1,0:T(8,128)(2,1)S(1)}, bf16[4,320,128]{2,1,0:T(8,128)(2,1)S(1)}, u32[]{:S(2)}, u32[]{:S(2)}) collective-permute-start(bf16[4,320,128]{2,1,0:T(8,128)(2,1)S(1)} %broadcast_select_fusion), channel_id=1, source_target_pairs={{4,0},{6,2},{8,4},{10,6},{12,8},{14,10},{5,1},{7,3},{9,5},{11,7},{... | collective-permute-start | bytes 983048 | tf_op jit(solution)/shard_map/ppermute | solution.py:252
  70.5 9.2 %copy-start.5 = (bf16[8,320,128]{2,1,0:T(8,128)(2,1)S(1)}, bf16[8,320,128]{2,1,0:T(8,128)(2,1)}, u32[]{:S(2)}) copy-start(bf16[8,320,128]{2,1,0:T(8,128)(2,1)} %copy-done.3) | copy-start | bytes 1966084
  70.5 18.9 %collective-permute-start.7 = (bf16[4,320,128]{2,1,0:T(8,128)(2,1)S(1)}, bf16[4,320,128]{2,1,0:T(8,128)(2,1)S(1)}, u32[]{:S(2)}, u32[]{:S(2)}) collective-permute-start(bf16[4,320,128]{2,1,0:T(8,128)(2,1)S(1)} %broadcast_select_fusion.1), channel_id=1, source_target_pairs={{4,0},{6,2},{8,4},{10,6},{12,8},{14,10},{5,1},{7,3},{9,5},{11,7},{... | collective-permute-start | bytes 983048 | tf_op jit(solution)/shard_map/ppermute | solution.py:252

commit v6 on v5

--- a/solution.py
+++ b/solution.py
@@ -15,6 +15,7 @@
 LANES = 128
 HOPS = 3
 ROWS = 64
+AT_ONCE = 1
 VMEM = 16 << 20
 
 
@@ -81,51 +82,66 @@
 
 
 def band_kernel(*refs, own_first, places, hops, first_tile, total_windows):
-    step = pl.program_id(0)
-    own_ref, mask_ref = refs[:2]
-    real_ref, imag_ref, right_ref, left_ref = refs[-4:]
-    _, block, depth = own_ref.shape
-    reach = min(HOPS * block - first_tile * LANES, real_ref.shape[2])
+    own_ref = refs[0]
+    real_ref, _, right_ref, _ = refs[-4:]
+    at_once, block, _ = real_ref.shape
+    depth = right_ref.shape[2]
+    start_bin = pl.program_id(0) * at_once
     origin = hops[0] * block
     filled = len(hops) * block
     parity = lax.rem(lax.axis_index("fiber"), 2)
-    own = own_ref[own_first + step]
-    if hops[0] == 0:
-        right_ref[:block] = own
-    if right_ref.shape[0] > filled:
-        right_ref[filled:] = jnp.zeros((right_ref.shape[0] - filled, depth), jnp.bfloat16)
 
     def gather(odd):
-        for hop, place in zip([hop for hop in hops if hop], places):
-            operand, first_bin = place[odd]
-            start = hop * block - origin
-            right_ref[start : start + block] = refs[operand][first_bin + step]
+        for inner in range(at_once):
+            for hop, place in zip([hop for hop in hops if hop], places):
+                operand, first_bin = place[odd]
+                start = hop * block - origin
+                right_ref[inner, start : start + block] = refs[operand][
+                    first_bin + start_bin + inner
+                ]
 
     pl.when(parity == 0)(lambda: gather(0))
     pl.when(parity == 1)(lambda: gather(1))
-
+    for inner in range(at_once):
+        own = own_ref[own_first + start_bin + inner]
+        if hops[0] == 0:
+            right_ref[inner, :block] = own
+        if right_ref.shape[1] > filled:
+            padding = (right_ref.shape[1] - filled, depth)
+            right_ref[inner, filled:] = jnp.zeros(padding, jnp.bfloat16)
+        one_bin(refs, own, inner, hops, first_tile, total_windows)
+
+
+def one_bin(refs, own, inner, hops, first_tile, total_windows):
+    mask_ref = refs[1]
+    real_ref, imag_ref, right_all, left_all = refs[-4:]
+    right_ref, left_ref = right_all.at[inner], left_all.at[inner]
+    block, depth = own.shape
+    reach = min(HOPS * block - first_tile * LANES, real_ref.shape[2])
+    origin = hops[0] * block
     wide = own.astype(jnp.float32) * (1.0 / math.sqrt(total_windows))
     part = depth // 4
     lane = lax.broadcasted_iota(jnp.int32, (block, depth), 1)
     turned = jnp.where(
         (lane // part) % 2 == 0, pltpu.roll(wide, depth - part, 1), -pltpu.roll(wide, part, 1)
     )
-    for group in range(block // ROWS):
-        rows = slice(group * ROWS, (group + 1) * ROWS)
-        left_ref[2 * group * ROWS : (2 * group + 1) * ROWS] = wide[rows].astype(jnp.bfloat16)
-        left_ref[(2 * group + 1) * ROWS : (2 * group + 2) * ROWS] = turned[rows].astype(jnp.bfloat16)
-    lane_of = lax.broadcasted_iota(jnp.int32, (ROWS, LANES), 1)
-    row_of = lax.broadcasted_iota(jnp.int32, (ROWS, LANES), 0)
+    for first in range(0, block, ROWS):
+        count = min(ROWS, block - first)
+        rows = slice(first, first + count)
+        left_ref[2 * first : 2 * first + count] = wide[rows].astype(jnp.bfloat16)
+        left_ref[2 * first + count : 2 * (first + count)] = turned[rows].astype(jnp.bfloat16)
     out_tiles = -(-reach // LANES)
     mask_from = 2 if first_tile == 0 else 0
-    for group in range(block // ROWS):
-        first = group * ROWS
+    for first in range(0, block, ROWS):
+        count = min(ROWS, block - first)
+        lane_of = lax.broadcasted_iota(jnp.int32, (count, LANES), 1)
+        row_of = lax.broadcasted_iota(jnp.int32, (count, LANES), 0)
         begin = first + 1 + first_tile * LANES - origin
         base = begin // LANES
         shift = begin - base * LANES + row_of
-        tiles = (begin + ROWS - 2 + reach) // LANES - base + 1
+        tiles = (begin + count - 2 + reach) // LANES - base + 1
         products = lax.dot_general(
-            left_ref[2 * first : 2 * first + 2 * ROWS],
+            left_ref[2 * first : 2 * (first + count)],
             right_ref[base * LANES : (base + tiles) * LANES],
             (((1,), (1,)), ((), ())),
             preferred_element_type=jnp.float32,
@@ -133,7 +149,7 @@
         keep = lane_of >= shift
         source = (lane_of + shift) % LANES
         for out_at, out_ref in enumerate((real_ref, imag_ref)):
-            rows = products[out_at * ROWS : (out_at + 1) * ROWS]
+            rows = products[out_at * count : (out_at + 1) * count]
             for tile in range(out_tiles):
                 start = tile * LANES
                 width = min(LANES, reach - start)
@@ -144,8 +160,8 @@
                 moved = moved.astype(jnp.bfloat16)
                 if tile >= mask_from:
                     column = (tile - mask_from) * LANES
-                    moved = moved * mask_ref[first : first + ROWS, column : column + LANES]
-                out_ref[0, first : first + ROWS, start : start + width] = moved[:, :width]
+                    moved = moved * mask_ref[first : first + count, column : column + LANES]
+                out_ref[inner, first : first + count, start : start + width] = moved[:, :width]
 
 
 def band(first_bin, bins, far, own, places, mask, so_far, bins_here, total_windows):
@@ -153,7 +169,9 @@
     out = jax.ShapeDtypeStruct((bins_here, block, HOPS * block), jnp.bfloat16)
     near_width = 2 * block
     hops = (2, 3) if far else (0, 1, 2)
-    out_spec = pl.BlockSpec((1, block, near_width), lambda i: (first_bin + i, 0, 1 if far else 0))
+    out_spec = pl.BlockSpec(
+        (AT_ONCE, block, near_width), lambda i: (first_bin // AT_ONCE + i, 0, 1 if far else 0)
+    )
     operands = [own[0], mask]
 
     def index_of(array):
@@ -180,12 +198,12 @@
             first_tile=near_width // LANES if far else 0,
             total_windows=total_windows,
         ),
-        grid=(bins,),
+        grid=(bins // AT_ONCE,),
         in_specs=in_specs,
         out_specs=[out_spec, out_spec],
         scratch_shapes=[
-            pltpu.VMEM((-(-len(hops) * block // LANES) * LANES, depth), jnp.bfloat16),
-            pltpu.VMEM((2 * block, depth), jnp.bfloat16),
+            pltpu.VMEM((AT_ONCE, -(-len(hops) * block // LANES) * LANES, depth), jnp.bfloat16),
+            pltpu.VMEM((AT_ONCE, 2 * block, depth), jnp.bfloat16),
         ],
         out_shape=[out, out],
         input_output_aliases=aliases,
@@ -259,38 +277,50 @@
     mask = (offsets[None, :] <= reach_limit[:, None]).astype(jnp.bfloat16)
     masks = (mask[:, 2 * LANES : near_reach], mask[:, near_reach:])
 
-    def near(outs, at, one, two):
+    def near(outs, chunk, one, two):
+        mine = (own[chunk // 2], chunk % 2 * quarter)
         return band(
-            at * half, half, 0, (own[at], 0), (one, two), masks[0], outs, bins_here, total_windows
-        )
-
-    def far(outs, at, first, bins, two, three):
+            chunk * quarter, quarter, 0, mine, (one, two), masks[0], outs, bins_here, total_windows
+        )
+
+    def far(outs, chunk, two, three):
+        mine = (own[chunk // 2], chunk % 2 * quarter)
         return band(
-            at * half + first, bins, 1, (own[at], first), (two, three), masks[1], outs, bins_here,
+            chunk * quarter, quarter, 1, mine, (two, three), masks[1], outs, bins_here,
             total_windows,
         )
 
+    def both(array, first=0):
+        return ((array, first), (array, first))
+
     ahead_low = send(own[0], to_even)
-    z_low = send(own[0], down)
-    own_high, ahead_low, *masks = after(own[1], ahead_low, *masks)
+    z_zero = send(own[0][:quarter], down)
+    z_payload, z_zero = after(own[0][quarter:], z_zero)
+    z_one = send(z_payload, down)
+    y_zero = send(z_zero, to_even + to_odd)
+    own_high, z_one, ahead_low, *masks = after(own[1], z_one, ahead_low, *masks)
     z_high = send(own_high, down)
-    y_low = send(z_low, to_even + to_odd)
-    up_high = send(z_high, to_odd)
-    own_high, y_low = after(own[1], y_low)
+    z_one, y_zero = after(z_one, y_zero)
+    y_one = send(z_one, to_even + to_odd)
+    outs = near(None, 0, ((ahead_low, 0), (y_zero, 0)), both(z_zero))
+    own_high, y_one = after(own[1], y_one)
     ahead_high = send(own_high, to_even)
-    z_next = send(y_low, down_odd)
-    outs = near(None, 0, ((ahead_low, 0), (y_low, 0)), ((z_low, 0), (z_low, 0)))
-    up_high, *outs = after(up_high, *outs)
-    last = [
-        send(pick(ahead_high[at : at + quarter], up_high[at : at + quarter]), down)
-        for at in (0, quarter)
-    ]
-    outs = near(outs, 1, ((ahead_high, 0), (up_high, 0)), ((z_high, 0), (z_high, 0)))
-    outs = far(outs, 0, 0, half, ((z_low, 0), (z_low, 0)), ((y_low, 0), (z_next, 0)))
-    for part, at in enumerate((0, quarter)):
-        outs = far(
-            outs, 1, at, quarter, ((z_high, at), (z_high, at)), ((last[part], 0), (last[part], 0))
-        )
+    outs = near(outs, 1, ((ahead_low, quarter), (y_one, 0)), both(z_one))
+    y_one, z_high, *outs = after(y_one, z_high, *outs)
+    up_two = send(z_high[:quarter], to_odd)
+    z_next = send(pick(z_zero, y_one), down)
+    z_three, up_two = after(z_high[quarter:], up_two)
+    up_three = send(z_three, to_odd)
+    last_two = send(pick(ahead_high[:quarter], up_two), down)
+    up_next = send(z_next, to_odd)
+    outs = near(outs, 2, ((ahead_high, 0), (up_two, 0)), both(z_high))
+    up_three, *outs = after(up_three, *outs)
+    last_three = send(pick(ahead_high[quarter:], up_three), down)
+    outs = far(outs, 1, both(z_one), ((y_one, 0), (z_next, 0)))
+    outs = near(outs, 3, ((ahead_high, quarter), (up_three, 0)), both(z_high, quarter))
+    outs = far(outs, 0, both(z_zero), ((y_zero, 0), (up_next, 0)))
+    outs = far(outs, 2, both(z_high), both(last_two))
+    outs = far(outs, 3, both(z_high, quarter), both(last_three))
     return tuple(outs)
 
 

time: 94.1 us -> 104 us (1.11)
  starting transfers between devices: 12.8 us -> 24.7 us
  local copies, waits for them, and re-layouts: 9.49 us -> 3.52 us
  Pallas kernels: 33.6 us -> 37.2 us
    ppermute x9 -> x13, starting transfers between devices: 12.3 us -> 24.1 us  [send(): return lax.ppermute(payload, 'fiber', route)]
    unnamed x22 -> x16, local copies, waits for them, and re-layouts: 9.35 us -> 2.48 us
    pallas_call x5 -> x8, Pallas kernels: 28.6 us -> 32.2 us  [band(): pl.pallas_call(functools.partial(band_kernel, own_first=own[1], places=pl...]
    ppermute x9 -> x13, waiting for transfers between devices: 32.7 us -> 32.7 us  [send(): return lax.ppermute(payload, 'fiber', route)]
  transfers between devices with their start and end apart: 10 -> 14, of which waited for: 4 -> 6; matrix products, arithmetic and copies ran while one was open for 1% -> 2% of each run, Pallas kernels for 27% -> 28%
where the time goes in v6:
time: 104 us; the launch traced here: 102 us
  Pallas kernels  37.2 us (36%)
  waiting for transfers between devices  34.5 us (33%)
  starting transfers between devices  24.7 us (24%)
  local copies, waits for them, and re-layouts  3.52 us (3%)
  between operations  1.49 us (1%)
  other arithmetic  1.06 us (1%)
    ppermute x13, waiting for transfers between devices, send(): return lax.ppermute(payload, 'fiber', route)  32.7 us
    pallas_call x8, Pallas kernels, band(): pl.pallas_call(functools.partial(band_kernel, own_first=own[1], places=pl...  32.2 us
    ppermute x13, starting transfers between devices, send(): return lax.ppermute(payload, 'fiber', route)  24.1 us
    pallas_call x1, Pallas kernels, body(): pl.pallas_call(spectra_kernel, in_specs=[pl.BlockSpec(memory_space=pltpu....  3.62 us
    unnamed x16, local copies, waits for them, and re-layouts  2.48 us
  transfers between devices with their start and end apart: 14, of which 6 were waited for; matrix products, arithmetic and copies ran while one was open for 2% of the time, Pallas kernels for 28%

profile of v6, /device:TPU:0, one launch (start us, length us, event | category | flops | bytes accessed | tf_op | source)
XLA Modules:
  0.0 102.4 jit_solution(9460592425488148540)
XLA Ops:
  1.4 1.7 %copy-done.2 = bf16[32,320,128]{2,1,0:T(8,128)(2,1)S(1)} copy-done((bf16[32,320,128]{2,1,0:T(8,128)(2,1)S(1)}, bf16[32,320,128]{2,1,0:T(8,128)(2,1)}, u32[]{:S(2)}) %copy-start.2) | copy-done | bytes 2621464
  3.8 3.6 %shard_map.59 = (bf16[8,320,128]{2,1,0:T(8,128)(2,1)S(1)}, bf16[8,320,128]{2,1,0:T(8,128)(2,1)S(1)}) custom-call(s32[2]{0:T(128)S(1)} %pad_add_fusion.place_ref, bf16[32,320,128]{2,1,0:T(8,128)(2,1)S(1)} %copy-done.2, bf16[64,128]{1,0:T(8,128)(2,1)S(1)} %copy-done.7), custom_call_target="tpu_custom_call" | custom-call | tf_op jit(solution)/shard_map/pallas_call | solution.py:230
  8.0 1.7 %collective-permute-done.theirs_ref = bf16[8,320,128]{2,1,0:T(8,128)(2,1)S(1)} collective-permute-done((bf16[8,320,128]{2,1,0:T(8,128)(2,1)S(1)}, bf16[8,320,128]{2,1,0:T(8,128)(2,1)S(1)}, u32[]{:S(2)}, u32[]{:S(2)}) %collective-permute-start) | collective-permute-done | bytes 655392 | tf_op jit(solution)/shard_map/ppermute | solution.py:248
  9.7 1.4 %shard_map.60 = (bf16[8,320,128]{2,1,0:T(8,128)(2,1)S(1)}, bf16[8,320,128]{2,1,0:T(8,128)(2,1)S(1)}) custom-call(bf16[8,320,128]{2,1,0:T(8,128)(2,1)S(1)} %get-tuple-element.49.mine_ref, bf16[8,320,128]{2,1,0:T(8,128)(2,1)S(1)} %collective-permute-done.theirs_ref), custom_call_target="tpu_custom_call" | custom-call | tf_op jit(solution)/shard_map/pallas_call | solution.py:252
  11.1 1.3 %collective-permute-start.1 = (bf16[4,320,128]{2,1,0:T(8,128)(2,1)S(1)}, bf16[4,320,128]{2,1,0:T(8,128)(2,1)S(1)}, u32[]{:S(2)}, u32[]{:S(2)}) collective-permute-start(bf16[4,320,128]{2,1,0:T(8,128)(2,1)S(1)} %get-tuple-element.102), channel_id=1, source_target_pairs={{4,0},{6,2},{8,4},{10,6},{12,8},{14,10},{5,1},{7,3},{9,5},{11,7},{... | collective-permute-start | bytes 983048 | tf_op jit(solution)/shard_map/ppermute | solution.py:270
  12.4 1.3 %collective-permute-start.3 = (bf16[8,320,128]{2,1,0:T(8,128)(2,1)S(1)}, bf16[8,320,128]{2,1,0:T(8,128)(2,1)S(1)}, u32[]{:S(2)}, u32[]{:S(2)}) collective-permute-start(bf16[8,320,128]{2,1,0:T(8,128)(2,1)S(1)} %get-tuple-element.52.refs_0_), channel_id=1, source_target_pairs={{2,0},{6,4},{10,8},{14,12},{3,1},{7,5},{11,9},{15,13},{18,16},{22,... | collective-permute-start | bytes 1966088 | tf_op jit(solution)/shard_map/ppermute | solution.py:270
  13.7 10.2 %collective-permute-done.1.refs_4_.refs_2_ = bf16[4,320,128]{2,1,0:T(8,128)(2,1)S(1)} collective-permute-done((bf16[4,320,128]{2,1,0:T(8,128)(2,1)S(1)}, bf16[4,320,128]{2,1,0:T(8,128)(2,1)S(1)}, u32[]{:S(2)}, u32[]{:S(2)}) %collective-permute-start.1) | collective-permute-done | bytes 327712 | tf_op jit(solution)/shard_map/ppermute | solution.py:270
  26.1 1.7 %collective-permute-start.4 = (bf16[4,320,128]{2,1,0:T(8,128)(2,1)S(1)}, bf16[4,320,128]{2,1,0:T(8,128)(2,1)S(1)}, u32[]{:S(2)}, u32[]{:S(2)}) collective-permute-start(bf16[4,320,128]{2,1,0:T(8,128)(2,1)S(1)} %collective-permute-done.1.refs_4_.refs_2_), channel_id=1, source_target_pairs={{2,0},{6,4},{10,8},{14,12},{0,2},{4,6},{8,10},{12,14},{3,1},{7,5},... | collective-permute-start | bytes 983048 | tf_op jit(solution)/shard_map/ppermute | solution.py:270
  27.9 7.2 %collective-permute-done.2.refs_4_.refs_2_ = bf16[4,320,128]{2,1,0:T(8,128)(2,1)S(1)} collective-permute-done((bf16[4,320,128]{2,1,0:T(8,128)(2,1)S(1)}, bf16[4,320,128]{2,1,0:T(8,128)(2,1)S(1)}, u32[]{:S(2)}, u32[]{:S(2)}) %collective-permute-start.2) | collective-permute-done | bytes 327712 | tf_op jit(solution)/shard_map/ppermute | solution.py:270
  36.4 2.2 %collective-permute-done.4.refs_3_ = bf16[4,320,128]{2,1,0:T(8,128)(2,1)S(1)} collective-permute-done((bf16[4,320,128]{2,1,0:T(8,128)(2,1)S(1)}, bf16[4,320,128]{2,1,0:T(8,128)(2,1)S(1)}, u32[]{:S(2)}, u32[]{:S(2)}) %collective-permute-start.4) | collective-permute-done | bytes 327712 | tf_op jit(solution)/shard_map/ppermute | solution.py:270
  38.7 9.2 %collective-permute-done.5.refs_3_ = bf16[4,320,128]{2,1,0:T(8,128)(2,1)S(1)} collective-permute-done((bf16[4,320,128]{2,1,0:T(8,128)(2,1)S(1)}, bf16[4,320,128]{2,1,0:T(8,128)(2,1)S(1)}, u32[]{:S(2)}, u32[]{:S(2)}) %collective-permute-start.5) | collective-permute-done | bytes 327712 | tf_op jit(solution)/shard_map/ppermute | solution.py:270
  49.2 4.3 %shard_map.61 = (bf16[16,320,960]{2,1,0:T(8,128)(2,1)}, bf16[16,320,960]{2,1,0:T(8,128)(2,1)}) custom-call(bf16[8,320,128]{2,1,0:T(8,128)(2,1)S(1)} %get-tuple-element.52.refs_0_, bf16[320,384]{1,0:T(8,128)(2,1)S(1)} %get-tuple-element.60.refs_1_, bf16[8,320,128]{2,1,0:T(8,128)(2,1)S(1)} %collective-permute-done.3.refs_2_, ...), custom_call_target="tpu_custom_call" | custom-call | flops 419430400 | bytes 3276800 | tf_op jit(solution)/shard_map/pallas_call | solution.py:192
  53.5 4.3 %shard_map.62 = (bf16[16,320,960]{2,1,0:T(8,128)(2,1)}, bf16[16,320,960]{2,1,0:T(8,128)(2,1)}) custom-call(bf16[8,320,128]{2,1,0:T(8,128)(2,1)S(1)} %get-tuple-element.52.refs_0_, bf16[320,384]{1,0:T(8,128)(2,1)S(1)} %get-tuple-element.60.refs_1_, ...), custom_call_target="tpu_custom_call", output_to_operand_aliasing={{0}: (5, {}), {1}: (6, {})} | custom-call | flops 419430400 | bytes 3276800 | tf_op jit(solution)/shard_map/pallas_call | solution.py:192
  58.7 5.3 %collective-permute-start.8 = (bf16[4,320,128]{2,1,0:T(8,128)(2,1)}, bf16[4,320,128]{2,1,0:T(8,128)(2,1)}, u32[]{:S(2)}, u32[]{:S(2)}) collective-permute-start(bf16[4,320,128]{2,1,0:T(8,128)(2,1)} %get-tuple-element.98), channel_id=1, source_target_pairs={{0,2},{4,6},{8,10},{12,14},{1,3},{5,7},{9,11},{13,15},{16,18},{20,... | collective-permute-start | bytes 983048 | tf_op jit(solution)/shard_map/ppermute | solution.py:270
  65.4 3.8 %collective-permute-done.8.refs_3_ = bf16[4,320,128]{2,1,0:T(8,128)(2,1)} collective-permute-done((bf16[4,320,128]{2,1,0:T(8,128)(2,1)}, bf16[4,320,128]{2,1,0:T(8,128)(2,1)}, u32[]{:S(2)}, u32[]{:S(2)}) %collective-permute-start.8) | collective-permute-done | bytes 327712 | tf_op jit(solution)/shard_map/ppermute | solution.py:270
  69.2 4.4 %collective-permute-start.9 = (bf16[4,320,128]{2,1,0:T(8,128)(2,1)}, bf16[4,320,128]{2,1,0:T(8,128)(2,1)S(1)}, u32[]{:S(2)}, u32[]{:S(2)}) collective-permute-start(bf16[4,320,128]{2,1,0:T(8,128)(2,1)} %get-tuple-element.69), channel_id=1, source_target_pairs={{0,2},{4,6},{8,10},{12,14},{1,3},{5,7},{9,11},{13,15},{16,18},{20,... | collective-permute-start | bytes 983048 | tf_op jit(solution)/shard_map/ppermute | solution.py:270
  73.7 1.4 %collective-permute-start.11 = (bf16[4,320,128]{2,1,0:T(8,128)(2,1)S(1)}, bf16[4,320,128]{2,1,0:T(8,128)(2,1)S(1)}, u32[]{:S(2)}, u32[]{:S(2)}) collective-permute-start(bf16[4,320,128]{2,1,0:T(8,128)(2,1)S(1)} %broadcast_select_fusion.1), channel_id=1, source_target_pairs={{4,0},{6,2},{8,4},{10,6},{12,8},{14,10},{5,1},{7,3},{9,5},{11,7},{... | collective-permute-start | bytes 983048 | tf_op jit(solution)/shard_map/ppermute | solution.py:270
  75.2 2.3 %collective-permute-start.13 = (bf16[4,320,128]{2,1,0:T(8,128)(2,1)S(1)}, bf16[4,320,128]{2,1,0:T(8,128)(2,1)S(1)}, u32[]{:S(2)}, u32[]{:S(2)}) collective-permute-start(bf16[4,320,128]{2,1,0:T(8,128)(2,1)S(1)} %collective-permute-done.12.refs_4_), channel_id=1, source_target_pairs={{0,2},{4,6},{8,10},{12,14},{1,3},{5,7},{9,11},{13,15},{16,18},{20,... | collective-permute-start | bytes 983048 | tf_op jit(solution)/shard_map/ppermute | solution.py:270
  77.4 5.3 %shard_map.63 = (bf16[16,320,960]{2,1,0:T(8,128)(2,1)}, bf16[16,320,960]{2,1,0:T(8,128)(2,1)}) custom-call(bf16[8,320,128]{2,1,0:T(8,128)(2,1)S(1)} %get-tuple-element.68.refs_0_, bf16[320,384]{1,0:T(8,128)(2,1)S(1)} %get-tuple-element.60.refs_1_, ...), custom_call_target="tpu_custom_call", output_to_operand_aliasing={{0}: (5, {}), {1}: (6, {})} | custom-call | flops 419430400 | bytes 3276800 | tf_op jit(solution)/shard_map/pallas_call | solution.py:192
  84.1 3.5 %shard_map.64 = (bf16[16,320,960]{2,1,0:T(8,128)(2,1)}, bf16[16,320,960]{2,1,0:T(8,128)(2,1)}) custom-call(bf16[8,320,128]{2,1,0:T(8,128)(2,1)S(1)} %get-tuple-element.52.refs_0_, bf16[320,384]{1,0:T(8,128)(2,1)S(1)} %get-tuple-element.54.refs_1_, bf16[4,320,128]{2,1,0:T(8,128)(2,1)S(1)} %copy-done.6, ...), custom_call_target="tpu_custom_call", output_to_operand_aliasing={{0}: (5, {}), {1}: (6, {})} | custom-call | flops 209715200 | bytes 1638400 | tf_op jit(solution)/shard_map/pallas_call | solution.py:192
  87.6 4.3 %shard_map.65 = (bf16[16,320,960]{2,1,0:T(8,128)(2,1)}, bf16[16,320,960]{2,1,0:T(8,128)(2,1)}) custom-call(bf16[8,320,128]{2,1,0:T(8,128)(2,1)S(1)} %get-tuple-element.68.refs_0_, bf16[320,384]{1,0:T(8,128)(2,1)S(1)} %get-tuple-element.60.refs_1_, ...), custom_call_target="tpu_custom_call", output_to_operand_aliasing={{0}: (5, {}), {1}: (6, {})} | custom-call | flops 419430400 | bytes 3276800 | tf_op jit(solution)/shard_map/pallas_call | solution.py:192
  91.9 3.5 %shard_map.66 = (bf16[16,320,960]{2,1,0:T(8,128)(2,1)}, bf16[16,320,960]{2,1,0:T(8,128)(2,1)}) custom-call(bf16[8,320,128]{2,1,0:T(8,128)(2,1)S(1)} %get-tuple-element.52.refs_0_, bf16[320,384]{1,0:T(8,128)(2,1)S(1)} %get-tuple-element.54.refs_1_, ...), custom_call_target="tpu_custom_call", output_to_operand_aliasing={{0}: (5, {}), {1}: (6, {})} | custom-call | flops 209715200 | bytes 1638400 | tf_op jit(solution)/shard_map/pallas_call | solution.py:192
  95.4 3.5 %shard_map.67 = (bf16[16,320,960]{2,1,0:T(8,128)(2,1)}, bf16[16,320,960]{2,1,0:T(8,128)(2,1)}) custom-call(bf16[8,320,128]{2,1,0:T(8,128)(2,1)S(1)} %get-tuple-element.68.refs_0_, bf16[320,384]{1,0:T(8,128)(2,1)S(1)} %get-tuple-element.54.refs_1_, ...), custom_call_target="tpu_custom_call", output_to_operand_aliasing={{0}: (4, {}), {1}: (5, {})} | custom-call | flops 209715200 | bytes 1638400 | tf_op jit(solution)/shard_map/pallas_call | solution.py:192
  98.9 3.5 %shard_map.68 = (bf16[16,320,960]{2,1,0:T(8,128)(2,1)}, bf16[16,320,960]{2,1,0:T(8,128)(2,1)}) custom-call(bf16[8,320,128]{2,1,0:T(8,128)(2,1)S(1)} %get-tuple-element.68.refs_0_, bf16[320,384]{1,0:T(8,128)(2,1)S(1)} %get-tuple-element.54.refs_1_, ...), custom_call_target="tpu_custom_call", output_to_operand_aliasing={{0}: (4, {}), {1}: (5, {})} | custom-call | flops 209715200 | bytes 1638400 | tf_op jit(solution)/shard_map/pallas_call | solution.py:192
  (40 shorter events, 9.8 us)
Async XLA Ops:
  1.4 1.7 %copy-start.2 = (bf16[32,320,128]{2,1,0:T(8,128)(2,1)S(1)}, bf16[32,320,128]{2,1,0:T(8,128)(2,1)}, u32[]{:S(2)}) copy-start(bf16[32,320,128]{2,1,0:T(8,128)(2,1)} %samples_ref.1) | copy-start | bytes 7864324
  3.1 0.7 copy-start.7
  7.4 2.2 %collective-permute-start = (bf16[8,320,128]{2,1,0:T(8,128)(2,1)S(1)}, bf16[8,320,128]{2,1,0:T(8,128)(2,1)S(1)}, u32[]{:S(2)}, u32[]{:S(2)}) collective-permute-start(bf16[8,320,128]{2,1,0:T(8,128)(2,1)S(1)} %get-tuple-element.50), channel_id=1, source_target_pairs={{0,1},{1,0},{2,3},{3,2},{4,5},{5,4},{6,7},{7,6},{8,9},{9,8},{10,11... | collective-permute-start | bytes 1966088 | tf_op jit(solution)/shard_map/ppermute | solution.py:248
  11.1 12.9 %collective-permute-start.1 = (bf16[4,320,128]{2,1,0:T(8,128)(2,1)S(1)}, bf16[4,320,128]{2,1,0:T(8,128)(2,1)S(1)}, u32[]{:S(2)}, u32[]{:S(2)}) collective-permute-start(bf16[4,320,128]{2,1,0:T(8,128)(2,1)S(1)} %get-tuple-element.102), channel_id=1, source_target_pairs={{4,0},{6,2},{8,4},{10,6},{12,8},{14,10},{5,1},{7,3},{9,5},{11,7},{... | collective-permute-start | bytes 983048 | tf_op jit(solution)/shard_map/ppermute | solution.py:270
  12.4 22.7 %collective-permute-start.3 = (bf16[8,320,128]{2,1,0:T(8,128)(2,1)S(1)}, bf16[8,320,128]{2,1,0:T(8,128)(2,1)S(1)}, u32[]{:S(2)}, u32[]{:S(2)}) collective-permute-start(bf16[8,320,128]{2,1,0:T(8,128)(2,1)S(1)} %get-tuple-element.52.refs_0_), channel_id=1, source_target_pairs={{2,0},{6,4},{10,8},{14,12},{3,1},{7,5},{11,9},{15,13},{18,16},{22,... | collective-permute-start | bytes 1966088 | tf_op jit(solution)/shard_map/ppermute | solution.py:270
  24.0 11.1 %collective-permute-start.2 = (bf16[4,320,128]{2,1,0:T(8,128)(2,1)S(1)}, bf16[4,320,128]{2,1,0:T(8,128)(2,1)S(1)}, u32[]{:S(2)}, u32[]{:S(2)}) collective-permute-start(bf16[4,320,128]{2,1,0:T(8,128)(2,1)S(1)} %get-tuple-element.53), channel_id=1, source_target_pairs={{4,0},{6,2},{8,4},{10,6},{12,8},{14,10},{5,1},{7,3},{9,5},{11,7},{... | collective-permute-start | bytes 983048 | tf_op jit(solution)/shard_map/ppermute | solution.py:270
  26.1 12.5 %collective-permute-start.4 = (bf16[4,320,128]{2,1,0:T(8,128)(2,1)S(1)}, bf16[4,320,128]{2,1,0:T(8,128)(2,1)S(1)}, u32[]{:S(2)}, u32[]{:S(2)}) collective-permute-start(bf16[4,320,128]{2,1,0:T(8,128)(2,1)S(1)} %collective-permute-done.1.refs_4_.refs_2_), channel_id=1, source_target_pairs={{2,0},{6,4},{10,8},{14,12},{0,2},{4,6},{8,10},{12,14},{3,1},{7,5},... | collective-permute-start | bytes 983048 | tf_op jit(solution)/shard_map/ppermute | solution.py:270
  35.1 22.7 %copy-start.5 = (bf16[4,320,128]{2,1,0:T(8,128)(2,1)}, bf16[4,320,128]{2,1,0:T(8,128)(2,1)S(1)}, u32[]{:S(2)}) copy-start(bf16[4,320,128]{2,1,0:T(8,128)(2,1)S(1)} %collective-permute-done.2.refs_4_.refs_2_) | copy-start | bytes 983044
  35.1 22.7 %collective-permute-start.6 = (bf16[8,320,128]{2,1,0:T(8,128)(2,1)S(1)}, bf16[8,320,128]{2,1,0:T(8,128)(2,1)S(1)}, u32[]{:S(2)}, u32[]{:S(2)}) collective-permute-start(bf16[8,320,128]{2,1,0:T(8,128)(2,1)S(1)} %get-tuple-element.68.refs_0_), channel_id=1, source_target_pairs={{4,0},{6,2},{8,4},{10,6},{12,8},{14,10},{5,1},{7,3},{9,5},{11,7},{... | collective-permute-start | bytes 1966088 | tf_op jit(solution)/shard_map/ppermute | solution.py:270
  38.6 19.2 %copy-start.3 = (bf16[4,320,128]{2,1,0:T(8,128)(2,1)}, bf16[4,320,128]{2,1,0:T(8,128)(2,1)S(1)}, u32[]{:S(2)}) copy-start(bf16[4,320,128]{2,1,0:T(8,128)(2,1)S(1)} %collective-permute-done.4.refs_3_) | copy-start | bytes 983044
  38.6 9.2 %collective-permute-start.5 = (bf16[4,320,128]{2,1,0:T(8,128)(2,1)S(1)}, bf16[4,320,128]{2,1,0:T(8,128)(2,1)S(1)}, u32[]{:S(2)}, u32[]{:S(2)}) collective-permute-start(bf16[4,320,128]{2,1,0:T(8,128)(2,1)S(1)} %collective-permute-done.2.refs_4_.refs_2_), channel_id=1, source_target_pairs={{2,0},{6,4},{10,8},{14,12},{0,2},{4,6},{8,10},{12,14},{3,1},{7,5},... | collective-permute-start | bytes 983048 | tf_op jit(solution)/shard_map/ppermute | solution.py:270
  47.9 9.9 %copy-start = (bf16[4,320,128]{2,1,0:T(8,128)(2,1)}, bf16[4,320,128]{2,1,0:T(8,128)(2,1)S(1)}, u32[]{:S(2)}) copy-start(bf16[4,320,128]{2,1,0:T(8,128)(2,1)S(1)} %collective-permute-done.5.refs_3_) | copy-start | bytes 983044
  47.9 25.7 %collective-permute-start.7 = (bf16[8,320,128]{2,1,0:T(8,128)(2,1)S(1)}, bf16[8,320,128]{2,1,0:T(8,128)(2,1)S(1)}, u32[]{:S(2)}, u32[]{:S(2)}) collective-permute-start(bf16[8,320,128]{2,1,0:T(8,128)(2,1)S(1)} %get-tuple-element.68.refs_0_), channel_id=1, source_target_pairs={{2,0},{6,4},{10,8},{14,12},{3,1},{7,5},{11,9},{15,13},{18,16},{22,... | collective-permute-start | bytes 1966088 | tf_op jit(solution)/shard_map/ppermute | solution.py:270
  58.7 10.5 %collective-permute-start.8 = (bf16[4,320,128]{2,1,0:T(8,128)(2,1)}, bf16[4,320,128]{2,1,0:T(8,128)(2,1)}, u32[]{:S(2)}, u32[]{:S(2)}) collective-permute-start(bf16[4,320,128]{2,1,0:T(8,128)(2,1)} %get-tuple-element.98), channel_id=1, source_target_pairs={{0,2},{4,6},{8,10},{12,14},{1,3},{5,7},{9,11},{13,15},{16,18},{20,... | collective-permute-start | bytes 983048 | tf_op jit(solution)/shard_map/ppermute | solution.py:270
  64.1 11.1 %collective-permute-start.12 = (bf16[4,320,128]{2,1,0:T(8,128)(2,1)S(1)}, bf16[4,320,128]{2,1,0:T(8,128)(2,1)S(1)}, u32[]{:S(2)}, u32[]{:S(2)}) collective-permute-start(bf16[4,320,128]{2,1,0:T(8,128)(2,1)S(1)} %broadcast_select_fusion), channel_id=1, source_target_pairs={{4,0},{6,2},{8,4},{10,6},{12,8},{14,10},{5,1},{7,3},{9,5},{11,7},{... | collective-permute-start | bytes 983048 | tf_op jit(solution)/shard_map/ppermute | solution.py:270
  69.2 13.6 %collective-permute-start.9 = (bf16[4,320,128]{2,1,0:T(8,128)(2,1)}, bf16[4,320,128]{2,1,0:T(8,128)(2,1)S(1)}, u32[]{:S(2)}, u32[]{:S(2)}) collective-permute-start(bf16[4,320,128]{2,1,0:T(8,128)(2,1)} %get-tuple-element.69), channel_id=1, source_target_pairs={{0,2},{4,6},{8,10},{12,14},{1,3},{5,7},{9,11},{13,15},{16,18},{20,... | collective-permute-start | bytes 983048 | tf_op jit(solution)/shard_map/ppermute | solution.py:270
  73.7 10.4 %copy-start.1 = (bf16[4,320,128]{2,1,0:T(8,128)(2,1)S(1)}, bf16[4,320,128]{2,1,0:T(8,128)(2,1)}, u32[]{:S(2)}) copy-start(bf16[4,320,128]{2,1,0:T(8,128)(2,1)} %copy-done) | copy-start | bytes 983044
  73.7 10.4 %copy-start.6 = (bf16[4,320,128]{2,1,0:T(8,128)(2,1)S(1)}, bf16[4,320,128]{2,1,0:T(8,128)(2,1)}, u32[]{:S(2)}) copy-start(bf16[4,320,128]{2,1,0:T(8,128)(2,1)} %copy-done.5) | copy-start | bytes 983044
  73.7 21.7 %collective-permute-start.11 = (bf16[4,320,128]{2,1,0:T(8,128)(2,1)S(1)}, bf16[4,320,128]{2,1,0:T(8,128)(2,1)S(1)}, u32[]{:S(2)}, u32[]{:S(2)}) collective-permute-start(bf16[4,320,128]{2,1,0:T(8,128)(2,1)S(1)} %broadcast_select_fusion.1), channel_id=1, source_target_pairs={{4,0},{6,2},{8,4},{10,6},{12,8},{14,10},{5,1},{7,3},{9,5},{11,7},{... | collective-permute-start | bytes 983048 | tf_op jit(solution)/shard_map/ppermute | solution.py:270
  75.2 16.8 %collective-permute-start.13 = (bf16[4,320,128]{2,1,0:T(8,128)(2,1)S(1)}, bf16[4,320,128]{2,1,0:T(8,128)(2,1)S(1)}, u32[]{:S(2)}, u32[]{:S(2)}) collective-permute-start(bf16[4,320,128]{2,1,0:T(8,128)(2,1)S(1)} %collective-permute-done.12.refs_4_), channel_id=1, source_target_pairs={{0,2},{4,6},{8,10},{12,14},{1,3},{5,7},{9,11},{13,15},{16,18},{20,... | collective-permute-start | bytes 983048 | tf_op jit(solution)/shard_map/ppermute | solution.py:270
  82.8 16.1 %collective-permute-start.10 = (bf16[4,320,128]{2,1,0:T(8,128)(2,1)S(1)}, bf16[4,320,128]{2,1,0:T(8,128)(2,1)S(1)}, u32[]{:S(2)}, u32[]{:S(2)}) collective-permute-start(bf16[4,320,128]{2,1,0:T(8,128)(2,1)S(1)} %broadcast_select_fusion.2), channel_id=1, source_target_pairs={{4,0},{6,2},{8,4},{10,6},{12,8},{14,10},{5,1},{7,3},{9,5},{11,7},{... | collective-permute-start | bytes 983048 | tf_op jit(solution)/shard_map/ppermute | solution.py:270
  87.6 4.3 %copy-start.4 = (bf16[4,320,128]{2,1,0:T(8,128)(2,1)S(1)}, bf16[4,320,128]{2,1,0:T(8,128)(2,1)}, u32[]{:S(2)}) copy-start(bf16[4,320,128]{2,1,0:T(8,128)(2,1)} %copy-done.3) | copy-start | bytes 983044

commit v7 on v6

--- a/solution.py
+++ b/solution.py
@@ -15,7 +15,7 @@
 LANES = 128
 HOPS = 3
 ROWS = 64
-AT_ONCE = 1
+AT_ONCE = 2
 VMEM = 16 << 20
 
 
@@ -277,50 +277,38 @@
     mask = (offsets[None, :] <= reach_limit[:, None]).astype(jnp.bfloat16)
     masks = (mask[:, 2 * LANES : near_reach], mask[:, near_reach:])
 
-    def near(outs, chunk, one, two):
-        mine = (own[chunk // 2], chunk % 2 * quarter)
+    def near(outs, at, one, two):
         return band(
-            chunk * quarter, quarter, 0, mine, (one, two), masks[0], outs, bins_here, total_windows
-        )
-
-    def far(outs, chunk, two, three):
-        mine = (own[chunk // 2], chunk % 2 * quarter)
+            at * half, half, 0, (own[at], 0), (one, two), masks[0], outs, bins_here, total_windows
+        )
+
+    def far(outs, at, first, bins, two, three):
         return band(
-            chunk * quarter, quarter, 1, mine, (two, three), masks[1], outs, bins_here,
+            at * half + first, bins, 1, (own[at], first), (two, three), masks[1], outs, bins_here,
             total_windows,
         )
 
-    def both(array, first=0):
-        return ((array, first), (array, first))
-
     ahead_low = send(own[0], to_even)
-    z_zero = send(own[0][:quarter], down)
-    z_payload, z_zero = after(own[0][quarter:], z_zero)
-    z_one = send(z_payload, down)
-    y_zero = send(z_zero, to_even + to_odd)
-    own_high, z_one, ahead_low, *masks = after(own[1], z_one, ahead_low, *masks)
+    z_low = send(own[0], down)
+    own_high, ahead_low, *masks = after(own[1], ahead_low, *masks)
     z_high = send(own_high, down)
-    z_one, y_zero = after(z_one, y_zero)
-    y_one = send(z_one, to_even + to_odd)
-    outs = near(None, 0, ((ahead_low, 0), (y_zero, 0)), both(z_zero))
-    own_high, y_one = after(own[1], y_one)
+    y_low = send(z_low, to_even + to_odd)
+    up_high = send(z_high, to_odd)
+    own_high, y_low = after(own[1], y_low)
     ahead_high = send(own_high, to_even)
-    outs = near(outs, 1, ((ahead_low, quarter), (y_one, 0)), both(z_one))
-    y_one, z_high, *outs = after(y_one, z_high, *outs)
-    up_two = send(z_high[:quarter], to_odd)
-    z_next = send(pick(z_zero, y_one), down)
-    z_three, up_two = after(z_high[quarter:], up_two)
-    up_three = send(z_three, to_odd)
-    last_two = send(pick(ahead_high[:quarter], up_two), down)
-    up_next = send(z_next, to_odd)
-    outs = near(outs, 2, ((ahead_high, 0), (up_two, 0)), both(z_high))
-    up_three, *outs = after(up_three, *outs)
-    last_three = send(pick(ahead_high[quarter:], up_three), down)
-    outs = far(outs, 1, both(z_one), ((y_one, 0), (z_next, 0)))
-    outs = near(outs, 3, ((ahead_high, quarter), (up_three, 0)), both(z_high, quarter))
-    outs = far(outs, 0, both(z_zero), ((y_zero, 0), (up_next, 0)))
-    outs = far(outs, 2, both(z_high), both(last_two))
-    outs = far(outs, 3, both(z_high, quarter), both(last_three))
+    z_next = send(y_low, down_odd)
+    outs = near(None, 0, ((ahead_low, 0), (y_low, 0)), ((z_low, 0), (z_low, 0)))
+    up_high, *outs = after(up_high, *outs)
+    last = [
+        send(pick(ahead_high[at : at + quarter], up_high[at : at + quarter]), down)
+        for at in (0, quarter)
+    ]
+    outs = near(outs, 1, ((ahead_high, 0), (up_high, 0)), ((z_high, 0), (z_high, 0)))
+    outs = far(outs, 0, 0, half, ((z_low, 0), (z_low, 0)), ((y_low, 0), (z_next, 0)))
+    for part, at in enumerate((0, quarter)):
+        outs = far(
+            outs, 1, at, quarter, ((z_high, at), (z_high, at)), ((last[part], 0), (last[part], 0))
+        )
     return tuple(outs)
 
 

time: 104 us -> 90.5 us (0.87)
  starting transfers between devices: 24.7 us -> 12.8 us
  Pallas kernels: 37.2 us -> 28.9 us
  local copies, waits for them, and re-layouts: 3.52 us -> 9.49 us
  waiting for transfers between devices: 34.5 us -> 35.6 us
    ppermute x13 -> x9, starting transfers between devices: 24.1 us -> 12.3 us  [send(): return lax.ppermute(payload, 'fiber', route)]
    pallas_call x8 -> x5, Pallas kernels: 32.2 us -> 23.9 us  [band(): pl.pallas_call(functools.partial(band_kernel, own_first=own[1], places=pl...]
    unnamed x16 -> x22, local copies, waits for them, and re-layouts: 2.48 us -> 9.35 us
    ppermute x13 -> x9, waiting for transfers between devices: 32.7 us -> 33.9 us  [send(): return lax.ppermute(payload, 'fiber', route)]
  transfers between devices with their start and end apart: 14 -> 10, of which waited for: 6 -> 4; matrix products, arithmetic and copies ran while one was open for 2% -> 1% of each run, Pallas kernels for 28% -> 23%
where the time goes in v7:
time: 90.5 us; the launch traced here: 89.3 us
  waiting for transfers between devices  35.6 us (39%)
  Pallas kernels  28.9 us (32%)
  starting transfers between devices  12.8 us (14%)
  local copies, waits for them, and re-layouts  9.49 us (10%)
  between operations  1.48 us (2%)
  other arithmetic  1.01 us (1%)
    ppermute x9, waiting for transfers between devices, send(): return lax.ppermute(payload, 'fiber', route)  33.9 us
    pallas_call x5, Pallas kernels, band(): pl.pallas_call(functools.partial(band_kernel, own_first=own[1], places=pl...  23.9 us
    ppermute x9, starting transfers between devices, send(): return lax.ppermute(payload, 'fiber', route)  12.3 us
    unnamed x22, local copies, waits for them, and re-layouts  9.35 us
    pallas_call x1, Pallas kernels, body(): pl.pallas_call(spectra_kernel, in_specs=[pl.BlockSpec(memory_space=pltpu....  3.62 us
  transfers between devices with their start and end apart: 10, of which 4 were waited for; matrix products, arithmetic and copies ran while one was open for 1% of the time, Pallas kernels for 23%

profile of v7, /device:TPU:0, one launch (start us, length us, event | category | flops | bytes accessed | tf_op | source)
XLA Modules:
  0.0 89.3 jit_solution(15181193645469487869)
XLA Ops:
  1.4 1.7 %copy-done = bf16[32,320,128]{2,1,0:T(8,128)(2,1)S(1)} copy-done((bf16[32,320,128]{2,1,0:T(8,128)(2,1)S(1)}, bf16[32,320,128]{2,1,0:T(8,128)(2,1)}, u32[]{:S(2)}) %copy-start) | copy-done | bytes 2621464
  3.8 3.6 %shard_map.59 = (bf16[8,320,128]{2,1,0:T(8,128)(2,1)S(1)}, bf16[8,320,128]{2,1,0:T(8,128)(2,1)S(1)}) custom-call(s32[2]{0:T(128)S(1)} %pad_add_fusion.place_ref, bf16[32,320,128]{2,1,0:T(8,128)(2,1)S(1)} %copy-done, bf16[64,128]{1,0:T(8,128)(2,1)S(1)} %copy-done.8), custom_call_target="tpu_custom_call" | custom-call | tf_op jit(solution)/shard_map/pallas_call | solution.py:230
  8.0 1.7 %collective-permute-done.theirs_ref = bf16[8,320,128]{2,1,0:T(8,128)(2,1)S(1)} collective-permute-done((bf16[8,320,128]{2,1,0:T(8,128)(2,1)S(1)}, bf16[8,320,128]{2,1,0:T(8,128)(2,1)S(1)}, u32[]{:S(2)}, u32[]{:S(2)}) %collective-permute-start) | collective-permute-done | bytes 655392 | tf_op jit(solution)/shard_map/ppermute | solution.py:248
  9.7 1.4 %shard_map.60 = (bf16[8,320,128]{2,1,0:T(8,128)(2,1)S(1)}, bf16[8,320,128]{2,1,0:T(8,128)(2,1)S(1)}) custom-call(bf16[8,320,128]{2,1,0:T(8,128)(2,1)S(1)} %get-tuple-element.29.mine_ref, bf16[8,320,128]{2,1,0:T(8,128)(2,1)S(1)} %collective-permute-done.theirs_ref), custom_call_target="tpu_custom_call" | custom-call | tf_op jit(solution)/shard_map/pallas_call | solution.py:252
  11.1 1.3 %collective-permute-start.1 = (bf16[8,320,128]{2,1,0:T(8,128)(2,1)S(1)}, bf16[8,320,128]{2,1,0:T(8,128)(2,1)S(1)}, u32[]{:S(2)}, u32[]{:S(2)}) collective-permute-start(bf16[8,320,128]{2,1,0:T(8,128)(2,1)S(1)} %get-tuple-element.32.refs_0_), channel_id=1, source_target_pairs={{2,0},{6,4},{10,8},{14,12},{3,1},{7,5},{11,9},{15,13},{18,16},{22,... | collective-permute-start | bytes 1966088 | tf_op jit(solution)/shard_map/ppermute | solution.py:270
  12.4 1.3 %collective-permute-start.3 = (bf16[8,320,128]{2,1,0:T(8,128)(2,1)S(1)}, bf16[8,320,128]{2,1,0:T(8,128)(2,1)S(1)}, u32[]{:S(2)}, u32[]{:S(2)}) collective-permute-start(bf16[8,320,128]{2,1,0:T(8,128)(2,1)S(1)} %get-tuple-element.32.refs_0_), channel_id=1, source_target_pairs={{4,0},{6,2},{8,4},{10,6},{12,8},{14,10},{5,1},{7,3},{9,5},{11,7},{... | collective-permute-start | bytes 1966088 | tf_op jit(solution)/shard_map/ppermute | solution.py:270
  14.6 15.7 %collective-permute-done.1.refs_2_ = bf16[8,320,128]{2,1,0:T(8,128)(2,1)S(1)} collective-permute-done((bf16[8,320,128]{2,1,0:T(8,128)(2,1)S(1)}, bf16[8,320,128]{2,1,0:T(8,128)(2,1)S(1)}, u32[]{:S(2)}, u32[]{:S(2)}) %collective-permute-start.1) | collective-permute-done | bytes 655392 | tf_op jit(solution)/shard_map/ppermute | solution.py:270
  31.1 1.3 %collective-permute-start.2 = (bf16[8,320,128]{2,1,0:T(8,128)(2,1)S(1)}, bf16[8,320,128]{2,1,0:T(8,128)(2,1)S(1)}, u32[]{:S(2)}, u32[]{:S(2)}) collective-permute-start(bf16[8,320,128]{2,1,0:T(8,128)(2,1)S(1)} %get-tuple-element.35.refs_0_), channel_id=1, source_target_pairs={{4,0},{6,2},{8,4},{10,6},{12,8},{14,10},{5,1},{7,3},{9,5},{11,7},{... | collective-permute-start | bytes 1966088 | tf_op jit(solution)/shard_map/ppermute | solution.py:270
  32.4 2.3 %collective-permute-start.4 = (bf16[8,320,128]{2,1,0:T(8,128)(2,1)S(1)}, bf16[8,320,128]{2,1,0:T(8,128)(2,1)S(1)}, u32[]{:S(2)}, u32[]{:S(2)}) collective-permute-start(bf16[8,320,128]{2,1,0:T(8,128)(2,1)S(1)} %collective-permute-done.3.refs_4_.refs_2_), channel_id=1, source_target_pairs={{2,0},{6,4},{10,8},{14,12},{0,2},{4,6},{8,10},{12,14},{3,1},{7,5},... | collective-permute-start | bytes 1966088 | tf_op jit(solution)/shard_map/ppermute | solution.py:270
  35.5 14.1 %collective-permute-done.2.refs_4_.refs_2_ = bf16[8,320,128]{2,1,0:T(8,128)(2,1)S(1)} collective-permute-done((bf16[8,320,128]{2,1,0:T(8,128)(2,1)S(1)}, bf16[8,320,128]{2,1,0:T(8,128)(2,1)S(1)}, u32[]{:S(2)}, u32[]{:S(2)}) %collective-permute-start.2) | collective-permute-done | bytes 655392 | tf_op jit(solution)/shard_map/ppermute | solution.py:270
  49.6 1.5 %collective-permute-start.6 = (bf16[8,320,128]{2,1,0:T(8,128)(2,1)S(1)}, bf16[8,320,128]{2,1,0:T(8,128)(2,1)S(1)}, u32[]{:S(2)}, u32[]{:S(2)}) collective-permute-start(bf16[8,320,128]{2,1,0:T(8,128)(2,1)S(1)} %collective-permute-done.2.refs_4_.refs_2_), channel_id=1, source_target_pairs={{0,2},{4,6},{8,10},{12,14},{1,3},{5,7},{9,11},{13,15},{16,18},{20,... | collective-permute-start | bytes 1966088 | tf_op jit(solution)/shard_map/ppermute | solution.py:270
  52.0 1.3 %collective-permute-start.5 = (bf16[8,320,128]{2,1,0:T(8,128)(2,1)S(1)}, bf16[8,320,128]{2,1,0:T(8,128)(2,1)S(1)}, u32[]{:S(2)}, u32[]{:S(2)}) collective-permute-start(bf16[8,320,128]{2,1,0:T(8,128)(2,1)S(1)} %get-tuple-element.35.refs_0_), channel_id=1, source_target_pairs={{2,0},{6,4},{10,8},{14,12},{3,1},{7,5},{11,9},{15,13},{18,16},{22,... | collective-permute-start | bytes 1966088 | tf_op jit(solution)/shard_map/ppermute | solution.py:270
  54.0 1.1 %copy-done.2 = bf16[8,320,128]{2,1,0:T(8,128)(2,1)S(1)} copy-done((bf16[8,320,128]{2,1,0:T(8,128)(2,1)S(1)}, bf16[8,320,128]{2,1,0:T(8,128)(2,1)}, u32[]{:S(2)}) %copy-start.2) | copy-done | bytes 655384
  55.1 1.1 %copy-done.4 = bf16[8,320,128]{2,1,0:T(8,128)(2,1)S(1)} copy-done((bf16[8,320,128]{2,1,0:T(8,128)(2,1)S(1)}, bf16[8,320,128]{2,1,0:T(8,128)(2,1)}, u32[]{:S(2)}) %copy-start.4) | copy-done | bytes 655384
  56.2 1.1 %copy-done.7 = bf16[8,320,128]{2,1,0:T(8,128)(2,1)S(1)} copy-done((bf16[8,320,128]{2,1,0:T(8,128)(2,1)S(1)}, bf16[8,320,128]{2,1,0:T(8,128)(2,1)}, u32[]{:S(2)}) %copy-start.7) | copy-done | bytes 655384
  57.3 1.1 %copy-done.10 = bf16[8,320,128]{2,1,0:T(8,128)(2,1)S(1)} copy-done((bf16[8,320,128]{2,1,0:T(8,128)(2,1)S(1)}, bf16[8,320,128]{2,1,0:T(8,128)(2,1)}, u32[]{:S(2)}) %copy-start.10) | copy-done | bytes 655384
  58.4 6.6 %shard_map.61 = (bf16[16,320,960]{2,1,0:T(8,128)(2,1)}, bf16[16,320,960]{2,1,0:T(8,128)(2,1)}) custom-call(bf16[8,320,128]{2,1,0:T(8,128)(2,1)S(1)} %copy-done.2, bf16[320,384]{1,0:T(8,128)(2,1)S(1)} %get-tuple-element.36.refs_1_, bf16[8,320,128]{2,1,0:T(8,128)(2,1)S(1)} %copy-done.10, bf16[8,320,128]{2,1,0:T(8,128)(2,1)S(1)} %copy-done.7, ...), custom_call_target="tpu_custom_call" | custom-call | flops 838860800 | bytes 6553600 | tf_op jit(solution)/shard_map/pallas_call | solution.py:192
  65.0 4.1 %collective-permute-done.5.refs_2_ = bf16[8,320,128]{2,1,0:T(8,128)(2,1)S(1)} collective-permute-done((bf16[8,320,128]{2,1,0:T(8,128)(2,1)S(1)}, bf16[8,320,128]{2,1,0:T(8,128)(2,1)S(1)}, u32[]{:S(2)}, u32[]{:S(2)}) %collective-permute-start.5) | collective-permute-done | bytes 655392 | tf_op jit(solution)/shard_map/ppermute | solution.py:270
  69.1 1.3 %collective-permute-start.8 = (bf16[4,320,128]{2,1,0:T(8,128)(2,1)S(1)}, bf16[4,320,128]{2,1,0:T(8,128)(2,1)S(1)}, u32[]{:S(2)}, u32[]{:S(2)}) collective-permute-start(bf16[4,320,128]{2,1,0:T(8,128)(2,1)S(1)} %broadcast_select_fusion), channel_id=1, source_target_pairs={{4,0},{6,2},{8,4},{10,6},{12,8},{14,10},{5,1},{7,3},{9,5},{11,7},{... | collective-permute-start | bytes 983048 | tf_op jit(solution)/shard_map/ppermute | solution.py:270
  70.5 1.4 %collective-permute-start.7 = (bf16[4,320,128]{2,1,0:T(8,128)(2,1)S(1)}, bf16[4,320,128]{2,1,0:T(8,128)(2,1)S(1)}, u32[]{:S(2)}, u32[]{:S(2)}) collective-permute-start(bf16[4,320,128]{2,1,0:T(8,128)(2,1)S(1)} %broadcast_select_fusion.1), channel_id=1, source_target_pairs={{4,0},{6,2},{8,4},{10,6},{12,8},{14,10},{5,1},{7,3},{9,5},{11,7},{... | collective-permute-start | bytes 983048 | tf_op jit(solution)/shard_map/ppermute | solution.py:270
  71.9 6.6 %shard_map.62 = (bf16[16,320,960]{2,1,0:T(8,128)(2,1)}, bf16[16,320,960]{2,1,0:T(8,128)(2,1)}) custom-call(bf16[8,320,128]{2,1,0:T(8,128)(2,1)S(1)} %get-tuple-element.35.refs_0_, bf16[320,384]{1,0:T(8,128)(2,1)S(1)} %get-tuple-element.36.refs_1_, ...), custom_call_target="tpu_custom_call", output_to_operand_aliasing={{0}: (5, {}), {1}: (6, {})} | custom-call | flops 838860800 | bytes 6553600 | tf_op jit(solution)/shard_map/pallas_call | solution.py:192
  78.5 4.9 %shard_map.63 = (bf16[16,320,960]{2,1,0:T(8,128)(2,1)}, bf16[16,320,960]{2,1,0:T(8,128)(2,1)}) custom-call(bf16[8,320,128]{2,1,0:T(8,128)(2,1)S(1)} %copy-done.2, bf16[320,384]{1,0:T(8,128)(2,1)S(1)} %get-tuple-element.33.refs_1_, bf16[8,320,128]{2,1,0:T(8,128)(2,1)S(1)} %copy-done.5, ...), custom_call_target="tpu_custom_call", output_to_operand_aliasing={{0}: (5, {}), {1}: (6, {})} | custom-call | flops 419430400 | bytes 3276800 | tf_op jit(solution)/shard_map/pallas_call | solution.py:192
  83.5 2.9 %shard_map.64 = (bf16[16,320,960]{2,1,0:T(8,128)(2,1)}, bf16[16,320,960]{2,1,0:T(8,128)(2,1)}) custom-call(bf16[8,320,128]{2,1,0:T(8,128)(2,1)S(1)} %get-tuple-element.35.refs_0_, bf16[320,384]{1,0:T(8,128)(2,1)S(1)} %get-tuple-element.33.refs_1_, ...), custom_call_target="tpu_custom_call", output_to_operand_aliasing={{0}: (4, {}), {1}: (5, {})} | custom-call | flops 209715200 | bytes 1638400 | tf_op jit(solution)/shard_map/pallas_call | solution.py:192
  86.4 2.9 %shard_map.65 = (bf16[16,320,960]{2,1,0:T(8,128)(2,1)}, bf16[16,320,960]{2,1,0:T(8,128)(2,1)}) custom-call(bf16[8,320,128]{2,1,0:T(8,128)(2,1)S(1)} %get-tuple-element.35.refs_0_, bf16[320,384]{1,0:T(8,128)(2,1)S(1)} %get-tuple-element.33.refs_1_, ...), custom_call_target="tpu_custom_call", output_to_operand_aliasing={{0}: (4, {}), {1}: (5, {})} | custom-call | flops 209715200 | bytes 1638400 | tf_op jit(solution)/shard_map/pallas_call | solution.py:192
  (33 shorter events, 5.7 us)
Async XLA Ops:
  1.4 1.7 %copy-start = (bf16[32,320,128]{2,1,0:T(8,128)(2,1)S(1)}, bf16[32,320,128]{2,1,0:T(8,128)(2,1)}, u32[]{:S(2)}) copy-start(bf16[32,320,128]{2,1,0:T(8,128)(2,1)} %samples_ref.1) | copy-start | bytes 7864324
  3.1 0.7 copy-start.8
  7.4 2.2 %collective-permute-start = (bf16[8,320,128]{2,1,0:T(8,128)(2,1)S(1)}, bf16[8,320,128]{2,1,0:T(8,128)(2,1)S(1)}, u32[]{:S(2)}, u32[]{:S(2)}) collective-permute-start(bf16[8,320,128]{2,1,0:T(8,128)(2,1)S(1)} %get-tuple-element.30), channel_id=1, source_target_pairs={{0,1},{1,0},{2,3},{3,2},{4,5},{5,4},{6,7},{7,6},{8,9},{9,8},{10,11... | collective-permute-start | bytes 1966088 | tf_op jit(solution)/shard_map/ppermute | solution.py:248
  11.1 23.6 %copy-start.1 = (bf16[8,320,128]{2,1,0:T(8,128)(2,1)}, bf16[8,320,128]{2,1,0:T(8,128)(2,1)S(1)}, u32[]{:S(2)}) copy-start(bf16[8,320,128]{2,1,0:T(8,128)(2,1)S(1)} %get-tuple-element.32.refs_0_) | copy-start | bytes 1966084
  11.1 19.2 %collective-permute-start.1 = (bf16[8,320,128]{2,1,0:T(8,128)(2,1)S(1)}, bf16[8,320,128]{2,1,0:T(8,128)(2,1)S(1)}, u32[]{:S(2)}, u32[]{:S(2)}) collective-permute-start(bf16[8,320,128]{2,1,0:T(8,128)(2,1)S(1)} %get-tuple-element.32.refs_0_), channel_id=1, source_target_pairs={{2,0},{6,4},{10,8},{14,12},{3,1},{7,5},{11,9},{15,13},{18,16},{22,... | collective-permute-start | bytes 1966088 | tf_op jit(solution)/shard_map/ppermute | solution.py:270
  12.4 20.0 %collective-permute-start.3 = (bf16[8,320,128]{2,1,0:T(8,128)(2,1)S(1)}, bf16[8,320,128]{2,1,0:T(8,128)(2,1)S(1)}, u32[]{:S(2)}, u32[]{:S(2)}) collective-permute-start(bf16[8,320,128]{2,1,0:T(8,128)(2,1)S(1)} %get-tuple-element.32.refs_0_), channel_id=1, source_target_pairs={{4,0},{6,2},{8,4},{10,6},{12,8},{14,10},{5,1},{7,3},{9,5},{11,7},{... | collective-permute-start | bytes 1966088 | tf_op jit(solution)/shard_map/ppermute | solution.py:270
  30.3 0.8 copy-start.9
  31.1 18.5 %collective-permute-start.2 = (bf16[8,320,128]{2,1,0:T(8,128)(2,1)S(1)}, bf16[8,320,128]{2,1,0:T(8,128)(2,1)S(1)}, u32[]{:S(2)}, u32[]{:S(2)}) collective-permute-start(bf16[8,320,128]{2,1,0:T(8,128)(2,1)S(1)} %get-tuple-element.35.refs_0_), channel_id=1, source_target_pairs={{4,0},{6,2},{8,4},{10,6},{12,8},{14,10},{5,1},{7,3},{9,5},{11,7},{... | collective-permute-start | bytes 1966088 | tf_op jit(solution)/shard_map/ppermute | solution.py:270
  32.4 18.7 %collective-permute-start.4 = (bf16[8,320,128]{2,1,0:T(8,128)(2,1)S(1)}, bf16[8,320,128]{2,1,0:T(8,128)(2,1)S(1)}, u32[]{:S(2)}, u32[]{:S(2)}) collective-permute-start(bf16[8,320,128]{2,1,0:T(8,128)(2,1)S(1)} %collective-permute-done.3.refs_4_.refs_2_), channel_id=1, source_target_pairs={{2,0},{6,4},{10,8},{14,12},{0,2},{4,6},{8,10},{12,14},{3,1},{7,5},... | collective-permute-start | bytes 1966088 | tf_op jit(solution)/shard_map/ppermute | solution.py:270
  34.7 0.8 copy-start.3
  49.6 15.3 %collective-permute-start.6 = (bf16[8,320,128]{2,1,0:T(8,128)(2,1)S(1)}, bf16[8,320,128]{2,1,0:T(8,128)(2,1)S(1)}, u32[]{:S(2)}, u32[]{:S(2)}) collective-permute-start(bf16[8,320,128]{2,1,0:T(8,128)(2,1)S(1)} %collective-permute-done.2.refs_4_.refs_2_), channel_id=1, source_target_pairs={{0,2},{4,6},{8,10},{12,14},{1,3},{5,7},{9,11},{13,15},{16,18},{20,... | collective-permute-start | bytes 1966088 | tf_op jit(solution)/shard_map/ppermute | solution.py:270
  51.1 0.9 copy-start.6
  52.0 17.0 %collective-permute-start.5 = (bf16[8,320,128]{2,1,0:T(8,128)(2,1)S(1)}, bf16[8,320,128]{2,1,0:T(8,128)(2,1)S(1)}, u32[]{:S(2)}, u32[]{:S(2)}) collective-permute-start(bf16[8,320,128]{2,1,0:T(8,128)(2,1)S(1)} %get-tuple-element.35.refs_0_), channel_id=1, source_target_pairs={{2,0},{6,4},{10,8},{14,12},{3,1},{7,5},{11,9},{15,13},{18,16},{22,... | collective-permute-start | bytes 1966088 | tf_op jit(solution)/shard_map/ppermute | solution.py:270
  53.3 25.2 %collective-permute-start.9 = (bf16[8,320,128]{2,1,0:T(8,128)(2,1)}, bf16[8,320,128]{2,1,0:T(8,128)(2,1)S(1)}, u32[]{:S(2)}, u32[]{:S(2)}) collective-permute-start(bf16[8,320,128]{2,1,0:T(8,128)(2,1)} %copy-done.6), channel_id=1, source_target_pairs={{6,2},{10,6},{14,10},{7,3},{11,7},{15,11},{22,18},{26,22},{30,26},... | collective-permute-start | bytes 1966088 | tf_op jit(solution)/shard_map/ppermute | solution.py:270
  54.0 1.1 %copy-start.2 = (bf16[8,320,128]{2,1,0:T(8,128)(2,1)S(1)}, bf16[8,320,128]{2,1,0:T(8,128)(2,1)}, u32[]{:S(2)}) copy-start(bf16[8,320,128]{2,1,0:T(8,128)(2,1)} %copy-done.1) | copy-start | bytes 1966084
  55.1 1.1 %copy-start.4 = (bf16[8,320,128]{2,1,0:T(8,128)(2,1)S(1)}, bf16[8,320,128]{2,1,0:T(8,128)(2,1)}, u32[]{:S(2)}) copy-start(bf16[8,320,128]{2,1,0:T(8,128)(2,1)} %copy-done.3) | copy-start | bytes 1966084
  56.2 1.1 %copy-start.7 = (bf16[8,320,128]{2,1,0:T(8,128)(2,1)S(1)}, bf16[8,320,128]{2,1,0:T(8,128)(2,1)}, u32[]{:S(2)}) copy-start(bf16[8,320,128]{2,1,0:T(8,128)(2,1)} %copy-done.6) | copy-start | bytes 1966084
  57.3 1.1 %copy-start.10 = (bf16[8,320,128]{2,1,0:T(8,128)(2,1)S(1)}, bf16[8,320,128]{2,1,0:T(8,128)(2,1)}, u32[]{:S(2)}) copy-start(bf16[8,320,128]{2,1,0:T(8,128)(2,1)} %copy-done.9) | copy-start | bytes 1966084
  69.1 14.3 %collective-permute-start.8 = (bf16[4,320,128]{2,1,0:T(8,128)(2,1)S(1)}, bf16[4,320,128]{2,1,0:T(8,128)(2,1)S(1)}, u32[]{:S(2)}, u32[]{:S(2)}) collective-permute-start(bf16[4,320,128]{2,1,0:T(8,128)(2,1)S(1)} %broadcast_select_fusion), channel_id=1, source_target_pairs={{4,0},{6,2},{8,4},{10,6},{12,8},{14,10},{5,1},{7,3},{9,5},{11,7},{... | collective-permute-start | bytes 983048 | tf_op jit(solution)/shard_map/ppermute | solution.py:270
  70.5 8.1 %copy-start.5 = (bf16[8,320,128]{2,1,0:T(8,128)(2,1)S(1)}, bf16[8,320,128]{2,1,0:T(8,128)(2,1)}, u32[]{:S(2)}) copy-start(bf16[8,320,128]{2,1,0:T(8,128)(2,1)} %copy-done.3) | copy-start | bytes 1966084
  70.5 15.9 %collective-permute-start.7 = (bf16[4,320,128]{2,1,0:T(8,128)(2,1)S(1)}, bf16[4,320,128]{2,1,0:T(8,128)(2,1)S(1)}, u32[]{:S(2)}, u32[]{:S(2)}) collective-permute-start(bf16[4,320,128]{2,1,0:T(8,128)(2,1)S(1)} %broadcast_select_fusion.1), channel_id=1, source_target_pairs={{4,0},{6,2},{8,4},{10,6},{12,8},{14,10},{5,1},{7,3},{9,5},{11,7},{... | collective-permute-start | bytes 983048 | tf_op jit(solution)/shard_map/ppermute | solution.py:270

commit v8 on v7

--- a/solution.py
+++ b/solution.py
@@ -31,14 +31,29 @@
     return np.concatenate([cosines, sines], axis=0).astype(ml_dtypes.bfloat16)
 
 
-def spectra_kernel(place_ref, samples_ref, table_ref, mine_ref, other_ref, raw_ref):
+def spectra_kernel(
+    place_ref, samples_any, table_any, mine_ref, other_ref, raw_ref, samples_ref, table_ref, sems
+):
     windows, block, _ = samples_ref.shape
     pairs = mine_ref.shape[0]
     here = place_ref[0]
     tiles = raw_ref.shape[0]
+    groups = sems.shape[0] - 1
+    at_once = windows // groups
+    copies = [pltpu.make_async_copy(table_any, table_ref, sems.at[groups])]
+    for group in range(groups):
+        part = pl.ds(group * at_once, at_once)
+        copies.append(
+            pltpu.make_async_copy(samples_any.at[part], samples_ref.at[part], sems.at[group])
+        )
+    for copy in copies:
+        copy.start()
+    copies[0].wait()
     channel = lax.broadcasted_iota(jnp.int32, (1, block), 1)
     active = (channel < place_ref[1]).astype(jnp.float32)
     for w in range(windows):
+        if w % at_once == 0:
+            copies[1 + w // at_once].wait()
         raw = lax.dot_general(
             table_ref[...], samples_ref[w], (((1,), (1,)), ((), ())),
             preferred_element_type=jnp.float32,
@@ -231,15 +246,18 @@
         spectra_kernel,
         in_specs=[
             pl.BlockSpec(memory_space=pltpu.SMEM),
-            pl.BlockSpec(memory_space=pltpu.VMEM),
-            pl.BlockSpec(memory_space=pltpu.VMEM),
+            pl.BlockSpec(memory_space=pltpu.HBM),
+            pl.BlockSpec(memory_space=pltpu.HBM),
         ],
         out_specs=[pl.BlockSpec(memory_space=pltpu.VMEM)] * 2,
         out_shape=[pair_shape, pair_shape],
         scratch_shapes=[
-            pltpu.VMEM((-(-block // LANES), windows_here * 2 * FREQS, LANES), jnp.float32)
+            pltpu.VMEM((-(-block // LANES), windows_here * 2 * FREQS, LANES), jnp.float32),
+            pltpu.VMEM((windows_here, block, length), jnp.bfloat16),
+            pltpu.VMEM((2 * FREQS, length), jnp.bfloat16),
+            pltpu.SemaphoreType.DMA((5,)),
         ],
-        compiler_params=pltpu.CompilerParams(vmem_limit_bytes=VMEM),
+        compiler_params=pltpu.CompilerParams(vmem_limit_bytes=60 << 20),
     )(
         jnp.stack([here, counts[0]]),
         samples,
@@ -292,19 +310,20 @@
     z_low = send(own[0], down)
     own_high, ahead_low, *masks = after(own[1], ahead_low, *masks)
     z_high = send(own_high, down)
-    y_low = send(z_low, to_even + to_odd)
+    up_low = send(z_low, to_odd)
+    ahead_high = send(own_high, to_even)
     up_high = send(z_high, to_odd)
-    own_high, y_low = after(own[1], y_low)
-    ahead_high = send(own_high, to_even)
-    z_next = send(y_low, down_odd)
-    outs = near(None, 0, ((ahead_low, 0), (y_low, 0)), ((z_low, 0), (z_low, 0)))
+    z_back, ahead_high = after(z_low, ahead_high)
+    back_low = send(z_back, to_even)
+    z_next = send(up_low, down_odd)
+    outs = near(None, 0, ((ahead_low, 0), (up_low, 0)), ((z_low, 0), (z_low, 0)))
     up_high, *outs = after(up_high, *outs)
     last = [
         send(pick(ahead_high[at : at + quarter], up_high[at : at + quarter]), down)
         for at in (0, quarter)
     ]
     outs = near(outs, 1, ((ahead_high, 0), (up_high, 0)), ((z_high, 0), (z_high, 0)))
-    outs = far(outs, 0, 0, half, ((z_low, 0), (z_low, 0)), ((y_low, 0), (z_next, 0)))
+    outs = far(outs, 0, 0, half, ((z_low, 0), (z_low, 0)), ((back_low, 0), (z_next, 0)))
     for part, at in enumerate((0, quarter)):
         outs = far(
             outs, 1, at, quarter, ((z_high, at), (z_high, at)), ((last[part], 0), (last[part], 0))

time: 90.5 us -> 93.2 us (1.030)
  the two profiles are of different devices: /device:TPU:0 before, /device:TPU:30 now
where the time goes in v8:
time: 93.2 us; the launch traced here: 92.6 us
  Pallas kernels  34 us (36%)
  starting transfers between devices  26.1 us (28%)
  waiting for transfers between devices  25.2 us (27%)
  local copies, waits for them, and re-layouts  4.24 us (5%)
  other arithmetic  1.52 us (2%)
  between operations  1.49 us (2%)
    pallas_call x5, Pallas kernels, band(): pl.pallas_call(functools.partial(band_kernel, own_first=own[1], places=pl...  26.3 us
    ppermute x10, starting transfers between devices, send(): return lax.ppermute(payload, 'fiber', route)  26.1 us
    ppermute x10, waiting for transfers between devices, send(): return lax.ppermute(payload, 'fiber', route)  22.9 us
    pallas_call x1, Pallas kernels, body(): pl.pallas_call(spectra_kernel, in_specs=[pl.BlockSpec(memory_space=pltpu....  6.34 us
    unnamed x10, local copies, waits for them, and re-layouts  4.1 us
    ppermute x1, waiting for transfers between devices, body(): theirs = lax.ppermute(other, 'tm', [(0, 1), (1, 0)])  2.3 us
  transfers between devices with their start and end apart: 11, of which 5 were waited for; matrix products, arithmetic and copies ran while one was open for 1% of the time, Pallas kernels for 25%

profile of v8, /device:TPU:30, one launch (start us, length us, event | category | flops | bytes accessed | tf_op | source)
XLA Modules:
  0.0 92.6 jit_solution(14435174242663249385)
XLA Ops:
  1.9 6.3 %shard_map.59 = (bf16[8,320,128]{2,1,0:T(8,128)(2,1)}, bf16[8,320,128]{2,1,0:T(8,128)(2,1)}) custom-call(s32[2]{0:T(128)} %pad_add_fusion.place_ref, bf16[32,320,128]{2,1,0:T(8,128)(2,1)} %samples_any.1, bf16[64,128]{1,0:T(8,128)(2,1)} %constant.25.clone.table_any), custom_call_target="tpu_custom_call" | custom-call | tf_op jit(solution)/shard_map/pallas_call | solution.py:245
  8.3 2.3 %collective-permute-done.theirs_ref = bf16[8,320,128]{2,1,0:T(8,128)(2,1)S(1)} collective-permute-done((bf16[8,320,128]{2,1,0:T(8,128)(2,1)}, bf16[8,320,128]{2,1,0:T(8,128)(2,1)S(1)}, u32[]{:S(2)}, u32[]{:S(2)}) %collective-permute-start) | collective-permute-done | bytes 655392 | tf_op jit(solution)/shard_map/ppermute | solution.py:266
  10.6 1.1 %copy-done.2 = bf16[8,320,128]{2,1,0:T(8,128)(2,1)S(1)} copy-done((bf16[8,320,128]{2,1,0:T(8,128)(2,1)S(1)}, bf16[8,320,128]{2,1,0:T(8,128)(2,1)}, u32[]{:S(2)}) %copy-start.2) | copy-done | bytes 655384
  11.7 1.4 %shard_map.60 = (bf16[8,320,128]{2,1,0:T(8,128)(2,1)S(1)}, bf16[8,320,128]{2,1,0:T(8,128)(2,1)S(1)}) custom-call(bf16[8,320,128]{2,1,0:T(8,128)(2,1)S(1)} %copy-done.2, bf16[8,320,128]{2,1,0:T(8,128)(2,1)S(1)} %collective-permute-done.theirs_ref), custom_call_target="tpu_custom_call" | custom-call | tf_op jit(solution)/shard_map/pallas_call | solution.py:270
  13.1 2.5 %collective-permute-start.1 = (bf16[8,320,128]{2,1,0:T(8,128)(2,1)S(1)}, bf16[8,320,128]{2,1,0:T(8,128)(2,1)S(1)}, u32[]{:S(2)}, u32[]{:S(2)}) collective-permute-start(bf16[8,320,128]{2,1,0:T(8,128)(2,1)S(1)} %get-tuple-element.32.refs_0_), channel_id=1, source_target_pairs={{2,0},{6,4},{10,8},{14,12},{3,1},{7,5},{11,9},{15,13},{18,16},{22,... | collective-permute-start | bytes 1966088 | tf_op jit(solution)/shard_map/ppermute | solution.py:288
  15.6 3.2 %collective-permute-start.3 = (bf16[8,320,128]{2,1,0:T(8,128)(2,1)S(1)}, bf16[8,320,128]{2,1,0:T(8,128)(2,1)}, u32[]{:S(2)}, u32[]{:S(2)}) collective-permute-start(bf16[8,320,128]{2,1,0:T(8,128)(2,1)S(1)} %get-tuple-element.32.refs_0_), channel_id=1, source_target_pairs={{4,0},{6,2},{8,4},{10,6},{12,8},{14,10},{5,1},{7,3},{9,5},{11,7},{... | collective-permute-start | bytes 1966088 | tf_op jit(solution)/shard_map/ppermute | solution.py:288
  19.7 10.1 %collective-permute-done.1.refs_2_ = bf16[8,320,128]{2,1,0:T(8,128)(2,1)S(1)} collective-permute-done((bf16[8,320,128]{2,1,0:T(8,128)(2,1)S(1)}, bf16[8,320,128]{2,1,0:T(8,128)(2,1)S(1)}, u32[]{:S(2)}, u32[]{:S(2)}) %collective-permute-start.1) | collective-permute-done | bytes 655392 | tf_op jit(solution)/shard_map/ppermute | solution.py:288
  30.6 2.4 %collective-permute-start.2 = (bf16[8,320,128]{2,1,0:T(8,128)(2,1)S(1)}, bf16[8,320,128]{2,1,0:T(8,128)(2,1)S(1)}, u32[]{:S(2)}, u32[]{:S(2)}) collective-permute-start(bf16[8,320,128]{2,1,0:T(8,128)(2,1)S(1)} %get-tuple-element.34.refs_0_), channel_id=1, source_target_pairs={{4,0},{6,2},{8,4},{10,6},{12,8},{14,10},{5,1},{7,3},{9,5},{11,7},{... | collective-permute-start | bytes 1966088 | tf_op jit(solution)/shard_map/ppermute | solution.py:288
  33.0 4.4 %collective-permute-start.4 = (bf16[8,320,128]{2,1,0:T(8,128)(2,1)S(1)}, bf16[8,320,128]{2,1,0:T(8,128)(2,1)S(1)}, u32[]{:S(2)}, u32[]{:S(2)}) collective-permute-start(bf16[8,320,128]{2,1,0:T(8,128)(2,1)S(1)} %get-tuple-element.34.refs_0_), channel_id=1, source_target_pairs={{2,0},{6,4},{10,8},{14,12},{3,1},{7,5},{11,9},{15,13},{18,16},{22,... | collective-permute-start | bytes 1966088 | tf_op jit(solution)/shard_map/ppermute | solution.py:288
  37.4 1.3 %collective-permute-start.6 = (bf16[8,320,128]{2,1,0:T(8,128)(2,1)}, bf16[8,320,128]{2,1,0:T(8,128)(2,1)}, u32[]{:S(2)}, u32[]{:S(2)}) collective-permute-start(bf16[8,320,128]{2,1,0:T(8,128)(2,1)} %collective-permute-done.3.refs_4_.refs_2_), channel_id=1, source_target_pairs={{0,2},{4,6},{8,10},{12,14},{1,3},{5,7},{9,11},{13,15},{16,18},{20,... | collective-permute-start | bytes 1966088 | tf_op jit(solution)/shard_map/ppermute | solution.py:288
  38.8 7.7 %collective-permute-done.2.refs_4_.refs_2_ = bf16[8,320,128]{2,1,0:T(8,128)(2,1)S(1)} collective-permute-done((bf16[8,320,128]{2,1,0:T(8,128)(2,1)S(1)}, bf16[8,320,128]{2,1,0:T(8,128)(2,1)S(1)}, u32[]{:S(2)}, u32[]{:S(2)}) %collective-permute-start.2) | collective-permute-done | bytes 655392 | tf_op jit(solution)/shard_map/ppermute | solution.py:288
  46.4 1.3 %collective-permute-start.5 = (bf16[8,320,128]{2,1,0:T(8,128)(2,1)S(1)}, bf16[8,320,128]{2,1,0:T(8,128)(2,1)S(1)}, u32[]{:S(2)}, u32[]{:S(2)}) collective-permute-start(bf16[8,320,128]{2,1,0:T(8,128)(2,1)S(1)} %collective-permute-done.2.refs_4_.refs_2_), channel_id=1, source_target_pairs={{0,2},{4,6},{8,10},{12,14},{1,3},{5,7},{9,11},{13,15},{16,18},{20,... | collective-permute-start | bytes 1966088 | tf_op jit(solution)/shard_map/ppermute | solution.py:288
  47.7 3.0 %collective-permute-done.4.refs_2_ = bf16[8,320,128]{2,1,0:T(8,128)(2,1)S(1)} collective-permute-done((bf16[8,320,128]{2,1,0:T(8,128)(2,1)S(1)}, bf16[8,320,128]{2,1,0:T(8,128)(2,1)S(1)}, u32[]{:S(2)}, u32[]{:S(2)}) %collective-permute-start.4) | collective-permute-done | bytes 655392 | tf_op jit(solution)/shard_map/ppermute | solution.py:288
  50.7 4.4 %collective-permute-start.9 = (bf16[8,320,128]{2,1,0:T(8,128)(2,1)}, bf16[8,320,128]{2,1,0:T(8,128)(2,1)S(1)}, u32[]{:S(2)}, u32[]{:S(2)}) collective-permute-start(bf16[8,320,128]{2,1,0:T(8,128)(2,1)} %collective-permute-done.3.refs_4_.refs_2_), channel_id=1, source_target_pairs={{2,0},{6,4},{10,8},{14,12},{3,1},{7,5},{11,9},{15,13},{18,16},{22,... | collective-permute-start | bytes 1966088 | tf_op jit(solution)/shard_map/ppermute | solution.py:288
  55.1 2.2 %collective-permute-done.6.refs_3_ = bf16[8,320,128]{2,1,0:T(8,128)(2,1)} collective-permute-done((bf16[8,320,128]{2,1,0:T(8,128)(2,1)}, bf16[8,320,128]{2,1,0:T(8,128)(2,1)}, u32[]{:S(2)}, u32[]{:S(2)}) %collective-permute-start.6) | collective-permute-done | bytes 655392 | tf_op jit(solution)/shard_map/ppermute | solution.py:288
  57.3 2.3 %collective-permute-start.10 = (bf16[8,320,128]{2,1,0:T(8,128)(2,1)}, bf16[8,320,128]{2,1,0:T(8,128)(2,1)S(1)}, u32[]{:S(2)}, u32[]{:S(2)}) collective-permute-start(bf16[8,320,128]{2,1,0:T(8,128)(2,1)} %collective-permute-done.6.refs_3_), channel_id=1, source_target_pairs={{6,2},{10,6},{14,10},{7,3},{11,7},{15,11},{22,18},{26,22},{30,26},... | collective-permute-start | bytes 1966088 | tf_op jit(solution)/shard_map/ppermute | solution.py:288
  60.8 1.1 %copy-done.4 = bf16[8,320,128]{2,1,0:T(8,128)(2,1)S(1)} copy-done((bf16[8,320,128]{2,1,0:T(8,128)(2,1)S(1)}, bf16[8,320,128]{2,1,0:T(8,128)(2,1)}, u32[]{:S(2)}) %copy-start.4) | copy-done | bytes 655384
  61.9 7.8 %shard_map.61 = (bf16[16,320,960]{2,1,0:T(8,128)(2,1)}, bf16[16,320,960]{2,1,0:T(8,128)(2,1)}) custom-call(bf16[8,320,128]{2,1,0:T(8,128)(2,1)S(1)} %copy-done.1, bf16[320,384]{1,0:T(8,128)(2,1)S(1)} %get-tuple-element.36.refs_1_, bf16[8,320,128]{2,1,0:T(8,128)(2,1)S(1)} %copy-done.4, bf16[8,320,128]{2,1,0:T(8,128)(2,1)} %collective-permute-done.6.refs_3_, ...), custom_call_target="tpu_custom_call" | custom-call | flops 838860800 | bytes 6553600 | tf_op jit(solution)/shard_map/pallas_call | solution.py:207
  69.9 2.3 %collective-permute-start.8 = (bf16[4,320,128]{2,1,0:T(8,128)(2,1)S(1)}, bf16[4,320,128]{2,1,0:T(8,128)(2,1)S(1)}, u32[]{:S(2)}, u32[]{:S(2)}) collective-permute-start(bf16[4,320,128]{2,1,0:T(8,128)(2,1)S(1)} %broadcast_select_fusion), channel_id=1, source_target_pairs={{4,0},{6,2},{8,4},{10,6},{12,8},{14,10},{5,1},{7,3},{9,5},{11,7},{... | collective-permute-start | bytes 983048 | tf_op jit(solution)/shard_map/ppermute | solution.py:288
  72.2 1.9 %collective-permute-start.7 = (bf16[4,320,128]{2,1,0:T(8,128)(2,1)S(1)}, bf16[4,320,128]{2,1,0:T(8,128)(2,1)S(1)}, u32[]{:S(2)}, u32[]{:S(2)}) collective-permute-start(bf16[4,320,128]{2,1,0:T(8,128)(2,1)S(1)} %broadcast_select_fusion.1), channel_id=1, source_target_pairs={{4,0},{6,2},{8,4},{10,6},{12,8},{14,10},{5,1},{7,3},{9,5},{11,7},{... | collective-permute-start | bytes 983048 | tf_op jit(solution)/shard_map/ppermute | solution.py:288
  74.2 6.6 %shard_map.62 = (bf16[16,320,960]{2,1,0:T(8,128)(2,1)}, bf16[16,320,960]{2,1,0:T(8,128)(2,1)}) custom-call(bf16[8,320,128]{2,1,0:T(8,128)(2,1)S(1)} %get-tuple-element.34.refs_0_, bf16[320,384]{1,0:T(8,128)(2,1)S(1)} %get-tuple-element.36.refs_1_, ...), custom_call_target="tpu_custom_call", output_to_operand_aliasing={{0}: (5, {}), {1}: (6, {})} | custom-call | flops 838860800 | bytes 6553600 | tf_op jit(solution)/shard_map/pallas_call | solution.py:207
  80.8 6.0 %shard_map.63 = (bf16[16,320,960]{2,1,0:T(8,128)(2,1)}, bf16[16,320,960]{2,1,0:T(8,128)(2,1)}) custom-call(bf16[8,320,128]{2,1,0:T(8,128)(2,1)S(1)} %copy-done.1, bf16[320,384]{1,0:T(8,128)(2,1)S(1)} %get-tuple-element.33.refs_1_, bf16[8,320,128]{2,1,0:T(8,128)(2,1)} %collective-permute-done.3.refs_4_.refs_2_, ...), custom_call_target="tpu_custom_call", output_to_operand_aliasing={{0}: (5, {}), {1}: (6, {})} | custom-call | flops 419430400 | bytes 3276800 | tf_op jit(solution)/shard_map/pallas_call | solution.py:207
  86.8 2.9 %shard_map.64 = (bf16[16,320,960]{2,1,0:T(8,128)(2,1)}, bf16[16,320,960]{2,1,0:T(8,128)(2,1)}) custom-call(bf16[8,320,128]{2,1,0:T(8,128)(2,1)S(1)} %get-tuple-element.34.refs_0_, bf16[320,384]{1,0:T(8,128)(2,1)S(1)} %get-tuple-element.33.refs_1_, ...), custom_call_target="tpu_custom_call", output_to_operand_aliasing={{0}: (4, {}), {1}: (5, {})} | custom-call | flops 209715200 | bytes 1638400 | tf_op jit(solution)/shard_map/pallas_call | solution.py:207
  89.7 2.9 %shard_map.65 = (bf16[16,320,960]{2,1,0:T(8,128)(2,1)}, bf16[16,320,960]{2,1,0:T(8,128)(2,1)}) custom-call(bf16[8,320,128]{2,1,0:T(8,128)(2,1)S(1)} %get-tuple-element.34.refs_0_, bf16[320,384]{1,0:T(8,128)(2,1)S(1)} %get-tuple-element.33.refs_1_, ...), custom_call_target="tpu_custom_call", output_to_operand_aliasing={{0}: (4, {}), {1}: (5, {})} | custom-call | flops 209715200 | bytes 1638400 | tf_op jit(solution)/shard_map/pallas_call | solution.py:207
  (23 shorter events, 3.7 us)
Async XLA Ops:
  8.2 2.4 %collective-permute-start = (bf16[8,320,128]{2,1,0:T(8,128)(2,1)}, bf16[8,320,128]{2,1,0:T(8,128)(2,1)S(1)}, u32[]{:S(2)}, u32[]{:S(2)}) collective-permute-start(bf16[8,320,128]{2,1,0:T(8,128)(2,1)} %get-tuple-element.30), channel_id=1, source_target_pairs={{0,1},{1,0},{2,3},{3,2},{4,5},{5,4},{6,7},{7,6},{8,9},{9,8},{10,11... | collective-permute-start | bytes 1966088 | tf_op jit(solution)/shard_map/ppermute | solution.py:266
  10.6 1.1 %copy-start.2 = (bf16[8,320,128]{2,1,0:T(8,128)(2,1)S(1)}, bf16[8,320,128]{2,1,0:T(8,128)(2,1)}, u32[]{:S(2)}) copy-start(bf16[8,320,128]{2,1,0:T(8,128)(2,1)} %get-tuple-element.29.mine_ref) | copy-start | bytes 1966084
  13.1 25.7 %copy-start = (bf16[8,320,128]{2,1,0:T(8,128)(2,1)}, bf16[8,320,128]{2,1,0:T(8,128)(2,1)S(1)}, u32[]{:S(2)}) copy-start(bf16[8,320,128]{2,1,0:T(8,128)(2,1)S(1)} %get-tuple-element.32.refs_0_) | copy-start | bytes 1966084
  13.1 16.7 %collective-permute-start.1 = (bf16[8,320,128]{2,1,0:T(8,128)(2,1)S(1)}, bf16[8,320,128]{2,1,0:T(8,128)(2,1)S(1)}, u32[]{:S(2)}, u32[]{:S(2)}) collective-permute-start(bf16[8,320,128]{2,1,0:T(8,128)(2,1)S(1)} %get-tuple-element.32.refs_0_), channel_id=1, source_target_pairs={{2,0},{6,4},{10,8},{14,12},{3,1},{7,5},{11,9},{15,13},{18,16},{22,... | collective-permute-start | bytes 1966088 | tf_op jit(solution)/shard_map/ppermute | solution.py:288
  15.6 21.9 %collective-permute-start.3 = (bf16[8,320,128]{2,1,0:T(8,128)(2,1)S(1)}, bf16[8,320,128]{2,1,0:T(8,128)(2,1)}, u32[]{:S(2)}, u32[]{:S(2)}) collective-permute-start(bf16[8,320,128]{2,1,0:T(8,128)(2,1)S(1)} %get-tuple-element.32.refs_0_), channel_id=1, source_target_pairs={{4,0},{6,2},{8,4},{10,6},{12,8},{14,10},{5,1},{7,3},{9,5},{11,7},{... | collective-permute-start | bytes 1966088 | tf_op jit(solution)/shard_map/ppermute | solution.py:288
  29.8 0.8 copy-start.3
  30.6 15.8 %collective-permute-start.2 = (bf16[8,320,128]{2,1,0:T(8,128)(2,1)S(1)}, bf16[8,320,128]{2,1,0:T(8,128)(2,1)S(1)}, u32[]{:S(2)}, u32[]{:S(2)}) collective-permute-start(bf16[8,320,128]{2,1,0:T(8,128)(2,1)S(1)} %get-tuple-element.34.refs_0_), channel_id=1, source_target_pairs={{4,0},{6,2},{8,4},{10,6},{12,8},{14,10},{5,1},{7,3},{9,5},{11,7},{... | collective-permute-start | bytes 1966088 | tf_op jit(solution)/shard_map/ppermute | solution.py:288
  33.0 17.7 %collective-permute-start.4 = (bf16[8,320,128]{2,1,0:T(8,128)(2,1)S(1)}, bf16[8,320,128]{2,1,0:T(8,128)(2,1)S(1)}, u32[]{:S(2)}, u32[]{:S(2)}) collective-permute-start(bf16[8,320,128]{2,1,0:T(8,128)(2,1)S(1)} %get-tuple-element.34.refs_0_), channel_id=1, source_target_pairs={{2,0},{6,4},{10,8},{14,12},{3,1},{7,5},{11,9},{15,13},{18,16},{22,... | collective-permute-start | bytes 1966088 | tf_op jit(solution)/shard_map/ppermute | solution.py:288
  37.4 19.9 %collective-permute-start.6 = (bf16[8,320,128]{2,1,0:T(8,128)(2,1)}, bf16[8,320,128]{2,1,0:T(8,128)(2,1)}, u32[]{:S(2)}, u32[]{:S(2)}) collective-permute-start(bf16[8,320,128]{2,1,0:T(8,128)(2,1)} %collective-permute-done.3.refs_4_.refs_2_), channel_id=1, source_target_pairs={{0,2},{4,6},{8,10},{12,14},{1,3},{5,7},{9,11},{13,15},{16,18},{20,... | collective-permute-start | bytes 1966088 | tf_op jit(solution)/shard_map/ppermute | solution.py:288
  46.4 23.3 %collective-permute-start.5 = (bf16[8,320,128]{2,1,0:T(8,128)(2,1)S(1)}, bf16[8,320,128]{2,1,0:T(8,128)(2,1)S(1)}, u32[]{:S(2)}, u32[]{:S(2)}) collective-permute-start(bf16[8,320,128]{2,1,0:T(8,128)(2,1)S(1)} %collective-permute-done.2.refs_4_.refs_2_), channel_id=1, source_target_pairs={{0,2},{4,6},{8,10},{12,14},{1,3},{5,7},{9,11},{13,15},{16,18},{20,... | collective-permute-start | bytes 1966088 | tf_op jit(solution)/shard_map/ppermute | solution.py:288
  50.7 30.1 %collective-permute-start.9 = (bf16[8,320,128]{2,1,0:T(8,128)(2,1)}, bf16[8,320,128]{2,1,0:T(8,128)(2,1)S(1)}, u32[]{:S(2)}, u32[]{:S(2)}) collective-permute-start(bf16[8,320,128]{2,1,0:T(8,128)(2,1)} %collective-permute-done.3.refs_4_.refs_2_), channel_id=1, source_target_pairs={{2,0},{6,4},{10,8},{14,12},{3,1},{7,5},{11,9},{15,13},{18,16},{22,... | collective-permute-start | bytes 1966088 | tf_op jit(solution)/shard_map/ppermute | solution.py:288
  57.3 23.5 %collective-permute-start.10 = (bf16[8,320,128]{2,1,0:T(8,128)(2,1)}, bf16[8,320,128]{2,1,0:T(8,128)(2,1)S(1)}, u32[]{:S(2)}, u32[]{:S(2)}) collective-permute-start(bf16[8,320,128]{2,1,0:T(8,128)(2,1)} %collective-permute-done.6.refs_3_), channel_id=1, source_target_pairs={{6,2},{10,6},{14,10},{7,3},{11,7},{15,11},{22,18},{26,22},{30,26},... | collective-permute-start | bytes 1966088 | tf_op jit(solution)/shard_map/ppermute | solution.py:288
  59.7 1.1 %copy-start.1 = (bf16[8,320,128]{2,1,0:T(8,128)(2,1)S(1)}, bf16[8,320,128]{2,1,0:T(8,128)(2,1)}, u32[]{:S(2)}) copy-start(bf16[8,320,128]{2,1,0:T(8,128)(2,1)} %copy-done) | copy-start | bytes 1966084
  60.8 1.1 %copy-start.4 = (bf16[8,320,128]{2,1,0:T(8,128)(2,1)S(1)}, bf16[8,320,128]{2,1,0:T(8,128)(2,1)}, u32[]{:S(2)}) copy-start(bf16[8,320,128]{2,1,0:T(8,128)(2,1)} %copy-done.3) | copy-start | bytes 1966084
  69.9 16.9 %collective-permute-start.8 = (bf16[4,320,128]{2,1,0:T(8,128)(2,1)S(1)}, bf16[4,320,128]{2,1,0:T(8,128)(2,1)S(1)}, u32[]{:S(2)}, u32[]{:S(2)}) collective-permute-start(bf16[4,320,128]{2,1,0:T(8,128)(2,1)S(1)} %broadcast_select_fusion), channel_id=1, source_target_pairs={{4,0},{6,2},{8,4},{10,6},{12,8},{14,10},{5,1},{7,3},{9,5},{11,7},{... | collective-permute-start | bytes 983048 | tf_op jit(solution)/shard_map/ppermute | solution.py:288
  72.2 17.5 %collective-permute-start.7 = (bf16[4,320,128]{2,1,0:T(8,128)(2,1)S(1)}, bf16[4,320,128]{2,1,0:T(8,128)(2,1)S(1)}, u32[]{:S(2)}, u32[]{:S(2)}) collective-permute-start(bf16[4,320,128]{2,1,0:T(8,128)(2,1)S(1)} %broadcast_select_fusion.1), channel_id=1, source_target_pairs={{4,0},{6,2},{8,4},{10,6},{12,8},{14,10},{5,1},{7,3},{9,5},{11,7},{... | collective-permute-start | bytes 983048 | tf_op jit(solution)/shard_map/ppermute | solution.py:288

commit v9 on v7

--- a/solution.py
+++ b/solution.py
@@ -292,19 +292,20 @@
     z_low = send(own[0], down)
     own_high, ahead_low, *masks = after(own[1], ahead_low, *masks)
     z_high = send(own_high, down)
-    y_low = send(z_low, to_even + to_odd)
+    up_low = send(z_low, to_odd)
+    ahead_high = send(own_high, to_even)
     up_high = send(z_high, to_odd)
-    own_high, y_low = after(own[1], y_low)
-    ahead_high = send(own_high, to_even)
-    z_next = send(y_low, down_odd)
-    outs = near(None, 0, ((ahead_low, 0), (y_low, 0)), ((z_low, 0), (z_low, 0)))
+    z_back, ahead_high = after(z_low, ahead_high)
+    back_low = send(z_back, to_even)
+    z_next = send(up_low, down_odd)
+    outs = near(None, 0, ((ahead_low, 0), (up_low, 0)), ((z_low, 0), (z_low, 0)))
     up_high, *outs = after(up_high, *outs)
     last = [
         send(pick(ahead_high[at : at + quarter], up_high[at : at + quarter]), down)
         for at in (0, quarter)
     ]
     outs = near(outs, 1, ((ahead_high, 0), (up_high, 0)), ((z_high, 0), (z_high, 0)))
-    outs = far(outs, 0, 0, half, ((z_low, 0), (z_low, 0)), ((y_low, 0), (z_next, 0)))
+    outs = far(outs, 0, 0, half, ((z_low, 0), (z_low, 0)), ((back_low, 0), (z_next, 0)))
     for part, at in enumerate((0, quarter)):
         outs = far(
             outs, 1, at, quarter, ((z_high, at), (z_high, at)), ((last[part], 0), (last[part], 0))

time: 90.5 us -> 91.1 us (level)
  the two profiles are of different devices: /device:TPU:0 before, /device:TPU:30 now
where the time goes in v9:
time: 91.1 us; the launch traced here: 90.5 us
  Pallas kernels  31.3 us (34%)
  starting transfers between devices  26.1 us (29%)
  waiting for transfers between devices  25 us (27%)
  local copies, waits for them, and re-layouts  5.61 us (6%)
  between operations  1.48 us (2%)
  other arithmetic  1 us (1%)
    pallas_call x5, Pallas kernels, band(): pl.pallas_call(functools.partial(band_kernel, own_first=own[1], places=pl...  26.3 us
    ppermute x10, starting transfers between devices, send(): return lax.ppermute(payload, 'fiber', route)  26.1 us
    ppermute x10, waiting for transfers between devices, send(): return lax.ppermute(payload, 'fiber', route)  22.9 us
    unnamed x12, local copies, waits for them, and re-layouts  5.47 us
    pallas_call x1, Pallas kernels, body(): pl.pallas_call(spectra_kernel, in_specs=[pl.BlockSpec(memory_space=pltpu....  3.63 us
    ppermute x1, waiting for transfers between devices, body(): theirs = lax.ppermute(other, 'tm', [(0, 1), (1, 0)])  2.08 us
  transfers between devices with their start and end apart: 11, of which 5 were waited for; matrix products, arithmetic and copies ran while one was open for 1% of the time, Pallas kernels for 26%

profile of v9, /device:TPU:30, one launch (start us, length us, event | category | flops | bytes accessed | tf_op | source)
XLA Modules:
  0.0 90.5 jit_solution(9622584890263647971)
XLA Ops:
  1.4 1.7 %copy-done = bf16[32,320,128]{2,1,0:T(8,128)(2,1)S(1)} copy-done((bf16[32,320,128]{2,1,0:T(8,128)(2,1)S(1)}, bf16[32,320,128]{2,1,0:T(8,128)(2,1)}, u32[]{:S(2)}) %copy-start) | copy-done | bytes 2621464
  3.8 3.6 %shard_map.59 = (bf16[8,320,128]{2,1,0:T(8,128)(2,1)S(1)}, bf16[8,320,128]{2,1,0:T(8,128)(2,1)S(1)}) custom-call(s32[2]{0:T(128)S(1)} %pad_add_fusion.place_ref, bf16[32,320,128]{2,1,0:T(8,128)(2,1)S(1)} %copy-done, bf16[64,128]{1,0:T(8,128)(2,1)S(1)} %copy-done.3), custom_call_target="tpu_custom_call" | custom-call | tf_op jit(solution)/shard_map/pallas_call | solution.py:230
  7.5 2.1 %collective-permute-done.theirs_ref = bf16[8,320,128]{2,1,0:T(8,128)(2,1)S(1)} collective-permute-done((bf16[8,320,128]{2,1,0:T(8,128)(2,1)S(1)}, bf16[8,320,128]{2,1,0:T(8,128)(2,1)S(1)}, u32[]{:S(2)}, u32[]{:S(2)}) %collective-permute-start) | collective-permute-done | bytes 655392 | tf_op jit(solution)/shard_map/ppermute | solution.py:248
  9.6 1.4 %shard_map.60 = (bf16[8,320,128]{2,1,0:T(8,128)(2,1)S(1)}, bf16[8,320,128]{2,1,0:T(8,128)(2,1)S(1)}) custom-call(bf16[8,320,128]{2,1,0:T(8,128)(2,1)S(1)} %get-tuple-element.29.mine_ref, bf16[8,320,128]{2,1,0:T(8,128)(2,1)S(1)} %collective-permute-done.theirs_ref), custom_call_target="tpu_custom_call" | custom-call | tf_op jit(solution)/shard_map/pallas_call | solution.py:252
  11.0 2.5 %collective-permute-start.1 = (bf16[8,320,128]{2,1,0:T(8,128)(2,1)S(1)}, bf16[8,320,128]{2,1,0:T(8,128)(2,1)S(1)}, u32[]{:S(2)}, u32[]{:S(2)}) collective-permute-start(bf16[8,320,128]{2,1,0:T(8,128)(2,1)S(1)} %get-tuple-element.32.refs_0_), channel_id=1, source_target_pairs={{2,0},{6,4},{10,8},{14,12},{3,1},{7,5},{11,9},{15,13},{18,16},{22,... | collective-permute-start | bytes 1966088 | tf_op jit(solution)/shard_map/ppermute | solution.py:270
  13.5 3.2 %collective-permute-start.3 = (bf16[8,320,128]{2,1,0:T(8,128)(2,1)S(1)}, bf16[8,320,128]{2,1,0:T(8,128)(2,1)}, u32[]{:S(2)}, u32[]{:S(2)}) collective-permute-start(bf16[8,320,128]{2,1,0:T(8,128)(2,1)S(1)} %get-tuple-element.32.refs_0_), channel_id=1, source_target_pairs={{4,0},{6,2},{8,4},{10,6},{12,8},{14,10},{5,1},{7,3},{9,5},{11,7},{... | collective-permute-start | bytes 1966088 | tf_op jit(solution)/shard_map/ppermute | solution.py:270
  17.6 10.1 %collective-permute-done.1.refs_2_ = bf16[8,320,128]{2,1,0:T(8,128)(2,1)S(1)} collective-permute-done((bf16[8,320,128]{2,1,0:T(8,128)(2,1)S(1)}, bf16[8,320,128]{2,1,0:T(8,128)(2,1)S(1)}, u32[]{:S(2)}, u32[]{:S(2)}) %collective-permute-start.1) | collective-permute-done | bytes 655392 | tf_op jit(solution)/shard_map/ppermute | solution.py:270
  28.5 2.4 %collective-permute-start.2 = (bf16[8,320,128]{2,1,0:T(8,128)(2,1)S(1)}, bf16[8,320,128]{2,1,0:T(8,128)(2,1)S(1)}, u32[]{:S(2)}, u32[]{:S(2)}) collective-permute-start(bf16[8,320,128]{2,1,0:T(8,128)(2,1)S(1)} %get-tuple-element.34.refs_0_), channel_id=1, source_target_pairs={{4,0},{6,2},{8,4},{10,6},{12,8},{14,10},{5,1},{7,3},{9,5},{11,7},{... | collective-permute-start | bytes 1966088 | tf_op jit(solution)/shard_map/ppermute | solution.py:270
  30.9 4.4 %collective-permute-start.4 = (bf16[8,320,128]{2,1,0:T(8,128)(2,1)S(1)}, bf16[8,320,128]{2,1,0:T(8,128)(2,1)S(1)}, u32[]{:S(2)}, u32[]{:S(2)}) collective-permute-start(bf16[8,320,128]{2,1,0:T(8,128)(2,1)S(1)} %get-tuple-element.34.refs_0_), channel_id=1, source_target_pairs={{2,0},{6,4},{10,8},{14,12},{3,1},{7,5},{11,9},{15,13},{18,16},{22,... | collective-permute-start | bytes 1966088 | tf_op jit(solution)/shard_map/ppermute | solution.py:270
  35.4 1.3 %collective-permute-start.6 = (bf16[8,320,128]{2,1,0:T(8,128)(2,1)}, bf16[8,320,128]{2,1,0:T(8,128)(2,1)}, u32[]{:S(2)}, u32[]{:S(2)}) collective-permute-start(bf16[8,320,128]{2,1,0:T(8,128)(2,1)} %collective-permute-done.3.refs_4_.refs_2_), channel_id=1, source_target_pairs={{0,2},{4,6},{8,10},{12,14},{1,3},{5,7},{9,11},{13,15},{16,18},{20,... | collective-permute-start | bytes 1966088 | tf_op jit(solution)/shard_map/ppermute | solution.py:270
  36.7 7.7 %collective-permute-done.2.refs_4_.refs_2_ = bf16[8,320,128]{2,1,0:T(8,128)(2,1)S(1)} collective-permute-done((bf16[8,320,128]{2,1,0:T(8,128)(2,1)S(1)}, bf16[8,320,128]{2,1,0:T(8,128)(2,1)S(1)}, u32[]{:S(2)}, u32[]{:S(2)}) %collective-permute-start.2) | collective-permute-done | bytes 655392 | tf_op jit(solution)/shard_map/ppermute | solution.py:270
  44.3 1.3 %collective-permute-start.5 = (bf16[8,320,128]{2,1,0:T(8,128)(2,1)S(1)}, bf16[8,320,128]{2,1,0:T(8,128)(2,1)S(1)}, u32[]{:S(2)}, u32[]{:S(2)}) collective-permute-start(bf16[8,320,128]{2,1,0:T(8,128)(2,1)S(1)} %collective-permute-done.2.refs_4_.refs_2_), channel_id=1, source_target_pairs={{0,2},{4,6},{8,10},{12,14},{1,3},{5,7},{9,11},{13,15},{16,18},{20,... | collective-permute-start | bytes 1966088 | tf_op jit(solution)/shard_map/ppermute | solution.py:270
  45.6 3.0 %collective-permute-done.4.refs_2_ = bf16[8,320,128]{2,1,0:T(8,128)(2,1)S(1)} collective-permute-done((bf16[8,320,128]{2,1,0:T(8,128)(2,1)S(1)}, bf16[8,320,128]{2,1,0:T(8,128)(2,1)S(1)}, u32[]{:S(2)}, u32[]{:S(2)}) %collective-permute-start.4) | collective-permute-done | bytes 655392 | tf_op jit(solution)/shard_map/ppermute | solution.py:270
  48.6 4.4 %collective-permute-start.9 = (bf16[8,320,128]{2,1,0:T(8,128)(2,1)}, bf16[8,320,128]{2,1,0:T(8,128)(2,1)S(1)}, u32[]{:S(2)}, u32[]{:S(2)}) collective-permute-start(bf16[8,320,128]{2,1,0:T(8,128)(2,1)} %collective-permute-done.3.refs_4_.refs_2_), channel_id=1, source_target_pairs={{2,0},{6,4},{10,8},{14,12},{3,1},{7,5},{11,9},{15,13},{18,16},{22,... | collective-permute-start | bytes 1966088 | tf_op jit(solution)/shard_map/ppermute | solution.py:270
  53.0 2.2 %collective-permute-done.6.refs_3_ = bf16[8,320,128]{2,1,0:T(8,128)(2,1)} collective-permute-done((bf16[8,320,128]{2,1,0:T(8,128)(2,1)}, bf16[8,320,128]{2,1,0:T(8,128)(2,1)}, u32[]{:S(2)}, u32[]{:S(2)}) %collective-permute-start.6) | collective-permute-done | bytes 655392 | tf_op jit(solution)/shard_map/ppermute | solution.py:270
  55.3 2.3 %collective-permute-start.10 = (bf16[8,320,128]{2,1,0:T(8,128)(2,1)}, bf16[8,320,128]{2,1,0:T(8,128)(2,1)S(1)}, u32[]{:S(2)}, u32[]{:S(2)}) collective-permute-start(bf16[8,320,128]{2,1,0:T(8,128)(2,1)} %collective-permute-done.6.refs_3_), channel_id=1, source_target_pairs={{6,2},{10,6},{14,10},{7,3},{11,7},{15,11},{22,18},{26,22},{30,26},... | collective-permute-start | bytes 1966088 | tf_op jit(solution)/shard_map/ppermute | solution.py:270
  58.7 1.1 %copy-done.5 = bf16[8,320,128]{2,1,0:T(8,128)(2,1)S(1)} copy-done((bf16[8,320,128]{2,1,0:T(8,128)(2,1)S(1)}, bf16[8,320,128]{2,1,0:T(8,128)(2,1)}, u32[]{:S(2)}) %copy-start.5) | copy-done | bytes 655384
  59.8 7.8 %shard_map.61 = (bf16[16,320,960]{2,1,0:T(8,128)(2,1)}, bf16[16,320,960]{2,1,0:T(8,128)(2,1)}) custom-call(bf16[8,320,128]{2,1,0:T(8,128)(2,1)S(1)} %copy-done.2, bf16[320,384]{1,0:T(8,128)(2,1)S(1)} %get-tuple-element.36.refs_1_, bf16[8,320,128]{2,1,0:T(8,128)(2,1)S(1)} %copy-done.5, bf16[8,320,128]{2,1,0:T(8,128)(2,1)} %collective-permute-done.6.refs_3_, ...), custom_call_target="tpu_custom_call" | custom-call | flops 838860800 | bytes 6553600 | tf_op jit(solution)/shard_map/pallas_call | solution.py:192
  67.8 2.3 %collective-permute-start.8 = (bf16[4,320,128]{2,1,0:T(8,128)(2,1)S(1)}, bf16[4,320,128]{2,1,0:T(8,128)(2,1)S(1)}, u32[]{:S(2)}, u32[]{:S(2)}) collective-permute-start(bf16[4,320,128]{2,1,0:T(8,128)(2,1)S(1)} %broadcast_select_fusion), channel_id=1, source_target_pairs={{4,0},{6,2},{8,4},{10,6},{12,8},{14,10},{5,1},{7,3},{9,5},{11,7},{... | collective-permute-start | bytes 983048 | tf_op jit(solution)/shard_map/ppermute | solution.py:270
  70.2 1.9 %collective-permute-start.7 = (bf16[4,320,128]{2,1,0:T(8,128)(2,1)S(1)}, bf16[4,320,128]{2,1,0:T(8,128)(2,1)S(1)}, u32[]{:S(2)}, u32[]{:S(2)}) collective-permute-start(bf16[4,320,128]{2,1,0:T(8,128)(2,1)S(1)} %broadcast_select_fusion.1), channel_id=1, source_target_pairs={{4,0},{6,2},{8,4},{10,6},{12,8},{14,10},{5,1},{7,3},{9,5},{11,7},{... | collective-permute-start | bytes 983048 | tf_op jit(solution)/shard_map/ppermute | solution.py:270
  72.1 6.6 %shard_map.62 = (bf16[16,320,960]{2,1,0:T(8,128)(2,1)}, bf16[16,320,960]{2,1,0:T(8,128)(2,1)}) custom-call(bf16[8,320,128]{2,1,0:T(8,128)(2,1)S(1)} %get-tuple-element.34.refs_0_, bf16[320,384]{1,0:T(8,128)(2,1)S(1)} %get-tuple-element.36.refs_1_, ...), custom_call_target="tpu_custom_call", output_to_operand_aliasing={{0}: (5, {}), {1}: (6, {})} | custom-call | flops 838860800 | bytes 6553600 | tf_op jit(solution)/shard_map/pallas_call | solution.py:192
  78.7 6.0 %shard_map.63 = (bf16[16,320,960]{2,1,0:T(8,128)(2,1)}, bf16[16,320,960]{2,1,0:T(8,128)(2,1)}) custom-call(bf16[8,320,128]{2,1,0:T(8,128)(2,1)S(1)} %copy-done.2, bf16[320,384]{1,0:T(8,128)(2,1)S(1)} %get-tuple-element.33.refs_1_, bf16[8,320,128]{2,1,0:T(8,128)(2,1)} %collective-permute-done.3.refs_4_.refs_2_, ...), custom_call_target="tpu_custom_call", output_to_operand_aliasing={{0}: (5, {}), {1}: (6, {})} | custom-call | flops 419430400 | bytes 3276800 | tf_op jit(solution)/shard_map/pallas_call | solution.py:192
  84.7 2.9 %shard_map.64 = (bf16[16,320,960]{2,1,0:T(8,128)(2,1)}, bf16[16,320,960]{2,1,0:T(8,128)(2,1)}) custom-call(bf16[8,320,128]{2,1,0:T(8,128)(2,1)S(1)} %get-tuple-element.34.refs_0_, bf16[320,384]{1,0:T(8,128)(2,1)S(1)} %get-tuple-element.33.refs_1_, ...), custom_call_target="tpu_custom_call", output_to_operand_aliasing={{0}: (4, {}), {1}: (5, {})} | custom-call | flops 209715200 | bytes 1638400 | tf_op jit(solution)/shard_map/pallas_call | solution.py:192
  87.6 2.9 %shard_map.65 = (bf16[16,320,960]{2,1,0:T(8,128)(2,1)}, bf16[16,320,960]{2,1,0:T(8,128)(2,1)}) custom-call(bf16[8,320,128]{2,1,0:T(8,128)(2,1)S(1)} %get-tuple-element.34.refs_0_, bf16[320,384]{1,0:T(8,128)(2,1)S(1)} %get-tuple-element.33.refs_1_, ...), custom_call_target="tpu_custom_call", output_to_operand_aliasing={{0}: (4, {}), {1}: (5, {})} | custom-call | flops 209715200 | bytes 1638400 | tf_op jit(solution)/shard_map/pallas_call | solution.py:192
  (25 shorter events, 3.9 us)
Async XLA Ops:
  1.4 1.7 %copy-start = (bf16[32,320,128]{2,1,0:T(8,128)(2,1)S(1)}, bf16[32,320,128]{2,1,0:T(8,128)(2,1)}, u32[]{:S(2)}) copy-start(bf16[32,320,128]{2,1,0:T(8,128)(2,1)} %samples_ref.1) | copy-start | bytes 7864324
  3.1 0.7 copy-start.3
  7.4 2.2 %collective-permute-start = (bf16[8,320,128]{2,1,0:T(8,128)(2,1)S(1)}, bf16[8,320,128]{2,1,0:T(8,128)(2,1)S(1)}, u32[]{:S(2)}, u32[]{:S(2)}) collective-permute-start(bf16[8,320,128]{2,1,0:T(8,128)(2,1)S(1)} %get-tuple-element.30), channel_id=1, source_target_pairs={{0,1},{1,0},{2,3},{3,2},{4,5},{5,4},{6,7},{7,6},{8,9},{9,8},{10,11... | collective-permute-start | bytes 1966088 | tf_op jit(solution)/shard_map/ppermute | solution.py:248
  11.0 25.7 %copy-start.1 = (bf16[8,320,128]{2,1,0:T(8,128)(2,1)}, bf16[8,320,128]{2,1,0:T(8,128)(2,1)S(1)}, u32[]{:S(2)}) copy-start(bf16[8,320,128]{2,1,0:T(8,128)(2,1)S(1)} %get-tuple-element.32.refs_0_) | copy-start | bytes 1966084
  11.0 16.7 %collective-permute-start.1 = (bf16[8,320,128]{2,1,0:T(8,128)(2,1)S(1)}, bf16[8,320,128]{2,1,0:T(8,128)(2,1)S(1)}, u32[]{:S(2)}, u32[]{:S(2)}) collective-permute-start(bf16[8,320,128]{2,1,0:T(8,128)(2,1)S(1)} %get-tuple-element.32.refs_0_), channel_id=1, source_target_pairs={{2,0},{6,4},{10,8},{14,12},{3,1},{7,5},{11,9},{15,13},{18,16},{22,... | collective-permute-start | bytes 1966088 | tf_op jit(solution)/shard_map/ppermute | solution.py:270
  13.5 21.9 %collective-permute-start.3 = (bf16[8,320,128]{2,1,0:T(8,128)(2,1)S(1)}, bf16[8,320,128]{2,1,0:T(8,128)(2,1)}, u32[]{:S(2)}, u32[]{:S(2)}) collective-permute-start(bf16[8,320,128]{2,1,0:T(8,128)(2,1)S(1)} %get-tuple-element.32.refs_0_), channel_id=1, source_target_pairs={{4,0},{6,2},{8,4},{10,6},{12,8},{14,10},{5,1},{7,3},{9,5},{11,7},{... | collective-permute-start | bytes 1966088 | tf_op jit(solution)/shard_map/ppermute | solution.py:270
  27.7 0.8 copy-start.4
  28.5 15.8 %collective-permute-start.2 = (bf16[8,320,128]{2,1,0:T(8,128)(2,1)S(1)}, bf16[8,320,128]{2,1,0:T(8,128)(2,1)S(1)}, u32[]{:S(2)}, u32[]{:S(2)}) collective-permute-start(bf16[8,320,128]{2,1,0:T(8,128)(2,1)S(1)} %get-tuple-element.34.refs_0_), channel_id=1, source_target_pairs={{4,0},{6,2},{8,4},{10,6},{12,8},{14,10},{5,1},{7,3},{9,5},{11,7},{... | collective-permute-start | bytes 1966088 | tf_op jit(solution)/shard_map/ppermute | solution.py:270
  30.9 17.7 %collective-permute-start.4 = (bf16[8,320,128]{2,1,0:T(8,128)(2,1)S(1)}, bf16[8,320,128]{2,1,0:T(8,128)(2,1)S(1)}, u32[]{:S(2)}, u32[]{:S(2)}) collective-permute-start(bf16[8,320,128]{2,1,0:T(8,128)(2,1)S(1)} %get-tuple-element.34.refs_0_), channel_id=1, source_target_pairs={{2,0},{6,4},{10,8},{14,12},{3,1},{7,5},{11,9},{15,13},{18,16},{22,... | collective-permute-start | bytes 1966088 | tf_op jit(solution)/shard_map/ppermute | solution.py:270
  35.4 19.9 %collective-permute-start.6 = (bf16[8,320,128]{2,1,0:T(8,128)(2,1)}, bf16[8,320,128]{2,1,0:T(8,128)(2,1)}, u32[]{:S(2)}, u32[]{:S(2)}) collective-permute-start(bf16[8,320,128]{2,1,0:T(8,128)(2,1)} %collective-permute-done.3.refs_4_.refs_2_), channel_id=1, source_target_pairs={{0,2},{4,6},{8,10},{12,14},{1,3},{5,7},{9,11},{13,15},{16,18},{20,... | collective-permute-start | bytes 1966088 | tf_op jit(solution)/shard_map/ppermute | solution.py:270
  44.3 23.3 %collective-permute-start.5 = (bf16[8,320,128]{2,1,0:T(8,128)(2,1)S(1)}, bf16[8,320,128]{2,1,0:T(8,128)(2,1)S(1)}, u32[]{:S(2)}, u32[]{:S(2)}) collective-permute-start(bf16[8,320,128]{2,1,0:T(8,128)(2,1)S(1)} %collective-permute-done.2.refs_4_.refs_2_), channel_id=1, source_target_pairs={{0,2},{4,6},{8,10},{12,14},{1,3},{5,7},{9,11},{13,15},{16,18},{20,... | collective-permute-start | bytes 1966088 | tf_op jit(solution)/shard_map/ppermute | solution.py:270
  48.6 30.1 %collective-permute-start.9 = (bf16[8,320,128]{2,1,0:T(8,128)(2,1)}, bf16[8,320,128]{2,1,0:T(8,128)(2,1)S(1)}, u32[]{:S(2)}, u32[]{:S(2)}) collective-permute-start(bf16[8,320,128]{2,1,0:T(8,128)(2,1)} %collective-permute-done.3.refs_4_.refs_2_), channel_id=1, source_target_pairs={{2,0},{6,4},{10,8},{14,12},{3,1},{7,5},{11,9},{15,13},{18,16},{22,... | collective-permute-start | bytes 1966088 | tf_op jit(solution)/shard_map/ppermute | solution.py:270
  55.3 23.5 %collective-permute-start.10 = (bf16[8,320,128]{2,1,0:T(8,128)(2,1)}, bf16[8,320,128]{2,1,0:T(8,128)(2,1)S(1)}, u32[]{:S(2)}, u32[]{:S(2)}) collective-permute-start(bf16[8,320,128]{2,1,0:T(8,128)(2,1)} %collective-permute-done.6.refs_3_), channel_id=1, source_target_pairs={{6,2},{10,6},{14,10},{7,3},{11,7},{15,11},{22,18},{26,22},{30,26},... | collective-permute-start | bytes 1966088 | tf_op jit(solution)/shard_map/ppermute | solution.py:270
  57.6 1.1 %copy-start.2 = (bf16[8,320,128]{2,1,0:T(8,128)(2,1)S(1)}, bf16[8,320,128]{2,1,0:T(8,128)(2,1)}, u32[]{:S(2)}) copy-start(bf16[8,320,128]{2,1,0:T(8,128)(2,1)} %copy-done.1) | copy-start | bytes 1966084
  58.7 1.1 %copy-start.5 = (bf16[8,320,128]{2,1,0:T(8,128)(2,1)S(1)}, bf16[8,320,128]{2,1,0:T(8,128)(2,1)}, u32[]{:S(2)}) copy-start(bf16[8,320,128]{2,1,0:T(8,128)(2,1)} %copy-done.4) | copy-start | bytes 1966084
  67.8 16.9 %collective-permute-start.8 = (bf16[4,320,128]{2,1,0:T(8,128)(2,1)S(1)}, bf16[4,320,128]{2,1,0:T(8,128)(2,1)S(1)}, u32[]{:S(2)}, u32[]{:S(2)}) collective-permute-start(bf16[4,320,128]{2,1,0:T(8,128)(2,1)S(1)} %broadcast_select_fusion), channel_id=1, source_target_pairs={{4,0},{6,2},{8,4},{10,6},{12,8},{14,10},{5,1},{7,3},{9,5},{11,7},{... | collective-permute-start | bytes 983048 | tf_op jit(solution)/shard_map/ppermute | solution.py:270
  70.2 17.5 %collective-permute-start.7 = (bf16[4,320,128]{2,1,0:T(8,128)(2,1)S(1)}, bf16[4,320,128]{2,1,0:T(8,128)(2,1)S(1)}, u32[]{:S(2)}, u32[]{:S(2)}) collective-permute-start(bf16[4,320,128]{2,1,0:T(8,128)(2,1)S(1)} %broadcast_select_fusion.1), channel_id=1, source_target_pairs={{4,0},{6,2},{8,4},{10,6},{12,8},{14,10},{5,1},{7,3},{9,5},{11,7},{... | collective-permute-start | bytes 983048 | tf_op jit(solution)/shard_map/ppermute | solution.py:270
